TPU v7x, 128 devices: a whole 4x4x4 slice. The times are simulated.
128 devices in a mesh: row: 64 (over x, z, y), col: 2 (over core).
Axes of the slice: x: 4, y: 4, z: 4, core: 2. Of those that a mesh axis runs over, the one named last changes fastest.
Arguments:
- tsdf_prior: float32 [2048, 64, 256], P('row', None, 'col'), may hold values from -1 to 1
- prior_weight: float32 [2048, 64, 256], P('row', None, 'col'), may hold values from 0.5 to 8
- depth_maps: float32 [64, 131072], P('row'), may hold values from 0 to 64
- confidence: float32 [64, 131072], P('row'), may hold values from 0.2 to 5
- frustum_tiles: int32 [128, 128, 2], P(('row', 'col')), may hold values from -1 to 31, as said below
- pixel_index: int32 [128, 128, 2, 128], P(('row', 'col')), may hold values from 0 to 131071
- conv_weights: bfloat16 [3, 64, 16, 3, 3], replicated, may hold values from -0.5 to 0.5
Outputs:
- refined: float32 [2048, 64, 256], P('row', None, 'col')
- new_weight: float32 [2048, 64, 256], P('row', None, 'col')
Inputs may be any that keep to these rules, and one draw needn't show every extreme that they name: `frustum_tiles`: -1 marks an empty slot; otherwise the entry is one of the owner's 32 tiles, and slot s names a tile from the s-th of 2 equal runs of tile numbers.
All inputs are finite; a program needn't handle non-finite values.
Results may differ from a plain program's by a relative error of at most 0.003.
Values may be sent and summed in bfloat16 or wider, within the bound.
No kernel may reach another device: no remote copies, remote signals or barrier semaphores. Data moves between devices by JAX's collectives and lax.ppermute only.
A program may use at most 128 MiB of HBM per device.

v0:
```python
import jax
import jax.numpy as jnp
from jax import lax
from jax.sharding import PartitionSpec as P

GROUPS = 4
TRUNC = 4


def extended(array, sides, width):
    for axis, dim in sides:
        size, length = (lax.axis_size(axis), array.shape[dim])
        up = [(i, (i + 1) % size) for i in range(size - 1)]
        down = [(j, i) for i, j in up]
        last = lax.slice_in_dim(array, length - width, length, axis=dim)
        leading = lax.slice_in_dim(array, 0, width, axis=dim)
        before = lax.ppermute(last, axis, up)
        after = lax.ppermute(leading, axis, down)
        array = jnp.concatenate([before, array, after], axis=dim)
    return array


def contributions(blocks, heights, certainty):
    levels = jnp.arange(blocks.shape[-2], dtype=jnp.float32)[:, None]
    scaled = (heights[..., None, :] - levels) / TRUNC
    signed = jnp.clip(scaled, -1.0, 1.0)
    visible = jnp.clip(scaled + 2.0, 0.0, 1.0)
    mismatch = signed - blocks
    observed = certainty[..., None, :] * visible / (1.0 + 4.0 * mismatch * mismatch)
    return (observed * signed, observed)


def convolve(padded, kernel):
    row_count = padded.shape[0] - 2
    bin_count = padded.shape[1]
    wide = padded.shape[2]
    width_out = wide - 2
    per_group = bin_count // GROUPS
    grouped = padded.reshape(padded.shape[0], GROUPS, per_group, wide)
    weights = kernel.reshape(GROUPS, per_group, per_group, 3, 3)
    total = jnp.zeros((row_count, GROUPS, per_group, width_out), jnp.float32)
    for col_offset in range(3):
        partial_sum = jnp.zeros((row_count, GROUPS, per_group, wide), jnp.float32)
        for row_offset in range(3):
            partial_sum = partial_sum + jnp.einsum(
                "goi,hgiw->hgow",
                weights[:, :, :, row_offset, col_offset],
                grouped[row_offset : row_offset + row_count],
                preferred_element_type=jnp.float32,
            )
        total = total + partial_sum[:, :, :, col_offset : col_offset + width_out]
    return total.reshape(row_count, bin_count, width_out)


def on_device(
    tsdf_prior, prior_weight, depth_maps, confidence, frustum_tiles, pixel_index, conv_weights
):
    tile_rows, bin_count, columns = tsdf_prior.shape
    own_list = frustum_tiles[0]
    requested = lax.all_to_all(own_list, ("row", "col"), split_axis=0, concat_axis=0, tiled=True)
    places = pixel_index[0]
    heights = jnp.take(depth_maps[0], places, axis=0)
    certainty = jnp.take(confidence[0], places, axis=0)
    selector = (jnp.arange(tile_rows, dtype=jnp.int32)[:, None] == requested.reshape(1, -1)).astype(
        jnp.float32
    )
    flat_prior = tsdf_prior.reshape(tile_rows, bin_count * columns)
    picked = jnp.dot(
        selector.T, flat_prior, precision=lax.Precision.HIGHEST, preferred_element_type=jnp.float32
    )
    picked = picked.reshape(requested.shape + (bin_count, columns))
    heights_in, certainty_in = (
        lax.all_to_all(heights, ("row", "col"), split_axis=0, concat_axis=0, tiled=True),
        lax.all_to_all(certainty, ("row", "col"), split_axis=0, concat_axis=0, tiled=True),
    )
    weighted, observed = contributions(picked, heights_in, certainty_in)
    sum_weighted = jnp.dot(
        selector,
        weighted.reshape(-1, bin_count * columns),
        precision=lax.Precision.HIGHEST,
        preferred_element_type=jnp.float32,
    ).reshape(tile_rows, bin_count, columns)
    sum_observed = jnp.dot(
        selector,
        observed.reshape(-1, bin_count * columns),
        precision=lax.Precision.HIGHEST,
        preferred_element_type=jnp.float32,
    ).reshape(tile_rows, bin_count, columns)
    joined_field = (prior_weight * tsdf_prior + sum_weighted) / (prior_weight + sum_observed)
    new_weight = prior_weight + sum_observed
    layer_count = conv_weights.shape[0]
    current = joined_field
    for depth_step in range(layer_count):
        activated = jax.nn.silu(current).astype(jnp.bfloat16)
        padded = extended(activated, (("row", 0), ("col", 2)), 1)
        current = current + convolve(padded, conv_weights[depth_step])
    return (current, new_weight)


def solution(mesh):
    placed = (
        P("row", None, "col"),
        P("row", None, "col"),
        P("row", None),
        P("row", None),
        P(("row", "col"), None, None),
        P(("row", "col"), None, None, None),
        P(),
    )
    return jax.shard_map(
        on_device,
        mesh=mesh,
        in_specs=placed,
        out_specs=(P("row", None, "col"), P("row", None, "col")),
        check_vma=False,
    )
```

profile of v0, /device:TPU:3, one launch (start us, length us, event | category | flops | bytes accessed | tf_op | source)
XLA Modules:
  0.0 588.4 jit_solution(17620342904530682812)
XLA Ops:
  2.1 10.8 %all-to-all-start = ((s32[128,1,2]{2,1,0:T(1,128)}), s32[128,1,2]{2,1,0:T(1,128)S(1)}, u32[]{:S(2)}, u32[]{:S(2)}) async-start(s32[128,1,2]{2,1,0:T(1,128)} %bitcast), calls=%async_computation | async-start | bytes 131072 | tf_op jit(solution)/shard_map/all_to_all | solution.py:60
  14.0 180.5 %gather_fusion = f32[32768]{0:T(1024)S(1)} fusion(f32[131072]{0:T(1024)S(1)} %bitcast.299, s32[32768]{0:T(1024)S(1)} %broadcast_clamp_fusion), kind=kCustom, calls=%fused_computation.clone | custom fusion | bytes 393216 | tf_op jit(solution)/shard_map/jit(_take)/gather | solution.py:63
  194.6 180.5 %gather_fusion.1 = f32[32768]{0:T(1024)S(1)} fusion(f32[131072]{0:T(1024)S(1)} %bitcast.300, s32[32768]{0:T(1024)S(1)} %broadcast_clamp_fusion), kind=kCustom, calls=%fused_computation.1.clone | custom fusion | bytes 393216 | tf_op jit(solution)/shard_map/jit(_take)/gather | solution.py:62
  376.0 9.8 %all-to-all-start.2 = ((f32[128,2,128]{2,1,0:T(2,128)}), f32[128,2,128]{2,1,0:T(2,128)S(1)}, u32[]{:S(2)}, u32[]{:S(2)}) async-start(f32[128,2,128]{2,1,0:T(2,128)} %get-tuple-element.31), calls=%async_computation.2 | async-start | bytes 262144 | tf_op jit(solution)/shard_map/all_to_all | solution.py:73
  387.3 7.4 %all-to-all-done.2 = f32[128,2,128]{2,1,0:T(2,128)S(1)} async-done(((f32[128,2,128]{2,1,0:T(2,128)}), f32[128,2,128]{2,1,0:T(2,128)S(1)}, u32[]{:S(2)}, u32[]{:S(2)}) %all-to-all-start.2) | async-done | bytes 131104 | tf_op jit(solution)/shard_map/all_to_all | solution.py:73
  394.7 5.4 all-to-all-start.1
  400.2 8.7 %all-to-all-done.1 = f32[128,2,128]{2,1,0:T(2,128)S(1)} async-done(((f32[128,2,128]{2,1,0:T(2,128)}), f32[128,2,128]{2,1,0:T(2,128)S(1)}, u32[]{:S(2)}, u32[]{:S(2)}) %all-to-all-start.1) | async-done | bytes 131104 | tf_op jit(solution)/shard_map/all_to_all | solution.py:74
  408.9 10.1 %fusion.3 = (f32[128,2,64,128]{3,0,2,1:T(8,128)}, f32[128,2,64,128]{3,0,2,1:T(8,128)S(1)}) fusion(f32[128,2,128]{2,0,1:T(8,128)S(1)} %copy.100, pred[128,2,32,1]{2,1,0,3:T(4,128)(4,1)S(1)} %bitcast.365, f32[128,2,128]{2,0,1:T(8,128)S(1)} %copy.99, f32[4,8,64,128]{3,2,1,0:T(8,128)S(1)} %bitcast.334), kind=kOutput, calls=%fused_computation.9 | convolution fusion | flops 830472192 | bytes 18096128 | tf_op jit(solution)/shard_map/dot_general | solution.py:68
  419.0 4.9 copy.105
  423.9 11.1 %copy.265 = f32[32,8,64,128]{3,1,2,0:T(8,128)} copy(f32[32,8,64,128]{3,2,1,0:T(8,128)S(1)} %bitcast.303) | data formatting | bytes 16777216
  435.0 9.1 %copy.186 = f32[8192,256]{1,0:T(8,128)} copy(f32[8192,256]{0,1:T(8,128)} %bitcast.304) | data formatting | bytes 16777216 | tf_op jit(solution)/shard_map/dot_general | solution.py:83
  444.1 8.2 %copy.103 = f32[128,2,64,128]{3,2,1,0:T(8,128)S(1)} copy(f32[128,2,64,128]{3,0,2,1:T(8,128)} %get-tuple-element.35) | data formatting | bytes 16777216 | tf_op jit(solution)/shard_map/mul | solution.py:30
  452.3 11.4 %copy.266 = f32[32,8,64,128]{3,1,2,0:T(8,128)} copy(f32[32,8,64,128]{3,2,1,0:T(8,128)S(1)} %bitcast.305) | data formatting | bytes 16777216
  463.7 9.1 %copy.185 = f32[8192,256]{1,0:T(8,128)} copy(f32[8192,256]{0,1:T(8,128)} %bitcast.306) | data formatting | bytes 16777216 | tf_op jit(solution)/shard_map/dot_general | solution.py:77
  472.7 7.2 %convolution_add_fusion = f32[32,64,128]{2,0,1:T(8,128)S(1)} fusion(f32[64,128,256]{2,1,0:T(8,128)} %bitcast.301, f32[32,64,128]{2,1,0:T(8,128)S(1)} %copy-done.7, s32[256]{0:T(256)S(1)} %eq.31), kind=kOutput, calls=%fused_computation.19 | convolution fusion | flops 805576704 | bytes 10486784 | tf_op jit(solution)/shard_map/dot_general | solution.py:83
  480.0 5.0 multiply_convert_fusion.2
  487.3 7.2 %collective-permute-start.1 = (bf16[1,64,128]{2,0,1:T(2,128)(2,1)S(1)}, bf16[1,64,128]{2,0,1:T(2,128)(2,1)S(1)}, u32[]{:S(2)}, u32[]{:S(2)}) collective-permute-start(bf16[1,64,128]{2,0,1:T(2,128)(2,1)S(1)} %get-tuple-element.29), channel_id=1, source_target_pairs={{2,0},{4,2},{6,4},{8,6},{10,8},{12,10},{14,12},{16,14},{18,16},{20... | collective-permute-start | bytes 49160 | tf_op jit(solution)/shard_map/ppermute | solution.py:18
  498.4 3.7 collective-permute-start.3
  515.5 8.2 %collective-permute-start.5 = (bf16[1,64,128]{2,0,1:T(2,128)(2,1)S(1)}, bf16[1,64,128]{2,0,1:T(2,128)(2,1)S(1)}, u32[]{:S(2)}, u32[]{:S(2)}) collective-permute-start(bf16[1,64,128]{2,0,1:T(2,128)(2,1)S(1)} %get-tuple-element.27), channel_id=1, source_target_pairs={{2,0},{4,2},{6,4},{8,6},{10,8},{12,10},{14,12},{16,14},{18,16},{20... | collective-permute-start | bytes 49160 | tf_op jit(solution)/shard_map/ppermute | solution.py:18
  530.6 4.1 collective-permute-start.7
  537.2 2.3 pad_maximum_fusion.1
  550.6 8.2 %collective-permute-start.9 = (bf16[1,64,128]{2,0,1:T(2,128)(2,1)S(1)}, bf16[1,64,128]{2,0,1:T(2,128)(2,1)S(1)}, u32[]{:S(2)}, u32[]{:S(2)}) collective-permute-start(bf16[1,64,128]{2,0,1:T(2,128)(2,1)S(1)} %get-tuple-element.25), channel_id=1, source_target_pairs={{2,0},{4,2},{6,4},{8,6},{10,8},{12,10},{14,12},{16,14},{18,16},{20... | collective-permute-start | bytes 49160 | tf_op jit(solution)/shard_map/ppermute | solution.py:18
  565.2 3.8 collective-permute-start.11
  569.1 2.8 copy.154
  (123 shorter events, 67.6 us)
Async XLA Ops:
  0.6 13.3 %copy-start = (f32[1,131072]{1,0:T(1,128)S(1)}, f32[1,131072]{1,0:T(1,128)}, u32[]{:S(2)}) copy-start(f32[1,131072]{1,0:T(1,128)} %param.12) | copy-start | bytes 1572868
  2.1 373.9 %all-to-all-start = ((s32[128,1,2]{2,1,0:T(1,128)}), s32[128,1,2]{2,1,0:T(1,128)S(1)}, u32[]{:S(2)}, u32[]{:S(2)}) async-start(s32[128,1,2]{2,1,0:T(1,128)} %bitcast), calls=%async_computation | async-start | bytes 131072 | tf_op jit(solution)/shard_map/all_to_all | solution.py:60
  14.0 180.6 %copy-start.2 = (f32[1,131072]{1,0:T(1,128)S(1)}, f32[1,131072]{1,0:T(1,128)}, u32[]{:S(2)}) copy-start(f32[1,131072]{1,0:T(1,128)} %param.11) | copy-start | bytes 1572868
  194.6 180.6 %copy-start.10 = (s32[1,128,2,128]{3,2,1,0:T(2,128)S(1)}, s32[1,128,2,128]{3,2,1,0:T(2,128)}, u32[]{:S(2)}) copy-start(s32[1,128,2,128]{3,2,1,0:T(2,128)} %param.14) | copy-start | bytes 393220
  194.6 214.4 %copy-start.8 = (f32[32,64,128]{2,1,0:T(8,128)S(1)}, f32[32,64,128]{2,1,0:T(8,128)}, u32[]{:S(2)}) copy-start(f32[32,64,128]{2,1,0:T(8,128)} %param.9) | copy-start | bytes 3145732
  376.0 18.6 %all-to-all-start.2 = ((f32[128,2,128]{2,1,0:T(2,128)}), f32[128,2,128]{2,1,0:T(2,128)S(1)}, u32[]{:S(2)}, u32[]{:S(2)}) async-start(f32[128,2,128]{2,1,0:T(2,128)} %get-tuple-element.31), calls=%async_computation.2 | async-start | bytes 262144 | tf_op jit(solution)/shard_map/all_to_all | solution.py:73
  394.7 14.2 %all-to-all-start.1 = ((f32[128,2,128]{2,1,0:T(2,128)}), f32[128,2,128]{2,1,0:T(2,128)S(1)}, u32[]{:S(2)}, u32[]{:S(2)}) async-start(f32[128,2,128]{2,1,0:T(2,128)} %get-tuple-element.30), calls=%async_computation.1 | async-start | bytes 262144 | tf_op jit(solution)/shard_map/all_to_all | solution.py:74
  463.7 9.1 %copy-start.7 = (f32[32,64,128]{2,1,0:T(8,128)S(1)}, f32[32,64,128]{2,1,0:T(8,128)}, u32[]{:S(2)}) copy-start(f32[32,64,128]{2,1,0:T(8,128)} %param.10) | copy-start | bytes 3145732
  472.7 7.2 %copy-start.3 = (f32[8192,256]{1,0:T(8,128)S(1)}, f32[8192,256]{1,0:T(8,128)}, u32[]{:S(2)}) copy-start(f32[8192,256]{1,0:T(8,128)} %copy.185) | copy-start | bytes 25165828
  472.7 7.2 %copy-start.9 = (f32[32,64,128]{2,1,0:T(8,128)S(1)}, f32[32,64,128]{2,1,0:T(8,128)}, u32[]{:S(2)}) copy-start(f32[32,64,128]{2,1,0:T(8,128)} %param.9) | copy-start | bytes 3145732
  485.1 9.5 %collective-permute-start = (bf16[1,64,128]{2,0,1:T(2,128)(2,1)S(1)}, bf16[1,64,128]{2,0,1:T(2,128)(2,1)S(1)}, u32[]{:S(2)}, u32[]{:S(2)}) collective-permute-start(bf16[1,64,128]{2,0,1:T(2,128)(2,1)S(1)} %get-tuple-element.28), channel_id=1, source_target_pairs={{0,2},{2,4},{4,6},{6,8},{8,10},{10,12},{12,14},{14,16},{16,18},{18... | collective-permute-start | bytes 49160 | tf_op jit(solution)/shard_map/ppermute | solution.py:17
  487.3 8.3 %collective-permute-start.1 = (bf16[1,64,128]{2,0,1:T(2,128)(2,1)S(1)}, bf16[1,64,128]{2,0,1:T(2,128)(2,1)S(1)}, u32[]{:S(2)}, u32[]{:S(2)}) collective-permute-start(bf16[1,64,128]{2,0,1:T(2,128)(2,1)S(1)} %get-tuple-element.29), channel_id=1, source_target_pairs={{2,0},{4,2},{6,4},{8,6},{10,8},{12,10},{14,12},{16,14},{18,16},{20... | collective-permute-start | bytes 49160 | tf_op jit(solution)/shard_map/ppermute | solution.py:18
  495.9 6.2 %copy-start.12 = (bf16[3,64,16,3,3]{1,2,4,3,0:T(8,128)(2,1)S(1)}, bf16[3,64,16,3,3]{1,2,4,3,0:T(8,128)(2,1)}, u32[]{:S(2)}) copy-start(bf16[3,64,16,3,3]{1,2,4,3,0:T(8,128)(2,1)} %param.15) | copy-start | bytes 165892
  496.7 5.7 collective-permute-start.2
  498.4 4.4 collective-permute-start.3
  513.5 10.1 %collective-permute-start.4 = (bf16[1,64,128]{2,0,1:T(2,128)(2,1)S(1)}, bf16[1,64,128]{2,0,1:T(2,128)(2,1)S(1)}, u32[]{:S(2)}, u32[]{:S(2)}) collective-permute-start(bf16[1,64,128]{2,0,1:T(2,128)(2,1)S(1)} %get-tuple-element.26), channel_id=1, source_target_pairs={{0,2},{2,4},{4,6},{6,8},{8,10},{10,12},{12,14},{14,16},{16,18},{18... | collective-permute-start | bytes 49160 | tf_op jit(solution)/shard_map/ppermute | solution.py:17
  515.5 9.2 %collective-permute-start.5 = (bf16[1,64,128]{2,0,1:T(2,128)(2,1)S(1)}, bf16[1,64,128]{2,0,1:T(2,128)(2,1)S(1)}, u32[]{:S(2)}, u32[]{:S(2)}) collective-permute-start(bf16[1,64,128]{2,0,1:T(2,128)(2,1)S(1)} %get-tuple-element.27), channel_id=1, source_target_pairs={{2,0},{4,2},{6,4},{8,6},{10,8},{12,10},{14,12},{16,14},{18,16},{20... | collective-permute-start | bytes 49160 | tf_op jit(solution)/shard_map/ppermute | solution.py:18
  528.2 6.6 %collective-permute-start.6 = (bf16[34,64,1]{1,0,2:T(8,128)(2,1)S(1)}, bf16[34,64,1]{1,0,2:T(8,128)(2,1)S(1)}, u32[]{:S(2)}, u32[]{:S(2)}) collective-permute-start(bf16[34,64,1]{1,0,2:T(8,128)(2,1)S(1)} %copy.123), channel_id=1, source_target_pairs={{0,1},{2,3},{4,5},{6,7},{8,9},{10,11},{12,13},{14,15},{16,17},{18,... | collective-permute-start | bytes 13064 | tf_op jit(solution)/shard_map/ppermute | solution.py:17
  530.6 4.7 collective-permute-start.7
  548.2 11.9 %copy-start.4 = (f32[32,4,16,128]{3,0,2,1:T(8,128)}, f32[32,4,16,128]{3,0,2,1:T(8,128)S(1)}, u32[]{:S(2)}) copy-start(f32[32,4,16,128]{3,0,2,1:T(8,128)S(1)} %copy.137) | copy-start | bytes 3145732
  548.7 10.1 %collective-permute-start.8 = (bf16[1,64,128]{2,0,1:T(2,128)(2,1)S(1)}, bf16[1,64,128]{2,0,1:T(2,128)(2,1)S(1)}, u32[]{:S(2)}, u32[]{:S(2)}) collective-permute-start(bf16[1,64,128]{2,0,1:T(2,128)(2,1)S(1)} %get-tuple-element.24), channel_id=1, source_target_pairs={{0,2},{2,4},{4,6},{6,8},{8,10},{10,12},{12,14},{14,16},{16,18},{18... | collective-permute-start | bytes 49160 | tf_op jit(solution)/shard_map/ppermute | solution.py:17
  550.6 9.2 %collective-permute-start.9 = (bf16[1,64,128]{2,0,1:T(2,128)(2,1)S(1)}, bf16[1,64,128]{2,0,1:T(2,128)(2,1)S(1)}, u32[]{:S(2)}, u32[]{:S(2)}) collective-permute-start(bf16[1,64,128]{2,0,1:T(2,128)(2,1)S(1)} %get-tuple-element.25), channel_id=1, source_target_pairs={{2,0},{4,2},{6,4},{8,6},{10,8},{12,10},{14,12},{16,14},{18,16},{20... | collective-permute-start | bytes 49160 | tf_op jit(solution)/shard_map/ppermute | solution.py:18
  562.8 9.1 %collective-permute-start.10 = (bf16[34,64,1]{1,0,2:T(8,128)(2,1)S(1)}, bf16[34,64,1]{1,0,2:T(8,128)(2,1)S(1)}, u32[]{:S(2)}, u32[]{:S(2)}) collective-permute-start(bf16[34,64,1]{1,0,2:T(8,128)(2,1)S(1)} %copy.138), channel_id=1, source_target_pairs={{0,1},{2,3},{4,5},{6,7},{8,9},{10,11},{12,13},{14,15},{16,17},{18,... | collective-permute-start | bytes 13064 | tf_op jit(solution)/shard_map/ppermute | solution.py:17
  565.2 7.2 %collective-permute-start.11 = (bf16[34,64,1]{1,0,2:T(8,128)(2,1)}, bf16[34,64,1]{1,0,2:T(8,128)(2,1)}, u32[]{:S(2)}, u32[]{:S(2)}) collective-permute-start(bf16[34,64,1]{1,0,2:T(8,128)(2,1)} %copy.139), channel_id=1, source_target_pairs={{1,0},{3,2},{5,4},{7,6},{9,8},{11,10},{13,12},{15,14},{17,16},{19,... | collective-permute-start | bytes 13064 | tf_op jit(solution)/shard_map/ppermute | solution.py:18
  (4 other events, 9.0 us)
where the time goes:
time: 595 us; the launch traced here: 588 us
  local copies, waits for them, and re-layouts  441 us (74%)
  starting transfers between devices  71.1 us (12%)
  matrix products  43.2 us (7%)
  waiting for transfers between devices  19.1 us (3%)
  other arithmetic  12.5 us (2%)
    gather x1, local copies, waits for them, and re-layouts, on_device(): certainty = jnp.take(confidence[0], places, axis=0)  181 us
    gather x1, local copies, waits for them, and re-layouts, on_device(): heights = jnp.take(depth_maps[0], places, axis=0)  181 us
    ppermute x6, starting transfers between devices, extended(): after = lax.ppermute(leading, axis, down)  35.1 us
    unnamed x31, local copies, waits for them, and re-layouts  29.9 us
    dot_general x27, matrix products, convolve(): jnp.einsum('goi,hgiw->hgow', weights[:, :, :, row_offset, col_offset], gr...  20.9 us
  transfers between devices with their start and end apart: 15, of which 5 were waited for; matrix products, arithmetic and copies ran while one was open for 63% of the time, Pallas kernels for 0%

commit v1 on v0

v1 whole, which is shorter than its diff:
```python
import jax
import jax.numpy as jnp
from jax import lax
from jax.experimental import pallas as pl
from jax.experimental.pallas import tpu as pltpu
from jax.sharding import PartitionSpec as P

LANES = 128
BINS = 64
ROWS = 32
DEEP = 3
EXT = ROWS + 2 * DEEP
GROUP = 16
H_SCALE = 1023.0
C_SCALE = 13000.0
F32 = jnp.float32
BF16 = jnp.bfloat16
I32 = jnp.int32


def lookup_kernel(key_smem, key_ref, height_ref, conf_ref, out_ref, table):
    high = (height_ref[...] * H_SCALE + 0.5).astype(I32) - 32768
    low = (conf_ref[...] * C_SCALE + 0.5).astype(I32)
    table[...] = (high << 16) | low
    for block in range(key_ref.shape[0] // 8):
        index = key_ref[8 * block : 8 * block + 8, :]
        lane = index & (LANES - 1)
        line = index >> 7
        first = key_smem[8 * block, 0] >> 7
        last = key_smem[8 * block + 7, LANES - 1] >> 7

        def step(row, found):
            words = jnp.broadcast_to(table[pl.ds(row, 1), :], (8, LANES))
            taken = jnp.take_along_axis(words, lane, axis=1)
            return jnp.where(line == row, taken, found)

        out_ref[8 * block : 8 * block + 8, :] = lax.fori_loop(
            first, last + 1, step, jnp.zeros((8, LANES), I32)
        )


def lookup(keys, heights, confidence):
    return pl.pallas_call(
        lookup_kernel,
        out_shape=jax.ShapeDtypeStruct(keys.shape, I32),
        in_specs=[
            pl.BlockSpec(memory_space=pltpu.SMEM),
            pl.BlockSpec(memory_space=pltpu.VMEM),
            pl.BlockSpec(memory_space=pltpu.VMEM),
            pl.BlockSpec(memory_space=pltpu.VMEM),
        ],
        out_specs=pl.BlockSpec(memory_space=pltpu.VMEM),
        scratch_shapes=[pltpu.VMEM(heights.shape, I32)],
        compiler_params=pltpu.CompilerParams(vmem_limit_bytes=32 << 20),
        name="lookup",
    )(keys, keys, heights, confidence)


def join_kernel(
    spot_ref, list_ref, words_ref, prior_ref, weight_ref, joined_ref, new_ref, edge_ref, height, certainty
):
    col = spot_ref[1]
    word = words_ref[...]
    height[...] = ((word >> 16) + 32768).astype(F32) * (0.25 / H_SCALE)
    certainty[...] = (word & 0xFFFF).astype(F32) * (1.0 / C_SCALE)
    new_ref[...] = weight_ref[...]
    joined_ref[...] = weight_ref[...] * prior_ref[...]
    level = lax.broadcasted_iota(I32, (BINS, LANES), 0).astype(F32) * 0.25

    def term(reader, slot):
        tile = list_ref[reader, slot]
        prior = prior_ref[jnp.maximum(tile, 0)]
        scaled = height[pl.ds(2 * reader + slot, 1), :] - level
        signed = jnp.clip(scaled, -1.0, 1.0)
        visible = jnp.clip(scaled + 2.0, 0.0, 1.0)
        mismatch = signed - prior
        spread = 1.0 + 4.0 * (mismatch * mismatch)
        inverse = pl.reciprocal(spread, approx=True)
        inverse = inverse * (2.0 - spread * inverse)
        observed = (certainty[pl.ds(2 * reader + slot, 1), :] * visible) * inverse
        return tile, observed, observed * signed

    def add(tile, observed, weighted):
        @pl.when(tile >= 0)
        def _():
            new_ref[tile] += observed
            joined_ref[tile] += weighted

    def step(reader, carry):
        terms = [term(reader, slot) for slot in range(2)]
        for one in terms:
            add(*one)
        return carry

    lax.fori_loop(0, list_ref.shape[0], step, 0)
    lane = lax.broadcasted_iota(I32, (BINS, LANES), 1)
    source = jnp.where(col == 0, LANES - DEEP, 0)
    edge = jnp.zeros((BINS, LANES), F32)
    for row in range(ROWS):
        value = joined_ref[row] / new_ref[row]
        joined_ref[row] = value
        start = (row + DEEP) * DEEP
        moved = pltpu.roll(value, (start - source + LANES) % LANES, 1)
        edge = jnp.where((lane >= start) & (lane < start + DEEP), moved, edge)
    edge_ref[...] = edge


def join(spot, lists, words, prior, weight):
    tall = jax.ShapeDtypeStruct(prior.shape, F32)
    vmem = pl.BlockSpec(memory_space=pltpu.VMEM)
    smem = pl.BlockSpec(memory_space=pltpu.SMEM)
    return pl.pallas_call(
        join_kernel,
        out_shape=(tall, tall, jax.ShapeDtypeStruct((BINS, LANES), F32)),
        in_specs=[smem, smem, vmem, vmem, vmem],
        out_specs=(vmem, vmem, vmem),
        scratch_shapes=[pltpu.VMEM(words.shape, F32), pltpu.VMEM(words.shape, F32)],
        compiler_params=pltpu.CompilerParams(vmem_limit_bytes=32 << 20),
        name="join",
    )(spot, lists, words, prior, weight)


def silu(value):
    half = 0.5 * value
    return half + half * jnp.tanh(half)


def weight_matrices(taps_ref, matrix):
    layers, bins, taps = taps_ref.shape
    tap = lax.broadcasted_iota(I32, (taps, 3 * BINS), 0)
    place = lax.broadcasted_iota(I32, (taps, 3 * BINS), 1)
    out_bin = lax.broadcasted_iota(I32, (BINS, 3 * BINS), 0)
    in_bin = lax.broadcasted_iota(I32, (BINS, 3 * BINS), 1) & (BINS - 1)
    same = (out_bin // GROUP) == (in_bin // GROUP)
    wanted = (place & (GROUP - 1)) * 9 + (place // BINS) * 3
    for offset in range(3):
        chosen = (tap == wanted + offset).astype(F32).astype(BF16)
        for layer in range(layers):
            spread = jnp.dot(taps_ref[layer], chosen, preferred_element_type=F32)
            matrix[layer, BINS * offset : BINS * (offset + 1), :] = jnp.where(same, spread, 0.0).astype(BF16)


def refine_kernel(
    spot_ref, taps_ref, joined_ref, above_ref, below_ref, side_ref, out_ref, matrix, current, active, side_active
):
    row_index, col, last_row = spot_ref[0], spot_ref[1], spot_ref[2]
    weight_matrices(taps_ref, matrix)
    lane = lax.broadcasted_iota(I32, (BINS, LANES), 1)
    has_above = row_index > 0
    has_below = row_index < last_row
    inside = ((lane >= DEEP * DEEP) | has_above) & ((lane < (ROWS + DEEP) * DEEP) | has_below)
    edge_lane = jnp.where(col == 0, LANES - 1, 0)
    at_edge = lane == edge_lane
    near = jnp.where(col == 0, 0, DEEP - 1)

    side = side_ref[...]
    own = (lane >= DEEP * DEEP) & (lane < (ROWS + DEEP) * DEEP)
    side = jnp.where(own, side, 0.0)
    side = jnp.where(lane < DEEP * DEEP, pltpu.roll(above_ref[DEEP], LANES - ROWS * DEEP, 1), side)
    side = jnp.where(
        (lane >= (ROWS + DEEP) * DEEP) & (lane < EXT * DEEP), pltpu.roll(below_ref[DEEP], ROWS * DEEP, 1), side
    )
    side_current = side
    side_active[...] = jnp.where(inside, silu(side), 0.0).astype(BF16)

    for row in range(DEEP):
        current[row] = above_ref[row]
        current[ROWS + DEEP + row] = below_ref[row]
        active[0, row] = silu(above_ref[row]).astype(BF16)
        active[0, ROWS + DEEP + row] = silu(below_ref[row]).astype(BF16)

    def fill(row, carry):
        value = joined_ref[row]
        current[row + DEEP] = value
        active[0, row + DEEP] = silu(value).astype(BF16)
        return carry

    lax.fori_loop(0, ROWS, fill, 0, unroll=4)

    layers = taps_ref.shape[0]
    for layer in range(layers):
        now, later = layer % 2, (layer + 1) % 2
        taps = matrix[layer]
        inner = side_active[...].astype(F32)
        stack = jnp.concatenate(
            [pltpu.roll(inner, DEEP, 1), inner, pltpu.roll(inner, LANES - DEEP, 1)], axis=0
        ).astype(BF16)
        side_part = jnp.dot(taps, stack, preferred_element_type=F32)
        side_left, side_mid, side_right = (side_part[BINS * i : BINS * (i + 1)] for i in range(3))
        side_edge = jnp.where(col == 0, side_right, side_left)
        first = 1 + layer
        pairs = (EXT - 2 - 2 * layer) // 2
        final = layer == layers - 1

        def pair(step, injected):
            row = first + 2 * step
            planes = [active[now, row - 1 + i] for i in range(4)]
            stack = jnp.concatenate(
                [jnp.concatenate(planes[0:3], axis=0), jnp.concatenate(planes[1:4], axis=0)], axis=1
            )
            part = jnp.dot(taps, stack, preferred_element_type=F32)
            for i in range(2):
                here = row + i
                left, mid, right = (
                    part[BINS * k : BINS * (k + 1), LANES * i : LANES * (i + 1)] for k in range(3)
                )
                spot = here * DEEP + near
                moved = pltpu.roll(side_edge, (edge_lane - spot + LANES) % LANES, 1)
                response = mid + jnp.where(lane == 0, 0.0, pltpu.roll(left, 1, 1))
                response = response + jnp.where(lane == LANES - 1, 0.0, pltpu.roll(right, LANES - 1, 1))
                value = current[here] + (response + jnp.where(at_edge, moved, 0.0))
                if final:
                    out_ref[here - DEEP] = value
                else:
                    current[here] = value
                    keep = ((here >= DEEP) | has_above) & ((here < ROWS + DEEP) | has_below)
                    active[later, here] = jnp.where(keep, silu(value), 0.0).astype(BF16)
                    outward = jnp.where(col == 0, left, right)
                    thrown = pltpu.roll(outward, (spot - edge_lane + LANES) % LANES, 1)
                    injected = jnp.where(lane == spot, thrown, injected)
            return injected

        injected = lax.fori_loop(0, pairs, pair, jnp.zeros((BINS, LANES), F32))
        if not final:
            place = lane % DEEP
            from_left = jnp.where((place == 0) & (col == 0), injected, pltpu.roll(side_left, 1, 1))
            from_right = jnp.where((place == DEEP - 1) & (col != 0), injected, pltpu.roll(side_right, LANES - 1, 1))
            side_current = side_current + (side_mid + from_left + from_right)
            side_active[...] = jnp.where(inside, silu(side_current), 0.0).astype(BF16)


def refine(spot, taps, joined, above, below, side):
    vmem = pl.BlockSpec(memory_space=pltpu.VMEM)
    smem = pl.BlockSpec(memory_space=pltpu.SMEM)
    return pl.pallas_call(
        refine_kernel,
        out_shape=jax.ShapeDtypeStruct(joined.shape, F32),
        in_specs=[smem] + [vmem] * 5,
        out_specs=vmem,
        scratch_shapes=[
            pltpu.VMEM((taps.shape[0], 3 * BINS, 3 * BINS), BF16),
            pltpu.VMEM((EXT, BINS, LANES), F32),
            pltpu.VMEM((2, EXT, BINS, LANES), BF16),
            pltpu.VMEM((BINS, LANES), BF16),
        ],
        compiler_params=pltpu.CompilerParams(vmem_limit_bytes=32 << 20),
        name="refine",
    )(spot, taps, joined, above, below, side)


def on_device(tsdf_prior, prior_weight, depth_maps, confidence, frustum_tiles, pixel_index, conv_weights):
    row_count = lax.axis_size("row")
    spot = jnp.stack([lax.axis_index("row"), lax.axis_index("col"), jnp.int32(row_count - 1)]).astype(I32)
    readers = frustum_tiles.shape[1]
    pixels = pixel_index.reshape(-1)
    keys, origin = lax.sort((pixels, lax.iota(I32, pixels.shape[0])), num_keys=1, is_stable=False)
    words = lookup(
        keys.reshape(-1, LANES), depth_maps.reshape(-1, LANES), confidence.reshape(-1, LANES)
    )
    _, words = lax.sort((origin, words.reshape(-1)), num_keys=1, is_stable=False)
    lists = jnp.pad(frustum_tiles[0], ((0, 0), (0, LANES - 2)))[:, None, :]
    sent = jnp.concatenate([words.reshape(readers, 2, LANES), lists], axis=1)
    got = lax.all_to_all(sent, ("row", "col"), split_axis=0, concat_axis=0, tiled=True)
    joined, new_weight, edge = join(
        spot, got[:, 2, :2], got[:, :2, :].reshape(2 * readers, LANES), tsdf_prior, prior_weight
    )
    side = lax.ppermute(edge, "col", [(0, 1), (1, 0)])
    up = [(i, i + 1) for i in range(row_count - 1)]
    down = [(j, i) for i, j in up]
    above = lax.ppermute(jnp.concatenate([joined[ROWS - DEEP :], side[None]], axis=0), "row", up)
    below = lax.ppermute(jnp.concatenate([joined[:DEEP], side[None]], axis=0), "row", down)
    layers = conv_weights.shape[0]
    refined = refine(spot, conv_weights.reshape(layers, BINS, GROUP * 9), joined, above, below, side)
    return refined, new_weight


def solution(mesh):
    placed = (
        P("row", None, "col"),
        P("row", None, "col"),
        P("row", None),
        P("row", None),
        P(("row", "col"), None, None),
        P(("row", "col"), None, None, None),
        P(),
    )
    return jax.shard_map(
        on_device,
        mesh=mesh,
        in_specs=placed,
        out_specs=(P("row", None, "col"), P("row", None, "col")),
        check_vma=False,
    )
```

time: 595 us -> 164 us (0.28)
  local copies, waits for them, and re-layouts: 441 us -> 2.32 us
  Pallas kernels: 0 us -> 106 us
  starting transfers between devices: 71.1 us -> 17.5 us
  matrix products: 43.2 us -> 0 us
    gather x2 -> x0, local copies, waits for them, and re-layouts: 361 us -> none  [the longest x1 181 us: on_device(): certainty = jnp.take(confidence[0], places, axis=0)]
    pallas_call x0 -> x3, Pallas kernels: none -> 106 us  [the longest x1 78.8 us: lookup(): pl.pallas_call(lookup_kernel, out_shape=jax.ShapeDtypeStruct(keys.shape,...]
    dot_general x30 -> x0, matrix products: 43.2 us -> none  [the longest x27 20.9 us: convolve(): jnp.einsum('goi,hgiw->hgow', weights[:, :, :, row_offset, col_offset], gr...]
    ppermute x12 -> x3, starting transfers between devices: 45.1 us -> 6.58 us  [the longest x1 3.64 us: on_device(): lax.ppermute(jnp.concatenate([joined[:DEEP], side[None]], axis=0), 'row',...]
    unnamed x31 -> x12, local copies, waits for them, and re-layouts: 29.9 us -> 1.96 us
    dot_general x2 -> x0, local copies, waits for them, and re-layouts: 18.2 us -> none  [the longest x1 9.09 us: on_device(): jnp.dot(selector, observed.reshape(-1, bin_count * columns), precision=la...]
    sort x0 -> x2, other arithmetic: none -> 17.2 us  [the longest x1 8.72 us: on_device(): lax.sort((pixels, lax.iota(I32, pixels.shape[0])), num_keys=1, is_stable=...]
    all_to_all x3 -> x1, starting transfers between devices: 26 us -> 10.9 us  [on_device(): lax.all_to_all(sent, ('row', 'col'), split_axis=0, concat_axis=0, tiled=T...]
  transfers between devices with their start and end apart: 15 -> 4, of which waited for: 5 -> 4; matrix products, arithmetic and copies ran while one was open for 63% -> 0% of each run, Pallas kernels for 0% -> 0%
where the time goes in v1:
time: 164 us; the launch traced here: 163 us
  Pallas kernels  106 us (65%)
  waiting for transfers between devices  18.7 us (11%)
  other arithmetic  18.1 us (11%)
  starting transfers between devices  17.5 us (11%)
  local copies, waits for them, and re-layouts  2.32 us (1%)
    pallas_call x1, Pallas kernels, lookup(): pl.pallas_call(lookup_kernel, out_shape=jax.ShapeDtypeStruct(keys.shape,...  78.8 us
    pallas_call x1, Pallas kernels, refine(): pl.pallas_call(refine_kernel, out_shape=jax.ShapeDtypeStruct(joined.shape...  16.4 us
    all_to_all x1, starting transfers between devices, on_device(): lax.all_to_all(sent, ('row', 'col'), split_axis=0, concat_axis=0, tiled=T...  10.9 us
    pallas_call x1, Pallas kernels, join(): pl.pallas_call(join_kernel, out_shape=(tall, tall, jax.ShapeDtypeStruct((...  10.3 us
    all_to_all x1, waiting for transfers between devices, on_device(): lax.all_to_all(sent, ('row', 'col'), split_axis=0, concat_axis=0, tiled=T...  9.61 us
    sort x1, other arithmetic, on_device(): lax.sort((pixels, lax.iota(I32, pixels.shape[0])), num_keys=1, is_stable=...  8.72 us
    sort x1, other arithmetic, on_device(): lax.sort((origin, words.reshape(-1)), num_keys=1, is_stable=False)  8.46 us
    ppermute x1, waiting for transfers between devices, on_device(): lax.ppermute(jnp.concatenate([joined[ROWS - DEEP:], side[None]], axis=0),...  7.42 us
  transfers between devices with their start and end apart: 4, of which 4 were waited for; matrix products, arithmetic and copies ran while one was open for 0% of the time, Pallas kernels for 0%

profile of v1, /device:TPU:3, one launch (start us, length us, event | category | flops | bytes accessed | tf_op | source)
XLA Modules:
  0.0 163.0 jit_solution(14309978169694375390)
XLA Ops:
  0.6 0.0 copy-start.2
  0.6 0.8 copy.18
  1.5 8.7 %sort.30 = (s32[32768]{0:T(1024)S(1)}, s32[32768]{0:T(1024)S(1)}) sort(s32[32768]{0:T(1024)} %bitcast.28, s32[32768]{0:T(1024)S(1)} %iota.3), dimensions={0}, to_apply=%region_0.0 | sort | flops 491520 | bytes 524288 | tf_op jit(solution)/shard_map/sort | solution.py:256
  10.3 0.0 copy-start.3
  10.3 1.0 copy-done.3
  11.3 78.8 %lookup.1 = s32[256,128]{1,0:T(8,128)S(1)} custom-call(s32[256,128]{1,0:T(8,128)S(1)} %bitcast.21, s32[256,128]{1,0:T(8,128)S(1)} %bitcast.22, f32[1024,128]{1,0:T(8,128)S(1)} %bitcast.18, f32[1024,128]{1,0:T(8,128)S(1)} %bitcast.19), custom_call_target="tpu_custom_call" | custom-call | tf_op jit(solution)/shard_map/lookup/pallas_call | solution.py:43
  90.1 0.0 copy-start
  90.1 8.5 %sort.31 = (s32[32768]{0:T(1024)}, s32[32768]{0:T(1024)S(1)}) sort(s32[32768]{0:T(1024)S(1)} %get-tuple-element.8, s32[32768]{0:T(1024)S(1)} %bitcast.20), dimensions={0}, to_apply=%region_1.0 | sort | flops 491520 | bytes 524288 | tf_op jit(solution)/shard_map/sort | solution.py:260
  98.6 0.8 pad_add_fusion
  99.4 10.9 %all-to-all-start = ((s32[128,3,128]{2,1,0:T(4,128)}), s32[128,3,128]{2,1,0:T(4,128)S(1)}, u32[]{:S(2)}, u32[]{:S(2)}) async-start(s32[128,3,128]{2,1,0:T(4,128)} %pad_add_fusion), calls=%async_computation | async-start | bytes 524288 | tf_op jit(solution)/shard_map/all_to_all | solution.py:263
  110.3 0.1 pad_add_fusion.1.spot_ref
  110.4 9.6 %all-to-all-done = s32[128,3,128]{2,1,0:T(4,128)S(1)} async-done(((s32[128,3,128]{2,1,0:T(4,128)}), s32[128,3,128]{2,1,0:T(4,128)S(1)}, u32[]{:S(2)}, u32[]{:S(2)}) %all-to-all-start) | async-done | bytes 196640 | tf_op jit(solution)/shard_map/all_to_all | solution.py:263
  120.0 0.1 slice.16
  120.1 10.3 %join.1 = (f32[32,64,128]{2,1,0:T(8,128)S(1)}, f32[32,64,128]{2,1,0:T(8,128)}, f32[64,128]{1,0:T(8,128)S(1)}) custom-call(s32[3]{0:T(128)S(1)} %pad_add_fusion.1.spot_ref, s32[128,2]{1,0:T(8,128)S(1)} %bitcast.23, s32[256,128]{1,0:T(8,128)S(1)} %bitcast.17, f32[32,64,128]{2,1,0:T(8,128)S(1)} %copy-done, f32[32,64,128]{2,1,0:T(8,128)S(1)} %copy-done.1), custom_call_target="tpu_custom_call" | custom-call | tf_op jit(solution)/shard_map/join/pallas_call | solution.py:112
  130.5 1.0 collective-permute-start
  131.5 0.8 collective-permute-done.side_ref
  132.4 3.6 %collective-permute-start.2 = (f32[4,64,128]{2,1,0:T(8,128)S(1)}, f32[4,64,128]{2,1,0:T(8,128)S(1)}, u32[]{:S(2)}, u32[]{:S(2)}) collective-permute-start(f32[4,64,128]{2,1,0:T(8,128)S(1)} %get-tuple-element.16), channel_id=1, source_target_pairs={{2,0},{4,2},{6,4},{8,6},{10,8},{12,10},{14,12},{16,14},{18,16},{20... | collective-permute-start | bytes 393224 | tf_op jit(solution)/shard_map/ppermute | solution.py:271
  136.0 1.9 %collective-permute-start.1 = (f32[4,64,128]{2,1,0:T(8,128)S(1)}, f32[4,64,128]{2,1,0:T(8,128)S(1)}, u32[]{:S(2)}, u32[]{:S(2)}) collective-permute-start(f32[4,64,128]{2,1,0:T(8,128)S(1)} %get-tuple-element.17), channel_id=1, source_target_pairs={{0,2},{2,4},{4,6},{6,8},{8,10},{10,12},{12,14},{14,16},{16,18},{18... | collective-permute-start | bytes 393224 | tf_op jit(solution)/shard_map/ppermute | solution.py:270
  138.0 0.1 copy.17
  138.0 0.1 reshape.28
  138.1 0.1 copy.20.taps_ref
  138.2 0.9 collective-permute-done.2.below_ref
  139.1 7.4 %collective-permute-done.1.above_ref = f32[4,64,128]{2,1,0:T(8,128)S(1)} collective-permute-done((f32[4,64,128]{2,1,0:T(8,128)S(1)}, f32[4,64,128]{2,1,0:T(8,128)S(1)}, u32[]{:S(2)}, u32[]{:S(2)}) %collective-permute-start.1) | collective-permute-done | bytes 131104 | tf_op jit(solution)/shard_map/ppermute | solution.py:270
  146.5 16.4 %refine.1 = f32[32,64,128]{2,1,0:T(8,128)} custom-call(s32[3]{0:T(128)S(1)} %pad_add_fusion.1.spot_ref, bf16[3,64,144]{2,1,0:T(8,128)(2,1)S(1)} %copy.20.taps_ref, f32[32,64,128]{2,1,0:T(8,128)S(1)} %get-tuple-element.11.joined_ref, f32[4,64,128]{2,1,0:T(8,128)S(1)} %collective-permute-done.1.above_ref, f32[4,64,128]{2,1,0:T(8,128)S(1)} %collective-permute-done.2.below_ref, ...), custom_call_target="tpu_custom_call" | custom-call | tf_op jit(solution)/shard_map/refine/pallas_call | solution.py:235
  (11 shorter events, 0.1 us)
Async XLA Ops:
  0.6 9.6 %copy-start.2 = (f32[1,131072]{1,0:T(1,128)S(1)}, f32[1,131072]{1,0:T(1,128)}, u32[]{:S(2)}) copy-start(f32[1,131072]{1,0:T(1,128)} %param.9) | copy-start | bytes 1572868
  10.3 1.0 copy-start.3
  11.3 108.8 %copy-start.1 = (f32[32,64,128]{2,1,0:T(8,128)S(1)}, f32[32,64,128]{2,1,0:T(8,128)}, u32[]{:S(2)}) copy-start(f32[32,64,128]{2,1,0:T(8,128)} %weight_ref.1) | copy-start | bytes 3145732
  90.1 30.0 %copy-start = (f32[32,64,128]{2,1,0:T(8,128)S(1)}, f32[32,64,128]{2,1,0:T(8,128)}, u32[]{:S(2)}) copy-start(f32[32,64,128]{2,1,0:T(8,128)} %prior_ref.1) | copy-start | bytes 3145732
  99.4 20.6 %all-to-all-start = ((s32[128,3,128]{2,1,0:T(4,128)}), s32[128,3,128]{2,1,0:T(4,128)S(1)}, u32[]{:S(2)}, u32[]{:S(2)}) async-start(s32[128,3,128]{2,1,0:T(4,128)} %pad_add_fusion), calls=%async_computation | async-start | bytes 524288 | tf_op jit(solution)/shard_map/all_to_all | solution.py:263
  130.5 1.9 %collective-permute-start = (f32[64,128]{1,0:T(8,128)S(1)}, f32[64,128]{1,0:T(8,128)S(1)}, u32[]{:S(2)}, u32[]{:S(2)}) collective-permute-start(f32[64,128]{1,0:T(8,128)S(1)} %get-tuple-element.12), channel_id=1, source_target_pairs={{0,1},{1,0},{2,3},{3,2},{4,5},{5,4},{6,7},{7,6},{8,9},{9,8},{10,11... | collective-permute-start | bytes 98312 | tf_op jit(solution)/shard_map/ppermute | solution.py:267
  132.3 5.6 %copy-start.4 = (bf16[3,64,16,3,3]{1,2,4,3,0:T(8,128)(2,1)S(1)}, bf16[3,64,16,3,3]{1,2,4,3,0:T(8,128)(2,1)}, u32[]{:S(2)}) copy-start(bf16[3,64,16,3,3]{1,2,4,3,0:T(8,128)(2,1)} %param.13) | copy-start | bytes 165892
  132.4 6.8 %collective-permute-start.2 = (f32[4,64,128]{2,1,0:T(8,128)S(1)}, f32[4,64,128]{2,1,0:T(8,128)S(1)}, u32[]{:S(2)}, u32[]{:S(2)}) collective-permute-start(f32[4,64,128]{2,1,0:T(8,128)S(1)} %get-tuple-element.16), channel_id=1, source_target_pairs={{2,0},{4,2},{6,4},{8,6},{10,8},{12,10},{14,12},{16,14},{18,16},{20... | collective-permute-start | bytes 393224 | tf_op jit(solution)/shard_map/ppermute | solution.py:271
  136.0 10.5 %collective-permute-start.1 = (f32[4,64,128]{2,1,0:T(8,128)S(1)}, f32[4,64,128]{2,1,0:T(8,128)S(1)}, u32[]{:S(2)}, u32[]{:S(2)}) collective-permute-start(f32[4,64,128]{2,1,0:T(8,128)S(1)} %get-tuple-element.17), channel_id=1, source_target_pairs={{0,2},{2,4},{4,6},{6,8},{8,10},{10,12},{12,14},{14,16},{16,18},{18... | collective-permute-start | bytes 393224 | tf_op jit(solution)/shard_map/ppermute | solution.py:270

commit v2 on v1

--- a/solution.py
+++ b/solution.py
@@ -22,21 +22,36 @@
     high = (height_ref[...] * H_SCALE + 0.5).astype(I32) - 32768
     low = (conf_ref[...] * C_SCALE + 0.5).astype(I32)
     table[...] = (high << 16) | low
-    for block in range(key_ref.shape[0] // 8):
-        index = key_ref[8 * block : 8 * block + 8, :]
-        lane = index & (LANES - 1)
-        line = index >> 7
-        first = key_smem[8 * block, 0] >> 7
-        last = key_smem[8 * block + 7, LANES - 1] >> 7
-
-        def step(row, found):
-            words = jnp.broadcast_to(table[pl.ds(row, 1), :], (8, LANES))
-            taken = jnp.take_along_axis(words, lane, axis=1)
-            return jnp.where(line == row, taken, found)
-
-        out_ref[8 * block : 8 * block + 8, :] = lax.fori_loop(
-            first, last + 1, step, jnp.zeros((8, LANES), I32)
-        )
+    blocks = key_ref.shape[0] // 8
+    chunks = table.shape[0] // 8
+    together = 8
+
+    def steps(index, carry):
+        chunk, block = carry
+        found = []
+        for _ in range(together):
+            rows = pl.ds(pl.multiple_of(block * 8, 8), 8)
+            place = key_ref[rows, :]
+            lane = place & (LANES - 1)
+            line = place >> 7
+            value = jnp.zeros((8, LANES), I32)
+            for offset in range(8):
+                row = chunk * 8 + offset
+                words = jnp.broadcast_to(table[pl.ds(row, 1), :], (8, LANES))
+                taken = jnp.take_along_axis(words, lane, axis=1)
+                value = jnp.where(line == row, taken, value)
+            found.append((rows, (place >> 10) == chunk, value))
+            last = key_smem[8 * block + 7, LANES - 1] >> 10
+            after = jnp.minimum(block + 1, blocks - 1)
+            stay = last > chunk
+            follow = key_smem[8 * after, 0] >> 10
+            chunk = jnp.where(stay, chunk + 1, follow)
+            block = jnp.where(stay, block, after)
+        for rows, mine, value in found:
+            out_ref[rows, :] = jnp.where(mine, value, out_ref[rows, :])
+        return chunk, block
+
+    lax.fori_loop(0, (blocks + chunks) // together, steps, (key_smem[0, 0] >> 10, jnp.int32(0)))
 
 
 def lookup(keys, heights, confidence):

time: 164 us -> 91.6 us (0.56)
  Pallas kernels: 106 us -> 33.2 us
    pallas_call x1, Pallas kernels: 78.8 us -> 6.41 us  [lookup(): pl.pallas_call(lookup_kernel, out_shape=jax.ShapeDtypeStruct(keys.shape,...]
where the time goes in v2:
time: 91.6 us; the launch traced here: 90.6 us
  Pallas kernels  33.2 us (36%)
  waiting for transfers between devices  18.7 us (20%)
  other arithmetic  18.1 us (20%)
  starting transfers between devices  17.4 us (19%)
  local copies, waits for them, and re-layouts  2.32 us (3%)
    pallas_call x1, Pallas kernels, refine(): pl.pallas_call(refine_kernel, out_shape=jax.ShapeDtypeStruct(joined.shape...  16.4 us
    all_to_all x1, starting transfers between devices, on_device(): lax.all_to_all(sent, ('row', 'col'), split_axis=0, concat_axis=0, tiled=T...  10.8 us
    pallas_call x1, Pallas kernels, join(): pl.pallas_call(join_kernel, out_shape=(tall, tall, jax.ShapeDtypeStruct((...  10.4 us
    all_to_all x1, waiting for transfers between devices, on_device(): lax.all_to_all(sent, ('row', 'col'), split_axis=0, concat_axis=0, tiled=T...  9.61 us
    sort x1, other arithmetic, on_device(): lax.sort((pixels, lax.iota(I32, pixels.shape[0])), num_keys=1, is_stable=...  8.72 us
    sort x1, other arithmetic, on_device(): lax.sort((origin, words.reshape(-1)), num_keys=1, is_stable=False)  8.46 us
    ppermute x1, waiting for transfers between devices, on_device(): lax.ppermute(jnp.concatenate([joined[ROWS - DEEP:], side[None]], axis=0),...  7.35 us
    pallas_call x1, Pallas kernels, lookup(): pl.pallas_call(lookup_kernel, out_shape=jax.ShapeDtypeStruct(keys.shape,...  6.41 us
  transfers between devices with their start and end apart: 4, of which 4 were waited for; matrix products, arithmetic and copies ran while one was open for 0% of the time, Pallas kernels for 0%

profile of v2, /device:TPU:3, one launch (start us, length us, event | category | flops | bytes accessed | tf_op | source)
XLA Modules:
  0.0 90.6 jit_solution(15649458657645319728)
XLA Ops:
  0.6 0.0 copy-start.2
  0.6 0.8 copy.18
  1.5 8.7 %sort.30 = (s32[32768]{0:T(1024)S(1)}, s32[32768]{0:T(1024)S(1)}) sort(s32[32768]{0:T(1024)} %bitcast.28, s32[32768]{0:T(1024)S(1)} %iota.3), dimensions={0}, to_apply=%region_0.0 | sort | flops 491520 | bytes 524288 | tf_op jit(solution)/shard_map/sort | solution.py:271
  10.3 0.0 copy-start.3
  10.3 1.0 %copy-done.3 = f32[1,131072]{1,0:T(1,128)S(1)} copy-done((f32[1,131072]{1,0:T(1,128)S(1)}, f32[1,131072]{1,0:T(1,128)}, u32[]{:S(2)}) %copy-start.3) | copy-done | bytes 524312
  11.3 6.4 %lookup.1 = s32[256,128]{1,0:T(8,128)S(1)} custom-call(s32[256,128]{1,0:T(8,128)S(1)} %bitcast.21, s32[256,128]{1,0:T(8,128)S(1)} %bitcast.22, f32[1024,128]{1,0:T(8,128)S(1)} %bitcast.18, f32[1024,128]{1,0:T(8,128)S(1)} %bitcast.19), custom_call_target="tpu_custom_call" | custom-call | tf_op jit(solution)/shard_map/lookup/pallas_call | solution.py:58
  17.7 0.0 copy-start
  17.7 8.5 %sort.31 = (s32[32768]{0:T(1024)}, s32[32768]{0:T(1024)S(1)}) sort(s32[32768]{0:T(1024)S(1)} %get-tuple-element.8, s32[32768]{0:T(1024)S(1)} %bitcast.20), dimensions={0}, to_apply=%region_1.0 | sort | flops 491520 | bytes 524288 | tf_op jit(solution)/shard_map/sort | solution.py:275
  26.2 0.8 pad_add_fusion
  27.0 10.8 %all-to-all-start = ((s32[128,3,128]{2,1,0:T(4,128)}), s32[128,3,128]{2,1,0:T(4,128)S(1)}, u32[]{:S(2)}, u32[]{:S(2)}) async-start(s32[128,3,128]{2,1,0:T(4,128)} %pad_add_fusion), calls=%async_computation | async-start | bytes 524288 | tf_op jit(solution)/shard_map/all_to_all | solution.py:278
  37.9 0.1 pad_add_fusion.1.spot_ref
  37.9 9.6 %all-to-all-done = s32[128,3,128]{2,1,0:T(4,128)S(1)} async-done(((s32[128,3,128]{2,1,0:T(4,128)}), s32[128,3,128]{2,1,0:T(4,128)S(1)}, u32[]{:S(2)}, u32[]{:S(2)}) %all-to-all-start) | async-done | bytes 196640 | tf_op jit(solution)/shard_map/all_to_all | solution.py:278
  47.5 0.1 slice.16
  47.7 10.4 %join.1 = (f32[32,64,128]{2,1,0:T(8,128)S(1)}, f32[32,64,128]{2,1,0:T(8,128)}, f32[64,128]{1,0:T(8,128)S(1)}) custom-call(s32[3]{0:T(128)S(1)} %pad_add_fusion.1.spot_ref, s32[128,2]{1,0:T(8,128)S(1)} %bitcast.23, s32[256,128]{1,0:T(8,128)S(1)} %bitcast.17, f32[32,64,128]{2,1,0:T(8,128)S(1)} %copy-done, f32[32,64,128]{2,1,0:T(8,128)S(1)} %copy-done.1), custom_call_target="tpu_custom_call" | custom-call | tf_op jit(solution)/shard_map/join/pallas_call | solution.py:127
  58.1 1.1 %collective-permute-start = (f32[64,128]{1,0:T(8,128)S(1)}, f32[64,128]{1,0:T(8,128)S(1)}, u32[]{:S(2)}, u32[]{:S(2)}) collective-permute-start(f32[64,128]{1,0:T(8,128)S(1)} %get-tuple-element.12), channel_id=1, source_target_pairs={{0,1},{1,0},{2,3},{3,2},{4,5},{5,4},{6,7},{7,6},{8,9},{9,8},{10,11... | collective-permute-start | bytes 98312 | tf_op jit(solution)/shard_map/ppermute | solution.py:282
  59.2 0.8 collective-permute-done.side_ref
  60.0 3.6 %collective-permute-start.2 = (f32[4,64,128]{2,1,0:T(8,128)S(1)}, f32[4,64,128]{2,1,0:T(8,128)S(1)}, u32[]{:S(2)}, u32[]{:S(2)}) collective-permute-start(f32[4,64,128]{2,1,0:T(8,128)S(1)} %get-tuple-element.16), channel_id=1, source_target_pairs={{2,0},{4,2},{6,4},{8,6},{10,8},{12,10},{14,12},{16,14},{18,16},{20... | collective-permute-start | bytes 393224 | tf_op jit(solution)/shard_map/ppermute | solution.py:286
  63.6 1.9 %collective-permute-start.1 = (f32[4,64,128]{2,1,0:T(8,128)S(1)}, f32[4,64,128]{2,1,0:T(8,128)S(1)}, u32[]{:S(2)}, u32[]{:S(2)}) collective-permute-start(f32[4,64,128]{2,1,0:T(8,128)S(1)} %get-tuple-element.17), channel_id=1, source_target_pairs={{0,2},{2,4},{4,6},{6,8},{8,10},{10,12},{12,14},{14,16},{16,18},{18... | collective-permute-start | bytes 393224 | tf_op jit(solution)/shard_map/ppermute | solution.py:285
  65.6 0.1 copy.17
  65.6 0.1 reshape.28
  65.7 0.1 copy.20.taps_ref
  65.8 0.9 %collective-permute-done.2.below_ref = f32[4,64,128]{2,1,0:T(8,128)S(1)} collective-permute-done((f32[4,64,128]{2,1,0:T(8,128)S(1)}, f32[4,64,128]{2,1,0:T(8,128)S(1)}, u32[]{:S(2)}, u32[]{:S(2)}) %collective-permute-start.2) | collective-permute-done | bytes 131104 | tf_op jit(solution)/shard_map/ppermute | solution.py:286
  66.8 7.4 %collective-permute-done.1.above_ref = f32[4,64,128]{2,1,0:T(8,128)S(1)} collective-permute-done((f32[4,64,128]{2,1,0:T(8,128)S(1)}, f32[4,64,128]{2,1,0:T(8,128)S(1)}, u32[]{:S(2)}, u32[]{:S(2)}) %collective-permute-start.1) | collective-permute-done | bytes 131104 | tf_op jit(solution)/shard_map/ppermute | solution.py:285
  74.1 16.4 %refine.1 = f32[32,64,128]{2,1,0:T(8,128)} custom-call(s32[3]{0:T(128)S(1)} %pad_add_fusion.1.spot_ref, bf16[3,64,144]{2,1,0:T(8,128)(2,1)S(1)} %copy.20.taps_ref, f32[32,64,128]{2,1,0:T(8,128)S(1)} %get-tuple-element.11.joined_ref, f32[4,64,128]{2,1,0:T(8,128)S(1)} %collective-permute-done.1.above_ref, f32[4,64,128]{2,1,0:T(8,128)S(1)} %collective-permute-done.2.below_ref, ...), custom_call_target="tpu_custom_call" | custom-call | tf_op jit(solution)/shard_map/refine/pallas_call | solution.py:250
  (11 shorter events, 0.1 us)
Async XLA Ops:
  0.6 9.6 %copy-start.2 = (f32[1,131072]{1,0:T(1,128)S(1)}, f32[1,131072]{1,0:T(1,128)}, u32[]{:S(2)}) copy-start(f32[1,131072]{1,0:T(1,128)} %param.9) | copy-start | bytes 1572868
  10.3 1.0 %copy-start.3 = (f32[1,131072]{1,0:T(1,128)S(1)}, f32[1,131072]{1,0:T(1,128)}, u32[]{:S(2)}) copy-start(f32[1,131072]{1,0:T(1,128)} %param.10) | copy-start | bytes 1572868
  11.3 36.4 %copy-start.1 = (f32[32,64,128]{2,1,0:T(8,128)S(1)}, f32[32,64,128]{2,1,0:T(8,128)}, u32[]{:S(2)}) copy-start(f32[32,64,128]{2,1,0:T(8,128)} %weight_ref.1) | copy-start | bytes 3145732
  17.7 30.0 %copy-start = (f32[32,64,128]{2,1,0:T(8,128)S(1)}, f32[32,64,128]{2,1,0:T(8,128)}, u32[]{:S(2)}) copy-start(f32[32,64,128]{2,1,0:T(8,128)} %prior_ref.1) | copy-start | bytes 3145732
  27.0 20.5 %all-to-all-start = ((s32[128,3,128]{2,1,0:T(4,128)}), s32[128,3,128]{2,1,0:T(4,128)S(1)}, u32[]{:S(2)}, u32[]{:S(2)}) async-start(s32[128,3,128]{2,1,0:T(4,128)} %pad_add_fusion), calls=%async_computation | async-start | bytes 524288 | tf_op jit(solution)/shard_map/all_to_all | solution.py:278
  58.1 1.9 %collective-permute-start = (f32[64,128]{1,0:T(8,128)S(1)}, f32[64,128]{1,0:T(8,128)S(1)}, u32[]{:S(2)}, u32[]{:S(2)}) collective-permute-start(f32[64,128]{1,0:T(8,128)S(1)} %get-tuple-element.12), channel_id=1, source_target_pairs={{0,1},{1,0},{2,3},{3,2},{4,5},{5,4},{6,7},{7,6},{8,9},{9,8},{10,11... | collective-permute-start | bytes 98312 | tf_op jit(solution)/shard_map/ppermute | solution.py:282
  60.0 5.5 %copy-start.4 = (bf16[3,64,16,3,3]{1,2,4,3,0:T(8,128)(2,1)S(1)}, bf16[3,64,16,3,3]{1,2,4,3,0:T(8,128)(2,1)}, u32[]{:S(2)}) copy-start(bf16[3,64,16,3,3]{1,2,4,3,0:T(8,128)(2,1)} %param.13) | copy-start | bytes 165892
  60.0 6.8 %collective-permute-start.2 = (f32[4,64,128]{2,1,0:T(8,128)S(1)}, f32[4,64,128]{2,1,0:T(8,128)S(1)}, u32[]{:S(2)}, u32[]{:S(2)}) collective-permute-start(f32[4,64,128]{2,1,0:T(8,128)S(1)} %get-tuple-element.16), channel_id=1, source_target_pairs={{2,0},{4,2},{6,4},{8,6},{10,8},{12,10},{14,12},{16,14},{18,16},{20... | collective-permute-start | bytes 393224 | tf_op jit(solution)/shard_map/ppermute | solution.py:286
  63.6 10.5 %collective-permute-start.1 = (f32[4,64,128]{2,1,0:T(8,128)S(1)}, f32[4,64,128]{2,1,0:T(8,128)S(1)}, u32[]{:S(2)}, u32[]{:S(2)}) collective-permute-start(f32[4,64,128]{2,1,0:T(8,128)S(1)} %get-tuple-element.17), channel_id=1, source_target_pairs={{0,2},{2,4},{4,6},{6,8},{8,10},{10,12},{12,14},{14,16},{16,18},{18... | collective-permute-start | bytes 393224 | tf_op jit(solution)/shard_map/ppermute | solution.py:285

commit v3 on v2

--- a/solution.py
+++ b/solution.py
@@ -11,6 +11,8 @@
 DEEP = 3
 EXT = ROWS + 2 * DEEP
 GROUP = 16
+TOGETHER = 18
+AT_ONCE = 4
 H_SCALE = 1023.0
 C_SCALE = 13000.0
 F32 = jnp.float32
@@ -18,101 +20,227 @@
 I32 = jnp.int32
 
 
-def lookup_kernel(key_smem, key_ref, height_ref, conf_ref, out_ref, table):
-    high = (height_ref[...] * H_SCALE + 0.5).astype(I32) - 32768
-    low = (conf_ref[...] * C_SCALE + 0.5).astype(I32)
+BY_BLOCK = [("v", 0), ("v", 1), ("v", 2), ("v", 3), ("s", 0), ("s", 1), ("s", 2), ("l", 0), ("l", 1), ("l", 2)]
+BY_BLOCK += [("v", 4), ("l", 3), ("l", 4), ("l", 5), ("l", 6)]
+BY_LANE = [("v", i) for i in range(5)] + [("s", i) for i in range(3)] + [("l", i) for i in range(7)]
+REGISTERS = 32
+LAG = 8
+
+
+def along(kind):
+    return lax.broadcasted_iota(I32, (8, LANES), 0 if kind == "s" else 1)
+
+
+def exchange(parts, kind, bit):
+    distance = 1 << bit
+    if kind == "v":
+        parts = list(parts)
+        for low in range(REGISTERS):
+            if low & distance == 0:
+                one, two = parts[low], parts[low | distance]
+                parts[low], parts[low | distance] = jnp.minimum(one, two), jnp.maximum(one, two)
+        return parts
+    axis = 0 if kind == "s" else 1
+    size = (8, LANES)[axis]
+    upper = (along(kind) & distance) != 0
+    result = []
+    for part in parts:
+        from_low = pltpu.roll(part, distance, axis)
+        from_high = from_low if 2 * distance == size else pltpu.roll(part, size - distance, axis)
+        result.append(jnp.where(upper, jnp.maximum(part, from_low), jnp.minimum(part, from_high)))
+    return result
+
+
+def turn(parts, places):
+    fixed = [bit for kind, bit in places if kind == "v"]
+    mask = None
+    for kind, bit in places:
+        if kind != "v":
+            one = -((along(kind) >> bit) & 1)
+            mask = one if mask is None else mask ^ one
+    result = []
+    for register, part in enumerate(parts):
+        if sum((register >> bit) & 1 for bit in fixed) % 2:
+            part = ~part
+        result.append(part if mask is None else part ^ mask)
+    return result
+
+
+def sort_steps(order):
+    size = len(order)
+    for phase in range(1, size + 1):
+        yield "turn", [order[place] for place in (phase - 1, phase) if 0 < place < size and phase + place > 1]
+        for place in range(phase - 1, -1, -1):
+            yield "exchange", order[place]
+
+
+def advance(parts, step):
+    kind, what = step
+    return turn(parts, what) if kind == "turn" else exchange(parts, *what)
+
+
+def sample_kernel(pixel_ref, wanted_ref, height_hbm, conf_hbm, out_ref, maps, table, blocks, found, edges, bounds, sems):
+    copies = [
+        pltpu.make_async_copy(height_hbm, maps.at[0], sems.at[0]),
+        pltpu.make_async_copy(conf_hbm, maps.at[1], sems.at[1]),
+    ]
+    for copy in copies:
+        copy.start()
+    parts = []
+    for register in range(REGISTERS):
+        pixel = pixel_ref[8 * register : 8 * register + 8, :]
+        place = ((along("s") & 1) << 4) + (register >> 1)
+        place = place + ((4 * (register & 1) + (along("s") >> 1)) << 5) + (along("l") << 8)
+        parts.append(((pixel - 65536) << 15) | place)
+    for step in sort_steps(BY_BLOCK):
+        parts = advance(parts, step)
+    for i, register in enumerate((0, 16, 15, 31)):
+        edges[8 * i : 8 * i + 8, :] = parts[register]
+    to_scalar = pltpu.make_async_copy(edges, bounds, sems.at[2])
+    to_scalar.start()
+    for half in range(2):
+        turned = jnp.concatenate(parts[16 * half : 16 * half + 16], axis=0).T
+        for i in range(16):
+            blocks[8 * (2 * i + half) : 8 * (2 * i + half) + 8, :] = turned[8 * i : 8 * i + 8, :]
+    for copy in copies:
+        copy.wait()
+    high = (maps[0] * H_SCALE + 0.5).astype(I32) - 32768
+    low = (maps[1] * C_SCALE + 0.5).astype(I32)
     table[...] = (high << 16) | low
-    blocks = key_ref.shape[0] // 8
+    to_scalar.wait()
     chunks = table.shape[0] // 8
     together = 8
 
-    def steps(index, carry):
+    def first_chunk(block):
+        return (bounds[8 * (block & 1), 8 * (block >> 1)] >> 25) + 64
+
+    def last_chunk(block):
+        return (bounds[23 + 8 * (block & 1), 8 * (block >> 1) + 7] >> 25) + 64
+
+    def walk(index, carry):
         chunk, block = carry
-        found = []
+        pending = []
         for _ in range(together):
             rows = pl.ds(pl.multiple_of(block * 8, 8), 8)
-            place = key_ref[rows, :]
-            lane = place & (LANES - 1)
-            line = place >> 7
+            key = blocks[rows, :]
+            lane = (key >> 15) & (LANES - 1)
+            line = (key >> 22) + 512
             value = jnp.zeros((8, LANES), I32)
             for offset in range(8):
                 row = chunk * 8 + offset
                 words = jnp.broadcast_to(table[pl.ds(row, 1), :], (8, LANES))
                 taken = jnp.take_along_axis(words, lane, axis=1)
                 value = jnp.where(line == row, taken, value)
-            found.append((rows, (place >> 10) == chunk, value))
-            last = key_smem[8 * block + 7, LANES - 1] >> 10
-            after = jnp.minimum(block + 1, blocks - 1)
-            stay = last > chunk
-            follow = key_smem[8 * after, 0] >> 10
-            chunk = jnp.where(stay, chunk + 1, follow)
+            pending.append((rows, (line >> 3) == chunk, value))
+            after = jnp.minimum(block + 1, REGISTERS - 1)
+            stay = last_chunk(block) > chunk
+            chunk = jnp.where(stay, chunk + 1, first_chunk(after))
             block = jnp.where(stay, block, after)
-        for rows, mine, value in found:
-            out_ref[rows, :] = jnp.where(mine, value, out_ref[rows, :])
+        for rows, mine, value in pending:
+            found[rows, :] = jnp.where(mine, value, found[rows, :])
         return chunk, block
 
-    lax.fori_loop(0, (blocks + chunks) // together, steps, (key_smem[0, 0] >> 10, jnp.int32(0)))
-
-
-def lookup(keys, heights, confidence):
+    lax.fori_loop(0, (REGISTERS + chunks) // together, walk, (first_chunk(0), jnp.int32(0)))
+    highs, lows = [], []
+    for register in range(REGISTERS):
+        rows = slice(8 * register, 8 * register + 8)
+        place = ((blocks[rows, :] & 32767) - 16384) << 16
+        word = found[rows, :]
+        highs.append(place | ((word >> 16) & 0xFFFF))
+        lows.append(place | (word & 0xFFFF))
+    steps = list(sort_steps(BY_LANE))
+    for i in range(len(steps) + LAG):
+        if i < len(steps):
+            highs = advance(highs, steps[i])
+        if i >= LAG:
+            lows = advance(lows, steps[i - LAG])
+    for register in range(REGISTERS):
+        slot, owner = register >> 4, 8 * (register & 15)
+        out_ref[pl.ds(3 * owner + slot, 8, stride=3), :] = (highs[register] << 16) | (lows[register] & 0xFFFF)
+    wanted = jnp.concatenate([wanted_ref[...], jnp.zeros((LANES - 2, LANES), I32)], axis=0).T
+    for owner in range(0, LANES, 8):
+        out_ref[pl.ds(3 * owner + 2, 8, stride=3), :] = wanted[owner : owner + 8, :]
+
+
+def sample(pixels, wanted, heights, confidence):
+    flat = pltpu.VMEM(pixels.shape, I32)
     return pl.pallas_call(
-        lookup_kernel,
-        out_shape=jax.ShapeDtypeStruct(keys.shape, I32),
+        sample_kernel,
+        out_shape=jax.ShapeDtypeStruct((3 * wanted.shape[1], LANES), I32),
         in_specs=[
-            pl.BlockSpec(memory_space=pltpu.SMEM),
             pl.BlockSpec(memory_space=pltpu.VMEM),
             pl.BlockSpec(memory_space=pltpu.VMEM),
-            pl.BlockSpec(memory_space=pltpu.VMEM),
+            pl.BlockSpec(memory_space=pl.ANY),
+            pl.BlockSpec(memory_space=pl.ANY),
         ],
         out_specs=pl.BlockSpec(memory_space=pltpu.VMEM),
-        scratch_shapes=[pltpu.VMEM(heights.shape, I32)],
-        compiler_params=pltpu.CompilerParams(vmem_limit_bytes=32 << 20),
-        name="lookup",
-    )(keys, keys, heights, confidence)
+        scratch_shapes=[
+            pltpu.VMEM((2,) + heights.shape, F32),
+            pltpu.VMEM(heights.shape, I32),
+            flat,
+            flat,
+            pltpu.VMEM((32, LANES), I32),
+            pltpu.SMEM((32, LANES), I32),
+            pltpu.SemaphoreType.DMA((3,)),
+        ],
+        compiler_params=pltpu.CompilerParams(vmem_limit_bytes=60 << 20),
+        name="sample",
+    )(pixels, wanted, heights, confidence)
 
 
 def join_kernel(
-    spot_ref, list_ref, words_ref, prior_ref, weight_ref, joined_ref, new_ref, edge_ref, height, certainty
+    spot_ref, list_ref, words_ref, prior_ref, weight_ref, joined_ref, new_ref, edge_ref, order_ref, height, certainty
 ):
     col = spot_ref[1]
+    entries = words_ref.shape[0]
     word = words_ref[...]
-    height[...] = ((word >> 16) + 32768).astype(F32) * (0.25 / H_SCALE)
-    certainty[...] = (word & 0xFFFF).astype(F32) * (1.0 / C_SCALE)
+    height[0:entries, :] = ((word >> 16) + 32768).astype(F32) * (0.5 / H_SCALE)
+    certainty[0:entries, :] = (word & 0xFFFF).astype(F32) * (0.5 / C_SCALE)
+    height[entries:, :] = jnp.zeros((8, LANES), F32)
+    certainty[entries:, :] = jnp.zeros((8, LANES), F32)
     new_ref[...] = weight_ref[...]
-    joined_ref[...] = weight_ref[...] * prior_ref[...]
-    level = lax.broadcasted_iota(I32, (BINS, LANES), 0).astype(F32) * 0.25
-
-    def term(reader, slot):
-        tile = list_ref[reader, slot]
-        prior = prior_ref[jnp.maximum(tile, 0)]
-        scaled = height[pl.ds(2 * reader + slot, 1), :] - level
-        signed = jnp.clip(scaled, -1.0, 1.0)
-        visible = jnp.clip(scaled + 2.0, 0.0, 1.0)
-        mismatch = signed - prior
-        spread = 1.0 + 4.0 * (mismatch * mismatch)
+    joined_ref[...] = (2.0 * weight_ref[...]) * prior_ref[...]
+    level = lax.broadcasted_iota(I32, (BINS, LANES), 0).astype(F32) * 0.5
+
+    def pick(reader, count):
+        for slot in range(2):
+            tile = list_ref[reader, slot]
+            order_ref[count] = tile * 512 + (3 * reader + slot)
+            count = count + jnp.where(tile >= 0, 1, 0)
+        return count
+
+    count = lax.fori_loop(0, list_ref.shape[0], pick, jnp.int32(0), unroll=4)
+    for i in range(AT_ONCE):
+        order_ref[count + i] = entries
+
+    def term(place):
+        code = order_ref[place]
+        tile = code >> 9
+        entry = code & 511
+        prior = prior_ref[tile]
+        scaled = height[pl.ds(entry, 1), :] - level
+        signed = jnp.clip(scaled, -2.0, 2.0)
+        visible = jnp.clip(scaled + 4.0, 0.0, 2.0)
+        mismatch = signed - (prior + prior)
+        spread = 1.0 + mismatch * mismatch
         inverse = pl.reciprocal(spread, approx=True)
         inverse = inverse * (2.0 - spread * inverse)
-        observed = (certainty[pl.ds(2 * reader + slot, 1), :] * visible) * inverse
+        observed = (certainty[pl.ds(entry, 1), :] * visible) * inverse
         return tile, observed, observed * signed
 
-    def add(tile, observed, weighted):
-        @pl.when(tile >= 0)
-        def _():
+    def step(index, carry):
+        terms = [term(AT_ONCE * index + i) for i in range(AT_ONCE)]
+        for tile, observed, weighted in terms:
             new_ref[tile] += observed
             joined_ref[tile] += weighted
-
-    def step(reader, carry):
-        terms = [term(reader, slot) for slot in range(2)]
-        for one in terms:
-            add(*one)
         return carry
 
-    lax.fori_loop(0, list_ref.shape[0], step, 0)
+    lax.fori_loop(0, (count + AT_ONCE - 1) // AT_ONCE, step, 0)
     lane = lax.broadcasted_iota(I32, (BINS, LANES), 1)
     source = jnp.where(col == 0, LANES - DEEP, 0)
     edge = jnp.zeros((BINS, LANES), F32)
     for row in range(ROWS):
-        value = joined_ref[row] / new_ref[row]
+        value = (0.5 * joined_ref[row]) / new_ref[row]
         joined_ref[row] = value
         start = (row + DEEP) * DEEP
         moved = pltpu.roll(value, (start - source + LANES) % LANES, 1)
@@ -129,7 +257,8 @@
         out_shape=(tall, tall, jax.ShapeDtypeStruct((BINS, LANES), F32)),
         in_specs=[smem, smem, vmem, vmem, vmem],
         out_specs=(vmem, vmem, vmem),
-        scratch_shapes=[pltpu.VMEM(words.shape, F32), pltpu.VMEM(words.shape, F32)],
+        scratch_shapes=[pltpu.SMEM((2 * lists.shape[0] + AT_ONCE,), I32)]
+        + [pltpu.VMEM((words.shape[0] + 8, LANES), F32)] * 2,
         compiler_params=pltpu.CompilerParams(vmem_limit_bytes=32 << 20),
         name="join",
     )(spot, lists, words, prior, weight)
@@ -235,7 +364,15 @@
                     injected = jnp.where(lane == spot, thrown, injected)
             return injected
 
-        injected = lax.fori_loop(0, pairs, pair, jnp.zeros((BINS, LANES), F32))
+        def several(step, injected):
+            for i in range(TOGETHER):
+                injected = pair(TOGETHER * step + i, injected)
+            return injected
+
+        full = pairs // TOGETHER
+        injected = lax.fori_loop(0, full, several, jnp.zeros((BINS, LANES), F32))
+        for step in range(full * TOGETHER, pairs):
+            injected = pair(step, injected)
         if not final:
             place = lane % DEEP
             from_left = jnp.where((place == 0) & (col == 0), injected, pltpu.roll(side_left, 1, 1))
@@ -267,17 +404,16 @@
     row_count = lax.axis_size("row")
     spot = jnp.stack([lax.axis_index("row"), lax.axis_index("col"), jnp.int32(row_count - 1)]).astype(I32)
     readers = frustum_tiles.shape[1]
-    pixels = pixel_index.reshape(-1)
-    keys, origin = lax.sort((pixels, lax.iota(I32, pixels.shape[0])), num_keys=1, is_stable=False)
-    words = lookup(
-        keys.reshape(-1, LANES), depth_maps.reshape(-1, LANES), confidence.reshape(-1, LANES)
+    both = ("row", "col")
+    words = sample(
+        pixel_index.reshape(-1, LANES),
+        frustum_tiles[0].T,
+        depth_maps.reshape(-1, LANES),
+        confidence.reshape(-1, LANES),
     )
-    _, words = lax.sort((origin, words.reshape(-1)), num_keys=1, is_stable=False)
-    lists = jnp.pad(frustum_tiles[0], ((0, 0), (0, LANES - 2)))[:, None, :]
-    sent = jnp.concatenate([words.reshape(readers, 2, LANES), lists], axis=1)
-    got = lax.all_to_all(sent, ("row", "col"), split_axis=0, concat_axis=0, tiled=True)
+    got = lax.all_to_all(words.reshape(readers, 1, 3 * LANES), both, split_axis=0, concat_axis=0, tiled=True)
     joined, new_weight, edge = join(
-        spot, got[:, 2, :2], got[:, :2, :].reshape(2 * readers, LANES), tsdf_prior, prior_weight
+        spot, got[:, 0, 2 * LANES : 2 * LANES + 2], got.reshape(3 * readers, LANES), tsdf_prior, prior_weight
     )
     side = lax.ppermute(edge, "col", [(0, 1), (1, 0)])
     up = [(i, i + 1) for i in range(row_count - 1)]

time: 91.6 us -> 68.5 us (0.75)
  other arithmetic: 18.1 us -> 0.09 us
  Pallas kernels: 33.2 us -> 29.1 us
    sort x2 -> x0, other arithmetic: 17.2 us -> none  [the longest x1 8.72 us: on_device(): lax.sort((pixels, lax.iota(I32, pixels.shape[0])), num_keys=1, is_stable=...]
    pallas_call x1, Pallas kernels: 16.4 us -> 6.35 us  [refine(): pl.pallas_call(refine_kernel, out_shape=jax.ShapeDtypeStruct(joined.shape...]
    pallas_call x1, Pallas kernels: 6.41 us -> 14.8 us  [sample(): pl.pallas_call(sample_kernel, out_shape=jax.ShapeDtypeStruct((3 * wanted....]
    pallas_call x1, Pallas kernels: 10.4 us -> 7.92 us  [join(): pl.pallas_call(join_kernel, out_shape=(tall, tall, jax.ShapeDtypeStruct((...]
    unnamed x12 -> x7, local copies, waits for them, and re-layouts: 1.96 us -> 1.29 us
  transfers between devices with their start and end apart: 4 -> 4, of which waited for: 4 -> 4; matrix products, arithmetic and copies ran while one was open for 0% -> 1% of each run, Pallas kernels for 0% -> 0%
where the time goes in v3:
time: 68.5 us; the launch traced here: 67.5 us
  Pallas kernels  29.1 us (42%)
  waiting for transfers between devices  18.4 us (27%)
  starting transfers between devices  17.6 us (26%)
  local copies, waits for them, and re-layouts  1.56 us (2%)
  between operations  0.73 us (1%)
    pallas_call x1, Pallas kernels, sample(): pl.pallas_call(sample_kernel, out_shape=jax.ShapeDtypeStruct((3 * wanted....  14.8 us
    all_to_all x1, starting transfers between devices, on_device(): lax.all_to_all(words.reshape(readers, 1, 3 * LANES), both, split_axis=0,...  10.8 us
    all_to_all x1, waiting for transfers between devices, on_device(): lax.all_to_all(words.reshape(readers, 1, 3 * LANES), both, split_axis=0,...  9.24 us
    pallas_call x1, Pallas kernels, join(): pl.pallas_call(join_kernel, out_shape=(tall, tall, jax.ShapeDtypeStruct((...  7.92 us
    ppermute x1, waiting for transfers between devices, on_device(): lax.ppermute(jnp.concatenate([joined[ROWS - DEEP:], side[None]], axis=0),...  7.83 us
    pallas_call x1, Pallas kernels, refine(): pl.pallas_call(refine_kernel, out_shape=jax.ShapeDtypeStruct(joined.shape...  6.35 us
    ppermute x1, starting transfers between devices, on_device(): lax.ppermute(jnp.concatenate([joined[:DEEP], side[None]], axis=0), 'row',...  3.84 us
    ppermute x1, starting transfers between devices, on_device(): lax.ppermute(jnp.concatenate([joined[ROWS - DEEP:], side[None]], axis=0),...  2.1 us
  transfers between devices with their start and end apart: 4, of which 4 were waited for; matrix products, arithmetic and copies ran while one was open for 1% of the time, Pallas kernels for 0%

profile of v3, /device:TPU:3, one launch (start us, length us, event | category | flops | bytes accessed | tf_op | source)
XLA Modules:
  0.0 67.5 jit_solution(13153257374139683939)
XLA Ops:
  0.6 0.0 copy-start
  0.6 14.8 %sample.1 = s32[384,128]{1,0:T(8,128)} custom-call(s32[256,128]{1,0:T(8,128)} %bitcast.22, s32[2,128]{1,0:T(2,128)} %bitcast.23, f32[1024,128]{1,0:T(8,128)} %bitcast.20, f32[1024,128]{1,0:T(8,128)} %bitcast.21), custom_call_target="tpu_custom_call" | custom-call | tf_op jit(solution)/shard_map/sample/pallas_call | solution.py:167
  15.5 10.8 %all-to-all-start = ((s32[128,1,384]{2,1,0:T(1,128)}), s32[128,1,384]{2,1,0:T(1,128)S(1)}, u32[]{:S(2)}, u32[]{:S(2)}) async-start(s32[128,1,384]{2,1,0:T(1,128)} %bitcast.19), calls=%async_computation | async-start | bytes 393216 | tf_op jit(solution)/shard_map/all_to_all | solution.py:414
  26.3 0.1 pad_add_fusion.spot_ref
  26.4 9.2 %all-to-all-done = s32[128,1,384]{2,1,0:T(1,128)S(1)} async-done(((s32[128,1,384]{2,1,0:T(1,128)}), s32[128,1,384]{2,1,0:T(1,128)S(1)}, u32[]{:S(2)}, u32[]{:S(2)}) %all-to-all-start) | async-done | bytes 196640 | tf_op jit(solution)/shard_map/all_to_all | solution.py:414
  35.7 0.0 copy-done
  35.7 0.0 copy-start.1
  35.7 1.2 %copy-done.1 = f32[32,64,128]{2,1,0:T(8,128)S(1)} copy-done((f32[32,64,128]{2,1,0:T(8,128)S(1)}, f32[32,64,128]{2,1,0:T(8,128)}, u32[]{:S(2)}) %copy-start.1) | copy-done | bytes 1048600
  37.0 7.9 %join.1 = (f32[32,64,128]{2,1,0:T(8,128)S(1)}, f32[32,64,128]{2,1,0:T(8,128)}, f32[64,128]{1,0:T(8,128)S(1)}) custom-call(s32[3]{0:T(128)S(1)} %pad_add_fusion.spot_ref, s32[128,2]{1,0:T(8,128)S(1)} %bitcast.17, s32[384,128]{1,0:T(8,128)S(1)} %bitcast.16, f32[32,64,128]{2,1,0:T(8,128)S(1)} %copy-done, f32[32,64,128]{2,1,0:T(8,128)S(1)} %copy-done.1), custom_call_target="tpu_custom_call" | custom-call | tf_op jit(solution)/shard_map/join/pallas_call | solution.py:255
  44.9 0.8 %collective-permute-start = (f32[64,128]{1,0:T(8,128)S(1)}, f32[64,128]{1,0:T(8,128)S(1)}, u32[]{:S(2)}, u32[]{:S(2)}) collective-permute-start(f32[64,128]{1,0:T(8,128)S(1)} %get-tuple-element.6), channel_id=1, source_target_pairs={{0,1},{1,0},{2,3},{3,2},{4,5},{5,4},{6,7},{7,6},{8,9},{9,8},{10,11... | collective-permute-start | bytes 98312 | tf_op jit(solution)/shard_map/ppermute | solution.py:418
  45.7 0.8 %collective-permute-done.side_ref = f32[64,128]{1,0:T(8,128)S(1)} collective-permute-done((f32[64,128]{1,0:T(8,128)S(1)}, f32[64,128]{1,0:T(8,128)S(1)}, u32[]{:S(2)}, u32[]{:S(2)}) %collective-permute-start) | collective-permute-done | bytes 32800 | tf_op jit(solution)/shard_map/ppermute | solution.py:418
  46.5 0.0 copy-start.2
  46.6 3.8 %collective-permute-start.2 = (f32[4,64,128]{2,1,0:T(8,128)S(1)}, f32[4,64,128]{2,1,0:T(8,128)S(1)}, u32[]{:S(2)}, u32[]{:S(2)}) collective-permute-start(f32[4,64,128]{2,1,0:T(8,128)S(1)} %get-tuple-element.10), channel_id=1, source_target_pairs={{2,0},{4,2},{6,4},{8,6},{10,8},{12,10},{14,12},{16,14},{18,16},{20... | collective-permute-start | bytes 393224 | tf_op jit(solution)/shard_map/ppermute | solution.py:422
  50.4 2.1 %collective-permute-start.1 = (f32[4,64,128]{2,1,0:T(8,128)S(1)}, f32[4,64,128]{2,1,0:T(8,128)S(1)}, u32[]{:S(2)}, u32[]{:S(2)}) collective-permute-start(f32[4,64,128]{2,1,0:T(8,128)S(1)} %get-tuple-element.11), channel_id=1, source_target_pairs={{0,2},{2,4},{4,6},{6,8},{8,10},{10,12},{12,14},{14,16},{16,18},{18... | collective-permute-start | bytes 393224 | tf_op jit(solution)/shard_map/ppermute | solution.py:421
  52.5 0.0 copy-done.2
  52.5 0.1 copy.12
  52.6 0.1 reshape.22
  52.7 0.1 copy.15.taps_ref
  52.8 0.5 collective-permute-done.2.below_ref
  53.3 7.8 %collective-permute-done.1.above_ref = f32[4,64,128]{2,1,0:T(8,128)S(1)} collective-permute-done((f32[4,64,128]{2,1,0:T(8,128)S(1)}, f32[4,64,128]{2,1,0:T(8,128)S(1)}, u32[]{:S(2)}, u32[]{:S(2)}) %collective-permute-start.1) | collective-permute-done | bytes 131104 | tf_op jit(solution)/shard_map/ppermute | solution.py:421
  61.2 6.3 %refine.1 = f32[32,64,128]{2,1,0:T(8,128)} custom-call(s32[3]{0:T(128)S(1)} %pad_add_fusion.spot_ref, bf16[3,64,144]{2,1,0:T(8,128)(2,1)S(1)} %copy.15.taps_ref, f32[32,64,128]{2,1,0:T(8,128)S(1)} %get-tuple-element.5.joined_ref, f32[4,64,128]{2,1,0:T(8,128)S(1)} %collective-permute-done.1.above_ref, f32[4,64,128]{2,1,0:T(8,128)S(1)} %collective-permute-done.2.below_ref, ...), custom_call_target="tpu_custom_call" | custom-call | tf_op jit(solution)/shard_map/refine/pallas_call | solution.py:387
  (3 shorter events, 0.1 us)
Async XLA Ops:
  0.6 35.1 %copy-start = (f32[32,64,128]{2,1,0:T(8,128)S(1)}, f32[32,64,128]{2,1,0:T(8,128)}, u32[]{:S(2)}) copy-start(f32[32,64,128]{2,1,0:T(8,128)} %prior_ref.1) | copy-start | bytes 3145732
  15.5 20.2 %all-to-all-start = ((s32[128,1,384]{2,1,0:T(1,128)}), s32[128,1,384]{2,1,0:T(1,128)S(1)}, u32[]{:S(2)}, u32[]{:S(2)}) async-start(s32[128,1,384]{2,1,0:T(1,128)} %bitcast.19), calls=%async_computation | async-start | bytes 393216 | tf_op jit(solution)/shard_map/all_to_all | solution.py:414
  35.7 1.2 %copy-start.1 = (f32[32,64,128]{2,1,0:T(8,128)S(1)}, f32[32,64,128]{2,1,0:T(8,128)}, u32[]{:S(2)}) copy-start(f32[32,64,128]{2,1,0:T(8,128)} %weight_ref.1) | copy-start | bytes 3145732
  44.9 1.7 %collective-permute-start = (f32[64,128]{1,0:T(8,128)S(1)}, f32[64,128]{1,0:T(8,128)S(1)}, u32[]{:S(2)}, u32[]{:S(2)}) collective-permute-start(f32[64,128]{1,0:T(8,128)S(1)} %get-tuple-element.6), channel_id=1, source_target_pairs={{0,1},{1,0},{2,3},{3,2},{4,5},{5,4},{6,7},{7,6},{8,9},{9,8},{10,11... | collective-permute-start | bytes 98312 | tf_op jit(solution)/shard_map/ppermute | solution.py:418
  46.5 6.0 %copy-start.2 = (bf16[3,64,16,3,3]{1,2,4,3,0:T(8,128)(2,1)S(1)}, bf16[3,64,16,3,3]{1,2,4,3,0:T(8,128)(2,1)}, u32[]{:S(2)}) copy-start(bf16[3,64,16,3,3]{1,2,4,3,0:T(8,128)(2,1)} %param.13) | copy-start | bytes 165892
  46.6 6.8 %collective-permute-start.2 = (f32[4,64,128]{2,1,0:T(8,128)S(1)}, f32[4,64,128]{2,1,0:T(8,128)S(1)}, u32[]{:S(2)}, u32[]{:S(2)}) collective-permute-start(f32[4,64,128]{2,1,0:T(8,128)S(1)} %get-tuple-element.10), channel_id=1, source_target_pairs={{2,0},{4,2},{6,4},{8,6},{10,8},{12,10},{14,12},{16,14},{18,16},{20... | collective-permute-start | bytes 393224 | tf_op jit(solution)/shard_map/ppermute | solution.py:422
  50.4 10.7 %collective-permute-start.1 = (f32[4,64,128]{2,1,0:T(8,128)S(1)}, f32[4,64,128]{2,1,0:T(8,128)S(1)}, u32[]{:S(2)}, u32[]{:S(2)}) collective-permute-start(f32[4,64,128]{2,1,0:T(8,128)S(1)} %get-tuple-element.11), channel_id=1, source_target_pairs={{0,2},{2,4},{4,6},{6,8},{8,10},{10,12},{12,14},{14,16},{16,18},{18... | collective-permute-start | bytes 393224 | tf_op jit(solution)/shard_map/ppermute | solution.py:421

commit v4 on v3

--- a/solution.py
+++ b/solution.py
@@ -13,6 +13,8 @@
 GROUP = 16
 TOGETHER = 18
 AT_ONCE = 4
+WIDTH = 5
+JOIN_VMEM = 16
 H_SCALE = 1023.0
 C_SCALE = 13000.0
 F32 = jnp.float32
@@ -154,19 +156,43 @@
             highs = advance(highs, steps[i])
         if i >= LAG:
             lows = advance(lows, steps[i - LAG])
+    owners = wanted_ref.shape[1]
+    blank = jnp.zeros((1, LANES), I32)
+    for owner in range(2):
+        out_ref[WIDTH * owner + 3 : WIDTH * owner + 4, :] = blank
+        out_ref[WIDTH * (owners - 1 - owner) + 2 : WIDTH * (owners - 1 - owner) + 3, :] = blank
     for register in range(REGISTERS):
         slot, owner = register >> 4, 8 * (register & 15)
-        out_ref[pl.ds(3 * owner + slot, 8, stride=3), :] = (highs[register] << 16) | (lows[register] & 0xFFFF)
-    wanted = jnp.concatenate([wanted_ref[...], jnp.zeros((LANES - 2, LANES), I32)], axis=0).T
-    for owner in range(0, LANES, 8):
-        out_ref[pl.ds(3 * owner + 2, 8, stride=3), :] = wanted[owner : owner + 8, :]
+        word = (highs[register] << 16) | (lows[register] & 0xFFFF)
+        out_ref[pl.ds(WIDTH * owner + slot, 8, stride=WIDTH), :] = word
+        if slot == 0 and owner == 0:
+            out_ref[pl.ds(2, 6, stride=WIDTH), :] = word[2:8]
+        elif slot == 0:
+            out_ref[pl.ds(WIDTH * (owner - 2) + 2, 8, stride=WIDTH), :] = word
+        elif owner == owners - 8:
+            out_ref[pl.ds(WIDTH * (owner + 2) + 3, 6, stride=WIDTH), :] = word[0:6]
+        else:
+            out_ref[pl.ds(WIDTH * (owner + 2) + 3, 8, stride=WIDTH), :] = word
+    lane = lax.broadcasted_iota(I32, (1, LANES), 1)
+    first, second = wanted_ref[0:1, :], wanted_ref[1:2, :]
+    below = pltpu.roll(jnp.broadcast_to(first, (8, LANES)), LANES - 2, 1)[0:1]
+    above = pltpu.roll(jnp.broadcast_to(second, (8, LANES)), 2, 1)[0:1]
+    tiles = [
+        jnp.where(first >= 0, first + DEEP, -1),
+        jnp.where(second >= 0, second + DEEP, -1),
+        jnp.where((below >= 0) & (below < DEEP) & (lane < owners - 2), below + (ROWS + DEEP), -1),
+        jnp.where((above >= ROWS - DEEP) & (lane >= 2), above - (ROWS - DEEP), -1),
+    ]
+    turned = jnp.concatenate(tiles + [jnp.zeros((LANES - 4, LANES), I32)], axis=0).T
+    for owner in range(0, owners, 8):
+        out_ref[pl.ds(WIDTH * owner + WIDTH - 1, 8, stride=WIDTH), :] = turned[owner : owner + 8, :]
 
 
 def sample(pixels, wanted, heights, confidence):
     flat = pltpu.VMEM(pixels.shape, I32)
     return pl.pallas_call(
         sample_kernel,
-        out_shape=jax.ShapeDtypeStruct((3 * wanted.shape[1], LANES), I32),
+        out_shape=jax.ShapeDtypeStruct((WIDTH * wanted.shape[1], LANES), I32),
         in_specs=[
             pl.BlockSpec(memory_space=pltpu.VMEM),
             pl.BlockSpec(memory_space=pltpu.VMEM),
@@ -189,8 +215,17 @@
 
 
 def join_kernel(
-    spot_ref, list_ref, words_ref, prior_ref, weight_ref, joined_ref, new_ref, edge_ref, order_ref, height, certainty
+    spot_ref, list_ref, words_ref, above_ref, below_ref, prior_hbm, weight_hbm,
+    joined_ref, new_ref, edge_ref,
+    order_ref, height, certainty, prior_ref, total, sems,
 ):
+    inner = pl.ds(DEEP, ROWS)
+    copies = [
+        pltpu.make_async_copy(prior_hbm, prior_ref.at[inner], sems.at[0]),
+        pltpu.make_async_copy(weight_hbm, total.at[inner], sems.at[1]),
+    ]
+    for copy in copies:
+        copy.start()
     col = spot_ref[1]
     entries = words_ref.shape[0]
     word = words_ref[...]
@@ -198,25 +233,31 @@
     certainty[0:entries, :] = (word & 0xFFFF).astype(F32) * (0.5 / C_SCALE)
     height[entries:, :] = jnp.zeros((8, LANES), F32)
     certainty[entries:, :] = jnp.zeros((8, LANES), F32)
-    new_ref[...] = weight_ref[...]
-    joined_ref[...] = (2.0 * weight_ref[...]) * prior_ref[...]
     level = lax.broadcasted_iota(I32, (BINS, LANES), 0).astype(F32) * 0.5
 
     def pick(reader, count):
-        for slot in range(2):
+        for slot in range(WIDTH - 1):
             tile = list_ref[reader, slot]
-            order_ref[count] = tile * 512 + (3 * reader + slot)
+            order_ref[count] = tile * 1024 + (WIDTH * reader + slot)
             count = count + jnp.where(tile >= 0, 1, 0)
         return count
 
     count = lax.fori_loop(0, list_ref.shape[0], pick, jnp.int32(0), unroll=4)
     for i in range(AT_ONCE):
         order_ref[count + i] = entries
+    for copy in copies:
+        copy.wait()
+    for row in range(DEEP):
+        prior_ref[row] = above_ref[row]
+        prior_ref[ROWS + DEEP + row] = below_ref[row]
+        total[row] = above_ref[DEEP + row]
+        total[ROWS + DEEP + row] = below_ref[DEEP + row]
+    joined_ref[...] = (2.0 * total[...]) * prior_ref[...]
 
     def term(place):
         code = order_ref[place]
-        tile = code >> 9
-        entry = code & 511
+        tile = code >> 10
+        entry = code & 1023
         prior = prior_ref[tile]
         scaled = height[pl.ds(entry, 1), :] - level
         signed = jnp.clip(scaled, -2.0, 2.0)
@@ -231,37 +272,58 @@
     def step(index, carry):
         terms = [term(AT_ONCE * index + i) for i in range(AT_ONCE)]
         for tile, observed, weighted in terms:
-            new_ref[tile] += observed
+            total[tile] += observed
             joined_ref[tile] += weighted
         return carry
 
     lax.fori_loop(0, (count + AT_ONCE - 1) // AT_ONCE, step, 0)
     lane = lax.broadcasted_iota(I32, (BINS, LANES), 1)
     source = jnp.where(col == 0, LANES - DEEP, 0)
+    has_above = spot_ref[0] > 0
+    has_below = spot_ref[0] < spot_ref[2]
     edge = jnp.zeros((BINS, LANES), F32)
-    for row in range(ROWS):
-        value = (0.5 * joined_ref[row]) / new_ref[row]
+    for row in range(EXT):
+        value = (0.5 * joined_ref[row]) / total[row]
+        if row < DEEP:
+            value = jnp.where(has_above, value, 0.0)
+        elif row >= ROWS + DEEP:
+            value = jnp.where(has_below, value, 0.0)
+        else:
+            new_ref[row - DEEP] = total[row]
         joined_ref[row] = value
-        start = (row + DEEP) * DEEP
+        start = row * DEEP
         moved = pltpu.roll(value, (start - source + LANES) % LANES, 1)
         edge = jnp.where((lane >= start) & (lane < start + DEEP), moved, edge)
     edge_ref[...] = edge
 
 
-def join(spot, lists, words, prior, weight):
-    tall = jax.ShapeDtypeStruct(prior.shape, F32)
+def join(spot, lists, words, above, below, prior, weight):
+    rows, bins, lanes = prior.shape
+    tall = (rows + 2 * DEEP, bins, lanes)
     vmem = pl.BlockSpec(memory_space=pltpu.VMEM)
     smem = pl.BlockSpec(memory_space=pltpu.SMEM)
+    anywhere = pl.BlockSpec(memory_space=pl.ANY)
+    column = pltpu.VMEM((words.shape[0] + 8, LANES), F32)
     return pl.pallas_call(
         join_kernel,
-        out_shape=(tall, tall, jax.ShapeDtypeStruct((BINS, LANES), F32)),
-        in_specs=[smem, smem, vmem, vmem, vmem],
+        out_shape=(
+            jax.ShapeDtypeStruct(tall, F32),
+            jax.ShapeDtypeStruct(prior.shape, F32),
+            jax.ShapeDtypeStruct((BINS, LANES), F32),
+        ),
+        in_specs=[smem, smem, vmem, vmem, vmem, anywhere, anywhere],
         out_specs=(vmem, vmem, vmem),
-        scratch_shapes=[pltpu.SMEM((2 * lists.shape[0] + AT_ONCE,), I32)]
-        + [pltpu.VMEM((words.shape[0] + 8, LANES), F32)] * 2,
-        compiler_params=pltpu.CompilerParams(vmem_limit_bytes=32 << 20),
+        scratch_shapes=[
+            pltpu.SMEM(((WIDTH - 1) * lists.shape[0] + AT_ONCE,), I32),
+            column,
+            column,
+            pltpu.VMEM(tall, F32),
+            pltpu.VMEM(tall, F32),
+            pltpu.SemaphoreType.DMA((2,)),
+        ],
+        compiler_params=pltpu.CompilerParams(vmem_limit_bytes=JOIN_VMEM << 20),
         name="join",
-    )(spot, lists, words, prior, weight)
+    )(spot, lists, words, above, below, prior, weight)
 
 
 def silu(value):
@@ -285,7 +347,7 @@
 
 
 def refine_kernel(
-    spot_ref, taps_ref, joined_ref, above_ref, below_ref, side_ref, out_ref, matrix, current, active, side_active
+    spot_ref, taps_ref, joined_ref, side_ref, out_ref, matrix, current, active, side_active
 ):
     row_index, col, last_row = spot_ref[0], spot_ref[1], spot_ref[2]
     weight_matrices(taps_ref, matrix)
@@ -297,29 +359,14 @@
     at_edge = lane == edge_lane
     near = jnp.where(col == 0, 0, DEEP - 1)
 
-    side = side_ref[...]
-    own = (lane >= DEEP * DEEP) & (lane < (ROWS + DEEP) * DEEP)
-    side = jnp.where(own, side, 0.0)
-    side = jnp.where(lane < DEEP * DEEP, pltpu.roll(above_ref[DEEP], LANES - ROWS * DEEP, 1), side)
-    side = jnp.where(
-        (lane >= (ROWS + DEEP) * DEEP) & (lane < EXT * DEEP), pltpu.roll(below_ref[DEEP], ROWS * DEEP, 1), side
-    )
-    side_current = side
-    side_active[...] = jnp.where(inside, silu(side), 0.0).astype(BF16)
-
-    for row in range(DEEP):
-        current[row] = above_ref[row]
-        current[ROWS + DEEP + row] = below_ref[row]
-        active[0, row] = silu(above_ref[row]).astype(BF16)
-        active[0, ROWS + DEEP + row] = silu(below_ref[row]).astype(BF16)
+    side_current = side_ref[...]
+    side_active[...] = silu(side_current).astype(BF16)
 
     def fill(row, carry):
-        value = joined_ref[row]
-        current[row + DEEP] = value
-        active[0, row + DEEP] = silu(value).astype(BF16)
+        active[0, row] = silu(joined_ref[row]).astype(BF16)
         return carry
 
-    lax.fori_loop(0, ROWS, fill, 0, unroll=4)
+    lax.fori_loop(0, EXT, fill, 0, unroll=EXT // 2)
 
     layers = taps_ref.shape[0]
     for layer in range(layers):
@@ -352,7 +399,8 @@
                 moved = pltpu.roll(side_edge, (edge_lane - spot + LANES) % LANES, 1)
                 response = mid + jnp.where(lane == 0, 0.0, pltpu.roll(left, 1, 1))
                 response = response + jnp.where(lane == LANES - 1, 0.0, pltpu.roll(right, LANES - 1, 1))
-                value = current[here] + (response + jnp.where(at_edge, moved, 0.0))
+                before = joined_ref[here] if layer == 0 else current[here]
+                value = before + (response + jnp.where(at_edge, moved, 0.0))
                 if final:
                     out_ref[here - DEEP] = value
                 else:
@@ -381,13 +429,13 @@
             side_active[...] = jnp.where(inside, silu(side_current), 0.0).astype(BF16)
 
 
-def refine(spot, taps, joined, above, below, side):
+def refine(spot, taps, joined, side):
     vmem = pl.BlockSpec(memory_space=pltpu.VMEM)
     smem = pl.BlockSpec(memory_space=pltpu.SMEM)
     return pl.pallas_call(
         refine_kernel,
-        out_shape=jax.ShapeDtypeStruct(joined.shape, F32),
-        in_specs=[smem] + [vmem] * 5,
+        out_shape=jax.ShapeDtypeStruct((ROWS,) + joined.shape[1:], F32),
+        in_specs=[smem] + [vmem] * 3,
         out_specs=vmem,
         scratch_shapes=[
             pltpu.VMEM((taps.shape[0], 3 * BINS, 3 * BINS), BF16),
@@ -395,9 +443,9 @@
             pltpu.VMEM((2, EXT, BINS, LANES), BF16),
             pltpu.VMEM((BINS, LANES), BF16),
         ],
-        compiler_params=pltpu.CompilerParams(vmem_limit_bytes=32 << 20),
+        compiler_params=pltpu.CompilerParams(vmem_limit_bytes=16 << 20),
         name="refine",
-    )(spot, taps, joined, above, below, side)
+    )(spot, taps, joined, side)
 
 
 def on_device(tsdf_prior, prior_weight, depth_maps, confidence, frustum_tiles, pixel_index, conv_weights):
@@ -411,17 +459,25 @@
         depth_maps.reshape(-1, LANES),
         confidence.reshape(-1, LANES),
     )
-    got = lax.all_to_all(words.reshape(readers, 1, 3 * LANES), both, split_axis=0, concat_axis=0, tiled=True)
+    width = WIDTH * LANES
+    got = lax.all_to_all(words.reshape(readers, 1, width), both, split_axis=0, concat_axis=0, tiled=True)
+    up = [(i, i + 1) for i in range(row_count - 1)]
+    down = [(j, i) for i, j in up]
+    above = lax.ppermute(jnp.concatenate([tsdf_prior[ROWS - DEEP :], prior_weight[ROWS - DEEP :]], axis=0), "row", up)
+    below = lax.ppermute(jnp.concatenate([tsdf_prior[:DEEP], prior_weight[:DEEP]], axis=0), "row", down)
+    start = (WIDTH - 1) * LANES
     joined, new_weight, edge = join(
-        spot, got[:, 0, 2 * LANES : 2 * LANES + 2], got.reshape(3 * readers, LANES), tsdf_prior, prior_weight
+        spot,
+        got[:, 0, start : start + WIDTH - 1],
+        got.reshape(WIDTH * readers, LANES),
+        above,
+        below,
+        tsdf_prior,
+        prior_weight,
     )
     side = lax.ppermute(edge, "col", [(0, 1), (1, 0)])
-    up = [(i, i + 1) for i in range(row_count - 1)]
-    down = [(j, i) for i, j in up]
-    above = lax.ppermute(jnp.concatenate([joined[ROWS - DEEP :], side[None]], axis=0), "row", up)
-    below = lax.ppermute(jnp.concatenate([joined[:DEEP], side[None]], axis=0), "row", down)
     layers = conv_weights.shape[0]
-    refined = refine(spot, conv_weights.reshape(layers, BINS, GROUP * 9), joined, above, below, side)
+    refined = refine(spot, conv_weights.reshape(layers, BINS, GROUP * 9), joined, side)
     return refined, new_weight
 
 

time: 68.5 us -> 61 us (0.89)
  waiting for transfers between devices: 18.4 us -> 4.48 us
  starting transfers between devices: 17.6 us -> 21.4 us
  Pallas kernels: 29.1 us -> 31 us
  local copies, waits for them, and re-layouts: 1.56 us -> 2.7 us
    all_to_all x1, waiting for transfers between devices: 9.24 us -> 0.72 us  [on_device(): lax.all_to_all(words.reshape(readers, 1, width), both, split_axis=0, conc...]
    ppermute x2, waiting for transfers between devices: 8.33 us -> 3.19 us  [the longest x1 3.18 us: on_device(): lax.ppermute(jnp.concatenate([tsdf_prior[ROWS - DEEP:], prior_weight[ROWS...]
    ppermute x2, starting transfers between devices: 5.94 us -> 9.5 us  [the longest x1 6.41 us: on_device(): lax.ppermute(jnp.concatenate([tsdf_prior[:DEEP], prior_weight[:DEEP]], ax...]
    pallas_call x3, Pallas kernels: 29.1 us -> 31 us  [the longest x1 15 us: sample(): pl.pallas_call(sample_kernel, out_shape=jax.ShapeDtypeStruct((WIDTH * wan...]
    unnamed x7 -> x11, local copies, waits for them, and re-layouts: 1.29 us -> 2.41 us
  transfers between devices with their start and end apart: 4 -> 4, of which waited for: 4 -> 3; matrix products, arithmetic and copies ran while one was open for 1% -> 1% of each run, Pallas kernels for 0% -> 0%
where the time goes in v4:
time: 61 us; the launch traced here: 60.4 us
  Pallas kernels  31 us (51%)
  starting transfers between devices  21.4 us (35%)
  waiting for transfers between devices  4.48 us (7%)
  local copies, waits for them, and re-layouts  2.7 us (4%)
  between operations  0.76 us (1%)
    pallas_call x1, Pallas kernels, sample(): pl.pallas_call(sample_kernel, out_shape=jax.ShapeDtypeStruct((WIDTH * wan...  15 us
    all_to_all x1, starting transfers between devices, on_device(): lax.all_to_all(words.reshape(readers, 1, width), both, split_axis=0, conc...  10.8 us
    pallas_call x1, Pallas kernels, join(): pl.pallas_call(join_kernel, out_shape=(jax.ShapeDtypeStruct(tall, F32), j...  9.63 us
    ppermute x1, starting transfers between devices, on_device(): lax.ppermute(jnp.concatenate([tsdf_prior[:DEEP], prior_weight[:DEEP]], ax...  6.41 us
    pallas_call x1, Pallas kernels, refine(): pl.pallas_call(refine_kernel, out_shape=jax.ShapeDtypeStruct((ROWS,) + jo...  6.36 us
    ppermute x1, waiting for transfers between devices, on_device(): lax.ppermute(jnp.concatenate([tsdf_prior[ROWS - DEEP:], prior_weight[ROWS...  3.18 us
    ppermute x1, starting transfers between devices, on_device(): lax.ppermute(jnp.concatenate([tsdf_prior[ROWS - DEEP:], prior_weight[ROWS...  3.1 us
    unnamed x11, local copies, waits for them, and re-layouts  2.41 us
  transfers between devices with their start and end apart: 4, of which 3 were waited for; matrix products, arithmetic and copies ran while one was open for 1% of the time, Pallas kernels for 0%

profile of v4, /device:TPU:3, one launch (start us, length us, event | category | flops | bytes accessed | tf_op | source)
XLA Modules:
  0.0 60.4 jit_solution(6427659419761615767)
XLA Ops:
  0.6 0.0 copy-start.1
  0.6 0.0 copy-start
  0.7 15.0 %sample.1 = s32[640,128]{1,0:T(8,128)} custom-call(s32[256,128]{1,0:T(8,128)} %bitcast.20, s32[2,128]{1,0:T(2,128)} %bitcast.21, f32[1024,128]{1,0:T(8,128)} %bitcast.18, f32[1024,128]{1,0:T(8,128)} %bitcast.19), custom_call_target="tpu_custom_call" | custom-call | tf_op jit(solution)/shard_map/sample/pallas_call | solution.py:193
  15.6 10.8 %all-to-all-start = ((s32[128,1,640]{2,1,0:T(1,128)}), s32[128,1,640]{2,1,0:T(1,128)S(1)}, u32[]{:S(2)}, u32[]{:S(2)}) async-start(s32[128,1,640]{2,1,0:T(1,128)} %bitcast.17), calls=%async_computation | async-start | bytes 655360 | tf_op jit(solution)/shard_map/all_to_all | solution.py:463
  26.5 0.0 copy-done.1
  26.5 0.0 copy-done
  26.5 3.1 %collective-permute-start = (f32[6,64,128]{2,1,0:T(8,128)S(1)}, f32[6,64,128]{2,1,0:T(8,128)S(1)}, u32[]{:S(2)}, u32[]{:S(2)}) collective-permute-start(f32[6,64,128]{2,1,0:T(8,128)S(1)} %pad_maximum_fusion), channel_id=1, source_target_pairs={{0,2},{2,4},{4,6},{6,8},{8,10},{10,12},{12,14},{14,16},{16,18},{18... | collective-permute-start | bytes 589832 | tf_op jit(solution)/shard_map/ppermute | solution.py:466
  29.7 6.4 %collective-permute-start.1 = (f32[6,64,128]{2,1,0:T(8,128)S(1)}, f32[6,64,128]{2,1,0:T(8,128)S(1)}, u32[]{:S(2)}, u32[]{:S(2)}) collective-permute-start(f32[6,64,128]{2,1,0:T(8,128)S(1)} %pad_maximum_fusion.1), channel_id=1, source_target_pairs={{2,0},{4,2},{6,4},{8,6},{10,8},{12,10},{14,12},{16,14},{18,16},{20... | collective-permute-start | bytes 589832 | tf_op jit(solution)/shard_map/ppermute | solution.py:467
  36.1 0.1 pad_add_fusion.spot_ref
  36.2 0.7 %all-to-all-done = s32[128,1,640]{2,1,0:T(1,128)S(1)} async-done(((s32[128,1,640]{2,1,0:T(1,128)}), s32[128,1,640]{2,1,0:T(1,128)S(1)}, u32[]{:S(2)}, u32[]{:S(2)}) %all-to-all-start) | async-done | bytes 327712 | tf_op jit(solution)/shard_map/all_to_all | solution.py:463
  36.9 3.2 %collective-permute-done.above_ref = f32[6,64,128]{2,1,0:T(8,128)S(1)} collective-permute-done((f32[6,64,128]{2,1,0:T(8,128)S(1)}, f32[6,64,128]{2,1,0:T(8,128)S(1)}, u32[]{:S(2)}, u32[]{:S(2)}) %collective-permute-start) | collective-permute-done | bytes 196640 | tf_op jit(solution)/shard_map/ppermute | solution.py:466
  40.1 0.0 collective-permute-done.1.below_ref
  40.1 9.6 %join.1 = (f32[38,64,128]{2,1,0:T(8,128)S(1)}, f32[32,64,128]{2,1,0:T(8,128)}, f32[64,128]{1,0:T(8,128)S(1)}) custom-call(s32[3]{0:T(128)S(1)} %pad_add_fusion.spot_ref, s32[128,4]{1,0:T(8,128)S(1)} %bitcast.16, s32[640,128]{1,0:T(8,128)S(1)} %bitcast.15, f32[6,64,128]{2,1,0:T(8,128)S(1)} %collective-permute-done.above_ref, ...), custom_call_target="tpu_custom_call" | custom-call | tf_op jit(solution)/shard_map/join/pallas_call | solution.py:307
  49.8 0.0 copy-start.2
  49.8 1.0 %copy-done.2 = f32[38,64,128]{2,1,0:T(8,128)} copy-done((f32[38,64,128]{2,1,0:T(8,128)}, f32[38,64,128]{2,1,0:T(8,128)S(1)}, u32[]{:S(2)}) %copy-start.2) | copy-done | bytes 1245208
  50.8 1.1 %collective-permute-start.2 = (f32[64,128]{1,0:T(8,128)S(1)}, f32[64,128]{1,0:T(8,128)S(1)}, u32[]{:S(2)}, u32[]{:S(2)}) collective-permute-start(f32[64,128]{1,0:T(8,128)S(1)} %get-tuple-element.6), channel_id=1, source_target_pairs={{0,1},{1,0},{2,3},{3,2},{4,5},{5,4},{6,7},{7,6},{8,9},{9,8},{10,11... | collective-permute-start | bytes 98312 | tf_op jit(solution)/shard_map/ppermute | solution.py:478
  51.9 0.0 copy-done.4
  51.9 0.1 copy.12
  52.0 0.1 reshape.22
  52.0 0.1 copy.15.taps_ref
  52.2 0.6 collective-permute-done.2.side_ref
  52.7 0.0 copy-start.3
  52.7 1.3 %copy-done.3 = f32[38,64,128]{2,1,0:T(8,128)S(1)} copy-done((f32[38,64,128]{2,1,0:T(8,128)S(1)}, f32[38,64,128]{2,1,0:T(8,128)}, u32[]{:S(2)}) %copy-start.3) | copy-done | bytes 1245208
  54.0 6.4 %refine.1 = f32[32,64,128]{2,1,0:T(8,128)} custom-call(s32[3]{0:T(128)S(1)} %pad_add_fusion.spot_ref, bf16[3,64,144]{2,1,0:T(8,128)(2,1)S(1)} %copy.15.taps_ref, f32[38,64,128]{2,1,0:T(8,128)S(1)} %copy-done.3, f32[64,128]{1,0:T(8,128)S(1)} %collective-permute-done.2.side_ref), custom_call_target="tpu_custom_call" | custom-call | tf_op jit(solution)/shard_map/refine/pallas_call | solution.py:435
  (5 shorter events, 0.1 us)
Async XLA Ops:
  0.6 25.8 %copy-start.1 = (f32[32,64,128]{2,1,0:T(8,128)S(1)}, f32[32,64,128]{2,1,0:T(8,128)}, u32[]{:S(2)}) copy-start(f32[32,64,128]{2,1,0:T(8,128)} %weight_hbm.1) | copy-start | bytes 3145732
  0.6 25.8 %copy-start = (f32[32,64,128]{2,1,0:T(8,128)S(1)}, f32[32,64,128]{2,1,0:T(8,128)}, u32[]{:S(2)}) copy-start(f32[32,64,128]{2,1,0:T(8,128)} %prior_hbm.1) | copy-start | bytes 3145732
  15.6 21.3 %all-to-all-start = ((s32[128,1,640]{2,1,0:T(1,128)}), s32[128,1,640]{2,1,0:T(1,128)S(1)}, u32[]{:S(2)}, u32[]{:S(2)}) async-start(s32[128,1,640]{2,1,0:T(1,128)} %bitcast.17), calls=%async_computation | async-start | bytes 655360 | tf_op jit(solution)/shard_map/all_to_all | solution.py:463
  26.5 13.6 %collective-permute-start = (f32[6,64,128]{2,1,0:T(8,128)S(1)}, f32[6,64,128]{2,1,0:T(8,128)S(1)}, u32[]{:S(2)}, u32[]{:S(2)}) collective-permute-start(f32[6,64,128]{2,1,0:T(8,128)S(1)} %pad_maximum_fusion), channel_id=1, source_target_pairs={{0,2},{2,4},{4,6},{6,8},{8,10},{10,12},{12,14},{14,16},{16,18},{18... | collective-permute-start | bytes 589832 | tf_op jit(solution)/shard_map/ppermute | solution.py:466
  29.7 10.5 %collective-permute-start.1 = (f32[6,64,128]{2,1,0:T(8,128)S(1)}, f32[6,64,128]{2,1,0:T(8,128)S(1)}, u32[]{:S(2)}, u32[]{:S(2)}) collective-permute-start(f32[6,64,128]{2,1,0:T(8,128)S(1)} %pad_maximum_fusion.1), channel_id=1, source_target_pairs={{2,0},{4,2},{6,4},{8,6},{10,8},{12,10},{14,12},{16,14},{18,16},{20... | collective-permute-start | bytes 589832 | tf_op jit(solution)/shard_map/ppermute | solution.py:467
  40.1 11.8 %copy-start.4 = (bf16[3,64,16,3,3]{1,2,4,3,0:T(8,128)(2,1)S(1)}, bf16[3,64,16,3,3]{1,2,4,3,0:T(8,128)(2,1)}, u32[]{:S(2)}) copy-start(bf16[3,64,16,3,3]{1,2,4,3,0:T(8,128)(2,1)} %param.13) | copy-start | bytes 165892
  49.8 1.1 %copy-start.2 = (f32[38,64,128]{2,1,0:T(8,128)}, f32[38,64,128]{2,1,0:T(8,128)S(1)}, u32[]{:S(2)}) copy-start(f32[38,64,128]{2,1,0:T(8,128)S(1)} %get-tuple-element.5.joined_ref) | copy-start | bytes 3735556
  50.8 1.9 %collective-permute-start.2 = (f32[64,128]{1,0:T(8,128)S(1)}, f32[64,128]{1,0:T(8,128)S(1)}, u32[]{:S(2)}, u32[]{:S(2)}) collective-permute-start(f32[64,128]{1,0:T(8,128)S(1)} %get-tuple-element.6), channel_id=1, source_target_pairs={{0,1},{1,0},{2,3},{3,2},{4,5},{5,4},{6,7},{7,6},{8,9},{9,8},{10,11... | collective-permute-start | bytes 98312 | tf_op jit(solution)/shard_map/ppermute | solution.py:478
  52.7 1.3 %copy-start.3 = (f32[38,64,128]{2,1,0:T(8,128)S(1)}, f32[38,64,128]{2,1,0:T(8,128)}, u32[]{:S(2)}) copy-start(f32[38,64,128]{2,1,0:T(8,128)} %copy-done.2) | copy-start | bytes 3735556

commit v5 on v4

--- a/solution.py
+++ b/solution.py
@@ -11,10 +11,10 @@
 DEEP = 3
 EXT = ROWS + 2 * DEEP
 GROUP = 16
-TOGETHER = 18
-AT_ONCE = 4
+AT_ONCE = 8
 WIDTH = 5
 JOIN_VMEM = 16
+SENT = 4
 H_SCALE = 1023.0
 C_SCALE = 13000.0
 F32 = jnp.float32
@@ -216,7 +216,7 @@
 
 def join_kernel(
     spot_ref, list_ref, words_ref, above_ref, below_ref, prior_hbm, weight_hbm,
-    joined_ref, new_ref, edge_ref,
+    joined_ref, new_hbm, edge_ref,
     order_ref, height, certainty, prior_ref, total, sems,
 ):
     inner = pl.ds(DEEP, ROWS)
@@ -235,16 +235,23 @@
     certainty[entries:, :] = jnp.zeros((8, LANES), F32)
     level = lax.broadcasted_iota(I32, (BINS, LANES), 0).astype(F32) * 0.5
 
-    def pick(reader, count):
+    half = list_ref.shape[0] // 2
+    room = order_ref.shape[0] // 2
+
+    def pick(step, counts):
+        counts = list(counts)
         for slot in range(WIDTH - 1):
-            tile = list_ref[reader, slot]
-            order_ref[count] = tile * 1024 + (WIDTH * reader + slot)
-            count = count + jnp.where(tile >= 0, 1, 0)
-        return count
-
-    count = lax.fori_loop(0, list_ref.shape[0], pick, jnp.int32(0), unroll=4)
-    for i in range(AT_ONCE):
-        order_ref[count + i] = entries
+            for side in range(2):
+                reader = step + half * side
+                tile = list_ref[reader, slot]
+                order_ref[room * side + counts[side]] = tile * 1024 + (WIDTH * reader + slot)
+                counts[side] = counts[side] + jnp.where(tile >= 0, 1, 0)
+        return tuple(counts)
+
+    counts = lax.fori_loop(0, half, pick, (jnp.int32(0), jnp.int32(0)), unroll=4)
+    for side in range(2):
+        for i in range(AT_ONCE):
+            order_ref[room * side + counts[side] + i] = entries
     for copy in copies:
         copy.wait()
     for row in range(DEEP):
@@ -276,25 +283,32 @@
             joined_ref[tile] += weighted
         return carry
 
-    lax.fori_loop(0, (count + AT_ONCE - 1) // AT_ONCE, step, 0)
+    steps = [(count + AT_ONCE - 1) // AT_ONCE for count in counts]
+
+    def either(index, carry):
+        return step(jnp.where(index < steps[0], index, index - steps[0] + room // AT_ONCE), carry)
+
+    lax.fori_loop(0, steps[0] + steps[1], either, 0)
+    leaving = pltpu.make_async_copy(total.at[inner], new_hbm, sems.at[0])
+    leaving.start()
     lane = lax.broadcasted_iota(I32, (BINS, LANES), 1)
     source = jnp.where(col == 0, LANES - DEEP, 0)
     has_above = spot_ref[0] > 0
     has_below = spot_ref[0] < spot_ref[2]
     edge = jnp.zeros((BINS, LANES), F32)
     for row in range(EXT):
-        value = (0.5 * joined_ref[row]) / total[row]
+        inverse = pl.reciprocal(total[row], approx=True)
+        value = (0.5 * joined_ref[row]) * (inverse * (2.0 - total[row] * inverse))
         if row < DEEP:
             value = jnp.where(has_above, value, 0.0)
         elif row >= ROWS + DEEP:
             value = jnp.where(has_below, value, 0.0)
-        else:
-            new_ref[row - DEEP] = total[row]
         joined_ref[row] = value
         start = row * DEEP
         moved = pltpu.roll(value, (start - source + LANES) % LANES, 1)
         edge = jnp.where((lane >= start) & (lane < start + DEEP), moved, edge)
     edge_ref[...] = edge
+    leaving.wait()
 
 
 def join(spot, lists, words, above, below, prior, weight):
@@ -312,9 +326,9 @@
             jax.ShapeDtypeStruct((BINS, LANES), F32),
         ),
         in_specs=[smem, smem, vmem, vmem, vmem, anywhere, anywhere],
-        out_specs=(vmem, vmem, vmem),
+        out_specs=(vmem, anywhere, vmem),
         scratch_shapes=[
-            pltpu.SMEM(((WIDTH - 1) * lists.shape[0] + AT_ONCE,), I32),
+            pltpu.SMEM(((WIDTH - 1) * lists.shape[0] + 2 * AT_ONCE,), I32),
             column,
             column,
             pltpu.VMEM(tall, F32),
@@ -331,7 +345,7 @@
     return half + half * jnp.tanh(half)
 
 
-def weight_matrices(taps_ref, matrix):
+def weight_kernel(taps_ref, matrix):
     layers, bins, taps = taps_ref.shape
     tap = lax.broadcasted_iota(I32, (taps, 3 * BINS), 0)
     place = lax.broadcasted_iota(I32, (taps, 3 * BINS), 1)
@@ -346,14 +360,25 @@
             matrix[layer, BINS * offset : BINS * (offset + 1), :] = jnp.where(same, spread, 0.0).astype(BF16)
 
 
+def tap_matrices(taps):
+    return pl.pallas_call(
+        weight_kernel,
+        out_shape=jax.ShapeDtypeStruct((taps.shape[0], 3 * BINS, 3 * BINS), BF16),
+        in_specs=[pl.BlockSpec(memory_space=pltpu.VMEM)],
+        out_specs=pl.BlockSpec(memory_space=pltpu.VMEM),
+        compiler_params=pltpu.CompilerParams(vmem_limit_bytes=16 << 20),
+        name="tap_matrices",
+    )(taps)
+
+
 def refine_kernel(
-    spot_ref, taps_ref, joined_ref, side_ref, out_ref, matrix, current, active, side_active
+    spot_ref, matrix, joined_ref, side_ref, out_hbm, out_ref, current, active, side_active, sems
 ):
     row_index, col, last_row = spot_ref[0], spot_ref[1], spot_ref[2]
-    weight_matrices(taps_ref, matrix)
     lane = lax.broadcasted_iota(I32, (BINS, LANES), 1)
     has_above = row_index > 0
     has_below = row_index < last_row
+    leaving = []
     inside = ((lane >= DEEP * DEEP) | has_above) & ((lane < (ROWS + DEEP) * DEEP) | has_below)
     edge_lane = jnp.where(col == 0, LANES - 1, 0)
     at_edge = lane == edge_lane
@@ -366,9 +391,9 @@
         active[0, row] = silu(joined_ref[row]).astype(BF16)
         return carry
 
-    lax.fori_loop(0, EXT, fill, 0, unroll=EXT // 2)
-
-    layers = taps_ref.shape[0]
+    lax.fori_loop(0, EXT, fill, 0, unroll=EXT)
+
+    layers = matrix.shape[0]
     for layer in range(layers):
         now, later = layer % 2, (layer + 1) % 2
         taps = matrix[layer]
@@ -412,40 +437,44 @@
                     injected = jnp.where(lane == spot, thrown, injected)
             return injected
 
-        def several(step, injected):
-            for i in range(TOGETHER):
-                injected = pair(TOGETHER * step + i, injected)
-            return injected
-
-        full = pairs // TOGETHER
-        injected = lax.fori_loop(0, full, several, jnp.zeros((BINS, LANES), F32))
-        for step in range(full * TOGETHER, pairs):
+        injected = jnp.zeros((BINS, LANES), F32)
+        for step in range(pairs):
             injected = pair(step, injected)
+            if final and (step + 1) % SENT == 0:
+                rows = pl.ds(2 * (step + 1 - SENT), 2 * SENT)
+                copy = pltpu.make_async_copy(out_ref.at[rows], out_hbm.at[rows], sems.at[len(leaving)])
+                copy.start()
+                leaving.append(copy)
         if not final:
             place = lane % DEEP
             from_left = jnp.where((place == 0) & (col == 0), injected, pltpu.roll(side_left, 1, 1))
             from_right = jnp.where((place == DEEP - 1) & (col != 0), injected, pltpu.roll(side_right, LANES - 1, 1))
             side_current = side_current + (side_mid + from_left + from_right)
             side_active[...] = jnp.where(inside, silu(side_current), 0.0).astype(BF16)
-
-
-def refine(spot, taps, joined, side):
+    for copy in leaving:
+        copy.wait()
+
+
+def refine(spot, matrix, joined, side):
     vmem = pl.BlockSpec(memory_space=pltpu.VMEM)
     smem = pl.BlockSpec(memory_space=pltpu.SMEM)
+    anywhere = pl.BlockSpec(memory_space=pl.ANY)
+    flat = (ROWS,) + joined.shape[1:]
     return pl.pallas_call(
         refine_kernel,
-        out_shape=jax.ShapeDtypeStruct((ROWS,) + joined.shape[1:], F32),
-        in_specs=[smem] + [vmem] * 3,
-        out_specs=vmem,
+        out_shape=jax.ShapeDtypeStruct(flat, F32),
+        in_specs=[smem, vmem, vmem, vmem],
+        out_specs=anywhere,
         scratch_shapes=[
-            pltpu.VMEM((taps.shape[0], 3 * BINS, 3 * BINS), BF16),
-            pltpu.VMEM((EXT, BINS, LANES), F32),
-            pltpu.VMEM((2, EXT, BINS, LANES), BF16),
+            pltpu.VMEM(flat, F32),
+            pltpu.VMEM(joined.shape, F32),
+            pltpu.VMEM((2,) + joined.shape, BF16),
             pltpu.VMEM((BINS, LANES), BF16),
+            pltpu.SemaphoreType.DMA((ROWS // (2 * SENT),)),
         ],
         compiler_params=pltpu.CompilerParams(vmem_limit_bytes=16 << 20),
         name="refine",
-    )(spot, taps, joined, side)
+    )(spot, matrix, joined, side)
 
 
 def on_device(tsdf_prior, prior_weight, depth_maps, confidence, frustum_tiles, pixel_index, conv_weights):
@@ -465,6 +494,9 @@
     down = [(j, i) for i, j in up]
     above = lax.ppermute(jnp.concatenate([tsdf_prior[ROWS - DEEP :], prior_weight[ROWS - DEEP :]], axis=0), "row", up)
     below = lax.ppermute(jnp.concatenate([tsdf_prior[:DEEP], prior_weight[:DEEP]], axis=0), "row", down)
+    layers = conv_weights.shape[0]
+    matrix = tap_matrices(conv_weights.reshape(layers, BINS, GROUP * 9))
+    above, matrix = lax.optimization_barrier((above, matrix))
     start = (WIDTH - 1) * LANES
     joined, new_weight, edge = join(
         spot,
@@ -476,8 +508,7 @@
         prior_weight,
     )
     side = lax.ppermute(edge, "col", [(0, 1), (1, 0)])
-    layers = conv_weights.shape[0]
-    refined = refine(spot, conv_weights.reshape(layers, BINS, GROUP * 9), joined, side)
+    refined = refine(spot, matrix, joined, side)
     return refined, new_weight
 
 

time: 61 us -> 59 us (0.967)
  local copies, waits for them, and re-layouts: 2.7 us -> 0.36 us
  starting transfers between devices: 21.4 us -> 22.3 us
  waiting for transfers between devices: 4.48 us -> 3.75 us
  other arithmetic: 0.11 us -> 0.79 us
    unnamed x11 -> x7, local copies, waits for them, and re-layouts: 2.41 us -> 0.07 us
    ppermute x1, starting transfers between devices: 1.06 us -> 1.98 us  [on_device(): side = lax.ppermute(edge, 'col', [(0, 1), (1, 0)])]
    all_to_all x1, waiting for transfers between devices: 0.72 us -> 0.01 us  [on_device(): lax.all_to_all(words.reshape(readers, 1, width), both, split_axis=0, conc...]
    concatenate x1, other arithmetic: 0.02 us -> 0.69 us  [on_device(): jnp.concatenate([tsdf_prior[ROWS - DEEP:], prior_weight[ROWS - DEEP:]], a...]
    ppermute x1, waiting for transfers between devices: 3.18 us -> 2.52 us  [on_device(): lax.ppermute(jnp.concatenate([tsdf_prior[ROWS - DEEP:], prior_weight[ROWS...]
    pallas_call x1 -> x2, Pallas kernels: 6.36 us -> 5.97 us  [the longest x1 5.72 us: refine(): pl.pallas_call(refine_kernel, out_shape=jax.ShapeDtypeStruct(flat, F32),...]
  transfers between devices with their start and end apart: 4 -> 4, of which waited for: 3 -> 3; matrix products, arithmetic and copies ran while one was open for 1% -> 2% of each run, Pallas kernels for 0% -> 0%
where the time goes in v5:
time: 59 us; the launch traced here: 58.5 us
  Pallas kernels  30.4 us (52%)
  starting transfers between devices  22.3 us (38%)
  waiting for transfers between devices  3.75 us (6%)
  between operations  0.93 us (2%)
  other arithmetic  0.79 us (1%)
    pallas_call x1, Pallas kernels, sample(): pl.pallas_call(sample_kernel, out_shape=jax.ShapeDtypeStruct((WIDTH * wan...  15 us
    all_to_all x1, starting transfers between devices, on_device(): lax.all_to_all(words.reshape(readers, 1, width), both, split_axis=0, conc...  10.8 us
    pallas_call x1, Pallas kernels, join(): pl.pallas_call(join_kernel, out_shape=(jax.ShapeDtypeStruct(tall, F32), j...  9.46 us
    ppermute x1, starting transfers between devices, on_device(): lax.ppermute(jnp.concatenate([tsdf_prior[:DEEP], prior_weight[:DEEP]], ax...  6.41 us
    pallas_call x1, Pallas kernels, refine(): pl.pallas_call(refine_kernel, out_shape=jax.ShapeDtypeStruct(flat, F32),...  5.72 us
    ppermute x1, starting transfers between devices, on_device(): lax.ppermute(jnp.concatenate([tsdf_prior[ROWS - DEEP:], prior_weight[ROWS...  3.08 us
    ppermute x1, waiting for transfers between devices, on_device(): lax.ppermute(jnp.concatenate([tsdf_prior[ROWS - DEEP:], prior_weight[ROWS...  2.52 us
    ppermute x1, starting transfers between devices, on_device(): side = lax.ppermute(edge, 'col', [(0, 1), (1, 0)])  1.98 us
  transfers between devices with their start and end apart: 4, of which 3 were waited for; matrix products, arithmetic and copies ran while one was open for 2% of the time, Pallas kernels for 0%

profile of v5, /device:TPU:3, one launch (start us, length us, event | category | flops | bytes accessed | tf_op | source)
XLA Modules:
  0.0 58.5 jit_solution(6148081221144565626)
XLA Ops:
  0.6 0.0 copy-start.1
  0.6 0.0 copy-start
  0.7 15.0 %sample.1 = s32[640,128]{1,0:T(8,128)} custom-call(s32[256,128]{1,0:T(8,128)} %bitcast.20, s32[2,128]{1,0:T(2,128)} %bitcast.21, f32[1024,128]{1,0:T(8,128)} %bitcast.18, f32[1024,128]{1,0:T(8,128)} %bitcast.19), custom_call_target="tpu_custom_call" | custom-call | tf_op jit(solution)/shard_map/sample/pallas_call | solution.py:193
  15.6 0.0 copy-start.2
  15.6 10.8 %all-to-all-start = ((s32[128,1,640]{2,1,0:T(1,128)}), s32[128,1,640]{2,1,0:T(1,128)S(1)}, u32[]{:S(2)}, u32[]{:S(2)}) async-start(s32[128,1,640]{2,1,0:T(1,128)} %bitcast.17), calls=%async_computation | async-start | bytes 655360 | tf_op jit(solution)/shard_map/all_to_all | solution.py:492
  26.5 0.0 copy-done.1
  26.5 0.0 copy-done
  26.5 0.7 %pad_maximum_fusion = f32[6,64,128]{2,1,0:T(8,128)} fusion(f32[3,64,128]{2,1,0:T(8,128)S(1)} %get-tuple-element.16, f32[3,64,128]{2,1,0:T(8,128)S(1)} %get-tuple-element.13), kind=kLoop, calls=%fused_computation | loop fusion | flops 49152 | bytes 393216 | tf_op jit(solution)/shard_map/concatenate | solution.py:495
  27.2 3.1 %collective-permute-start = (f32[6,64,128]{2,1,0:T(8,128)}, f32[6,64,128]{2,1,0:T(8,128)S(1)}, u32[]{:S(2)}, u32[]{:S(2)}) collective-permute-start(f32[6,64,128]{2,1,0:T(8,128)} %pad_maximum_fusion), channel_id=1, source_target_pairs={{0,2},{2,4},{4,6},{6,8},{8,10},{10,12},{12,14},{14,16},{16,18},{18... | collective-permute-start | bytes 589832 | tf_op jit(solution)/shard_map/ppermute | solution.py:495
  30.3 6.4 %collective-permute-start.1 = (f32[6,64,128]{2,1,0:T(8,128)S(1)}, f32[6,64,128]{2,1,0:T(8,128)S(1)}, u32[]{:S(2)}, u32[]{:S(2)}) collective-permute-start(f32[6,64,128]{2,1,0:T(8,128)S(1)} %pad_maximum_fusion.1), channel_id=1, source_target_pairs={{2,0},{4,2},{6,4},{8,6},{10,8},{12,10},{14,12},{16,14},{18,16},{20... | collective-permute-start | bytes 589832 | tf_op jit(solution)/shard_map/ppermute | solution.py:496
  36.8 0.0 copy-done.2
  36.8 0.1 copy.12
  36.8 0.1 reshape.22
  36.9 0.1 copy.13.taps_ref
  37.1 0.2 tap_matrices.1.matrix
  37.3 0.1 pad_add_fusion.spot_ref
  37.4 2.5 %collective-permute-done.above_ref = f32[6,64,128]{2,1,0:T(8,128)S(1)} collective-permute-done((f32[6,64,128]{2,1,0:T(8,128)}, f32[6,64,128]{2,1,0:T(8,128)S(1)}, u32[]{:S(2)}, u32[]{:S(2)}) %collective-permute-start) | collective-permute-done | bytes 196640 | tf_op jit(solution)/shard_map/ppermute | solution.py:495
  39.9 0.0 all-to-all-done
  40.0 0.4 collective-permute-done.1.below_ref
  40.3 9.5 %join.1 = (f32[38,64,128]{2,1,0:T(8,128)S(1)}, f32[32,64,128]{2,1,0:T(8,128)}, f32[64,128]{1,0:T(8,128)S(1)}) custom-call(s32[3]{0:T(128)S(1)} %pad_add_fusion.spot_ref, s32[128,4]{1,0:T(8,128)S(1)} %bitcast.16, s32[640,128]{1,0:T(8,128)S(1)} %bitcast.15, f32[6,64,128]{2,1,0:T(8,128)S(1)} %collective-permute-done.above_ref, ...), custom_call_target="tpu_custom_call" | custom-call | tf_op jit(solution)/shard_map/join/pallas_call | solution.py:321
  49.8 2.0 %collective-permute-start.2 = (f32[64,128]{1,0:T(8,128)S(1)}, f32[64,128]{1,0:T(8,128)S(1)}, u32[]{:S(2)}, u32[]{:S(2)}) collective-permute-start(f32[64,128]{1,0:T(8,128)S(1)} %get-tuple-element.10), channel_id=1, source_target_pairs={{0,1},{1,0},{2,3},{3,2},{4,5},{5,4},{6,7},{7,6},{8,9},{9,8},{10,11... | collective-permute-start | bytes 98312 | tf_op jit(solution)/shard_map/ppermute | solution.py:510
  51.8 0.9 %collective-permute-done.2.side_ref = f32[64,128]{1,0:T(8,128)S(1)} collective-permute-done((f32[64,128]{1,0:T(8,128)S(1)}, f32[64,128]{1,0:T(8,128)S(1)}, u32[]{:S(2)}, u32[]{:S(2)}) %collective-permute-start.2) | collective-permute-done | bytes 32800 | tf_op jit(solution)/shard_map/ppermute | solution.py:510
  52.6 5.7 %refine.1 = f32[32,64,128]{2,1,0:T(8,128)} custom-call(s32[3]{0:T(128)S(1)} %pad_add_fusion.spot_ref, bf16[3,192,192]{2,1,0:T(8,128)(2,1)S(1)} %tap_matrices.1.matrix, f32[38,64,128]{2,1,0:T(8,128)S(1)} %get-tuple-element.9.joined_ref, f32[64,128]{1,0:T(8,128)S(1)} %collective-permute-done.2.side_ref), custom_call_target="tpu_custom_call" | custom-call | tf_op jit(solution)/shard_map/refine/pallas_call | solution.py:463
  (3 shorter events, 0.1 us)
Async XLA Ops:
  0.6 25.9 %copy-start.1 = (f32[32,64,128]{2,1,0:T(8,128)S(1)}, f32[32,64,128]{2,1,0:T(8,128)}, u32[]{:S(2)}) copy-start(f32[32,64,128]{2,1,0:T(8,128)} %weight_hbm.1) | copy-start | bytes 3145732
  0.6 25.9 %copy-start = (f32[32,64,128]{2,1,0:T(8,128)S(1)}, f32[32,64,128]{2,1,0:T(8,128)}, u32[]{:S(2)}) copy-start(f32[32,64,128]{2,1,0:T(8,128)} %prior_hbm.1) | copy-start | bytes 3145732
  15.6 21.1 %copy-start.2 = (bf16[3,64,16,3,3]{1,2,4,3,0:T(8,128)(2,1)S(1)}, bf16[3,64,16,3,3]{1,2,4,3,0:T(8,128)(2,1)}, u32[]{:S(2)}) copy-start(bf16[3,64,16,3,3]{1,2,4,3,0:T(8,128)(2,1)} %param.13) | copy-start | bytes 165892
  15.6 24.3 %all-to-all-start = ((s32[128,1,640]{2,1,0:T(1,128)}), s32[128,1,640]{2,1,0:T(1,128)S(1)}, u32[]{:S(2)}, u32[]{:S(2)}) async-start(s32[128,1,640]{2,1,0:T(1,128)} %bitcast.17), calls=%async_computation | async-start | bytes 655360 | tf_op jit(solution)/shard_map/all_to_all | solution.py:492
  27.2 12.7 %collective-permute-start = (f32[6,64,128]{2,1,0:T(8,128)}, f32[6,64,128]{2,1,0:T(8,128)S(1)}, u32[]{:S(2)}, u32[]{:S(2)}) collective-permute-start(f32[6,64,128]{2,1,0:T(8,128)} %pad_maximum_fusion), channel_id=1, source_target_pairs={{0,2},{2,4},{4,6},{6,8},{8,10},{10,12},{12,14},{14,16},{16,18},{18... | collective-permute-start | bytes 589832 | tf_op jit(solution)/shard_map/ppermute | solution.py:495
  30.3 10.0 %collective-permute-start.1 = (f32[6,64,128]{2,1,0:T(8,128)S(1)}, f32[6,64,128]{2,1,0:T(8,128)S(1)}, u32[]{:S(2)}, u32[]{:S(2)}) collective-permute-start(f32[6,64,128]{2,1,0:T(8,128)S(1)} %pad_maximum_fusion.1), channel_id=1, source_target_pairs={{2,0},{4,2},{6,4},{8,6},{10,8},{12,10},{14,12},{16,14},{18,16},{20... | collective-permute-start | bytes 589832 | tf_op jit(solution)/shard_map/ppermute | solution.py:496
  49.8 2.8 %collective-permute-start.2 = (f32[64,128]{1,0:T(8,128)S(1)}, f32[64,128]{1,0:T(8,128)S(1)}, u32[]{:S(2)}, u32[]{:S(2)}) collective-permute-start(f32[64,128]{1,0:T(8,128)S(1)} %get-tuple-element.10), channel_id=1, source_target_pairs={{0,1},{1,0},{2,3},{3,2},{4,5},{5,4},{6,7},{7,6},{8,9},{9,8},{10,11... | collective-permute-start | bytes 98312 | tf_op jit(solution)/shard_map/ppermute | solution.py:510

commit v6 on v5

--- a/solution.py
+++ b/solution.py
@@ -11,7 +11,7 @@
 DEEP = 3
 EXT = ROWS + 2 * DEEP
 GROUP = 16
-AT_ONCE = 8
+AT_ONCE = 4
 WIDTH = 5
 JOIN_VMEM = 16
 SENT = 4
@@ -111,7 +111,7 @@
     table[...] = (high << 16) | low
     to_scalar.wait()
     chunks = table.shape[0] // 8
-    together = 8
+    together = 16
 
     def first_chunk(block):
         return (bounds[8 * (block & 1), 8 * (block >> 1)] >> 25) + 64
@@ -240,39 +240,40 @@
 
     def pick(step, counts):
         counts = list(counts)
-        for slot in range(WIDTH - 1):
+        codes = [[list_ref[2 * step + i + half * side, slot] for i in range(2) for slot in range(WIDTH - 1)] for side in range(2)]
+        for pair in zip(*codes):
             for side in range(2):
-                reader = step + half * side
-                tile = list_ref[reader, slot]
-                order_ref[room * side + counts[side]] = tile * 1024 + (WIDTH * reader + slot)
-                counts[side] = counts[side] + jnp.where(tile >= 0, 1, 0)
+                order_ref[room * side + counts[side]] = pair[side]
+                counts[side] = counts[side] + (1 + (pair[side] >> 31))
         return tuple(counts)
 
-    counts = lax.fori_loop(0, half, pick, (jnp.int32(0), jnp.int32(0)), unroll=4)
+    counts = lax.fori_loop(0, half // 2, pick, (jnp.int32(0), jnp.int32(0)), unroll=2)
     for side in range(2):
         for i in range(AT_ONCE):
             order_ref[room * side + counts[side] + i] = entries
     for copy in copies:
         copy.wait()
     for row in range(DEEP):
-        prior_ref[row] = above_ref[row]
-        prior_ref[ROWS + DEEP + row] = below_ref[row]
-        total[row] = above_ref[DEEP + row]
-        total[ROWS + DEEP + row] = below_ref[DEEP + row]
-    joined_ref[...] = (2.0 * total[...]) * prior_ref[...]
+        prior_ref[row] = above_ref[row].astype(F32)
+        prior_ref[ROWS + DEEP + row] = below_ref[row].astype(F32)
+        total[row] = above_ref[DEEP + row].astype(F32)
+        total[ROWS + DEEP + row] = below_ref[DEEP + row].astype(F32)
+    for row in range(EXT):
+        twice = 2.0 * prior_ref[row]
+        prior_ref[row] = twice
+        joined_ref[row] = total[row] * twice
 
     def term(place):
         code = order_ref[place]
         tile = code >> 10
         entry = code & 1023
-        prior = prior_ref[tile]
+        twice = prior_ref[tile]
         scaled = height[pl.ds(entry, 1), :] - level
         signed = jnp.clip(scaled, -2.0, 2.0)
         visible = jnp.clip(scaled + 4.0, 0.0, 2.0)
-        mismatch = signed - (prior + prior)
+        mismatch = signed - twice
         spread = 1.0 + mismatch * mismatch
         inverse = pl.reciprocal(spread, approx=True)
-        inverse = inverse * (2.0 - spread * inverse)
         observed = (certainty[pl.ds(entry, 1), :] * visible) * inverse
         return tile, observed, observed * signed
 
@@ -298,7 +299,7 @@
     edge = jnp.zeros((BINS, LANES), F32)
     for row in range(EXT):
         inverse = pl.reciprocal(total[row], approx=True)
-        value = (0.5 * joined_ref[row]) * (inverse * (2.0 - total[row] * inverse))
+        value = (0.5 * joined_ref[row]) * inverse
         if row < DEEP:
             value = jnp.where(has_above, value, 0.0)
         elif row >= ROWS + DEEP:
@@ -490,17 +491,24 @@
     )
     width = WIDTH * LANES
     got = lax.all_to_all(words.reshape(readers, 1, width), both, split_axis=0, concat_axis=0, tiled=True)
+    def halo(first):
+        rows = slice(first, first + DEEP)
+        return jnp.concatenate([tsdf_prior[rows], prior_weight[rows]], axis=0).astype(BF16)
+
     up = [(i, i + 1) for i in range(row_count - 1)]
     down = [(j, i) for i, j in up]
-    above = lax.ppermute(jnp.concatenate([tsdf_prior[ROWS - DEEP :], prior_weight[ROWS - DEEP :]], axis=0), "row", up)
-    below = lax.ppermute(jnp.concatenate([tsdf_prior[:DEEP], prior_weight[:DEEP]], axis=0), "row", down)
+    above = lax.ppermute(halo(ROWS - DEEP), "row", up)
+    below = lax.ppermute(halo(0), "row", down)
     layers = conv_weights.shape[0]
     matrix = tap_matrices(conv_weights.reshape(layers, BINS, GROUP * 9))
     above, matrix = lax.optimization_barrier((above, matrix))
     start = (WIDTH - 1) * LANES
+    tiles = got[:, 0, start : start + WIDTH - 1]
+    places = lax.broadcasted_iota(I32, tiles.shape, 0) * WIDTH + lax.broadcasted_iota(I32, tiles.shape, 1)
+    codes = jnp.where(tiles >= 0, tiles * 1024 + places, -1)
     joined, new_weight, edge = join(
         spot,
-        got[:, 0, start : start + WIDTH - 1],
+        codes,
         got.reshape(WIDTH * readers, LANES),
         above,
         below,

time: 59 us -> 54.6 us (0.925)
  waiting for transfers between devices: 3.75 us -> 1.84 us
  Pallas kernels: 30.4 us -> 28.5 us
    ppermute x2, waiting for transfers between devices: 2.89 us -> 0.98 us  [the longest x1 0.97 us: on_device(): above = lax.ppermute(halo(ROWS - DEEP), 'row', up)]
    pallas_call x1, Pallas kernels: 9.46 us -> 8.29 us  [join(): pl.pallas_call(join_kernel, out_shape=(jax.ShapeDtypeStruct(tall, F32), j...]
    concatenate x2, other arithmetic: 0.71 us -> 0.02 us  [halo(): jnp.concatenate([tsdf_prior[rows], prior_weight[rows]], axis=0).astype(BF16)]
    pallas_call x1, Pallas kernels: 15 us -> 14.3 us  [sample(): pl.pallas_call(sample_kernel, out_shape=jax.ShapeDtypeStruct((WIDTH * wan...]
  transfers between devices with their start and end apart: 4 -> 4, of which waited for: 3 -> 2; matrix products, arithmetic and copies ran while one was open for 2% -> 1% of each run, Pallas kernels for 0% -> 0%
where the time goes in v6:
time: 54.6 us; the launch traced here: 54 us
  Pallas kernels  28.5 us (52%)
  starting transfers between devices  21.9 us (40%)
  waiting for transfers between devices  1.84 us (3%)
  between operations  0.98 us (2%)
    pallas_call x1, Pallas kernels, sample(): pl.pallas_call(sample_kernel, out_shape=jax.ShapeDtypeStruct((WIDTH * wan...  14.3 us
    all_to_all x1, starting transfers between devices, on_device(): lax.all_to_all(words.reshape(readers, 1, width), both, split_axis=0, conc...  10.8 us
    pallas_call x1, Pallas kernels, join(): pl.pallas_call(join_kernel, out_shape=(jax.ShapeDtypeStruct(tall, F32), j...  8.29 us
    ppermute x1, starting transfers between devices, on_device(): below = lax.ppermute(halo(0), 'row', down)  6.41 us
    pallas_call x1, Pallas kernels, refine(): pl.pallas_call(refine_kernel, out_shape=jax.ShapeDtypeStruct(flat, F32),...  5.72 us
    ppermute x1, starting transfers between devices, on_device(): above = lax.ppermute(halo(ROWS - DEEP), 'row', up)  3.1 us
    ppermute x1, starting transfers between devices, on_device(): side = lax.ppermute(edge, 'col', [(0, 1), (1, 0)])  1.58 us
  transfers between devices with their start and end apart: 4, of which 2 were waited for; matrix products, arithmetic and copies ran while one was open for 1% of the time, Pallas kernels for 0%

profile of v6, /device:TPU:3, one launch (start us, length us, event | category | flops | bytes accessed | tf_op | source)
XLA Modules:
  0.0 54.0 jit_solution(16672770725268906897)
XLA Ops:
  0.6 0.0 copy-start
  0.6 14.3 %sample.1 = s32[640,128]{1,0:T(8,128)} custom-call(s32[256,128]{1,0:T(8,128)} %bitcast.24, s32[2,128]{1,0:T(2,128)} %bitcast.25, f32[1024,128]{1,0:T(8,128)} %bitcast.21, f32[1024,128]{1,0:T(8,128)} %bitcast.22), custom_call_target="tpu_custom_call" | custom-call | tf_op jit(solution)/shard_map/sample/pallas_call | solution.py:193
  14.9 0.0 copy-start.1
  14.9 10.8 %all-to-all-start = ((s32[128,1,640]{2,1,0:T(1,128)}), s32[128,1,640]{2,1,0:T(1,128)S(1)}, u32[]{:S(2)}, u32[]{:S(2)}) async-start(s32[128,1,640]{2,1,0:T(1,128)} %bitcast.20), calls=%async_computation | async-start | bytes 655360 | tf_op jit(solution)/shard_map/all_to_all | solution.py:493
  25.8 0.0 copy-done
  25.8 0.1 convert.12
  25.9 0.0 copy-done.1
  25.9 0.0 copy-start.2
  25.9 0.1 convert.13
  26.0 3.1 %collective-permute-start = (bf16[6,64,128]{2,1,0:T(8,128)(2,1)S(1)}, bf16[6,64,128]{2,1,0:T(8,128)(2,1)S(1)}, u32[]{:S(2)}, u32[]{:S(2)}) collective-permute-start(bf16[6,64,128]{2,1,0:T(8,128)(2,1)S(1)} %pad_maximum_fusion), channel_id=1, source_target_pairs={{0,2},{2,4},{4,6},{6,8},{8,10},{10,12},{12,14},{14,16},{16,18},{18... | collective-permute-start | bytes 294920 | tf_op jit(solution)/shard_map/ppermute | solution.py:500
  29.2 6.4 %collective-permute-start.1 = (bf16[6,64,128]{2,1,0:T(8,128)(2,1)S(1)}, bf16[6,64,128]{2,1,0:T(8,128)(2,1)S(1)}, u32[]{:S(2)}, u32[]{:S(2)}) collective-permute-start(bf16[6,64,128]{2,1,0:T(8,128)(2,1)S(1)} %pad_maximum_fusion.1), channel_id=1, source_target_pairs={{2,0},{4,2},{6,4},{8,6},{10,8},{12,10},{14,12},{16,14},{18,16},{20... | collective-permute-start | bytes 294920 | tf_op jit(solution)/shard_map/ppermute | solution.py:501
  35.6 0.1 copy.12
  35.7 0.1 reshape.26
  35.8 0.1 copy.13.taps_ref
  35.9 0.2 tap_matrices.1.matrix
  36.2 0.1 pad_add_fusion.spot_ref
  36.2 1.0 %collective-permute-done.above_ref = bf16[6,64,128]{2,1,0:T(8,128)(2,1)S(1)} collective-permute-done((bf16[6,64,128]{2,1,0:T(8,128)(2,1)S(1)}, bf16[6,64,128]{2,1,0:T(8,128)(2,1)S(1)}, u32[]{:S(2)}, u32[]{:S(2)}) %collective-permute-start) | collective-permute-done | bytes 98336 | tf_op jit(solution)/shard_map/ppermute | solution.py:500
  37.2 0.0 all-to-all-done
  37.3 0.1 fusion.list_ref
  37.4 0.0 collective-permute-done.1.below_ref
  37.4 8.3 %join.1 = (f32[38,64,128]{2,1,0:T(8,128)S(1)}, f32[32,64,128]{2,1,0:T(8,128)}, f32[64,128]{1,0:T(8,128)S(1)}) custom-call(s32[3]{0:T(128)S(1)} %pad_add_fusion.spot_ref, s32[128,4]{1,0:T(8,128)S(1)} %fusion.list_ref, s32[640,128]{1,0:T(8,128)S(1)} %bitcast.19, bf16[6,64,128]{2,1,0:T(8,128)(2,1)S(1)} %collective-permute-done.above_ref, ...), custom_call_target="tpu_custom_call" | custom-call | tf_op jit(solution)/shard_map/join/pallas_call | solution.py:322
  45.7 1.6 %collective-permute-start.2 = (f32[64,128]{1,0:T(8,128)S(1)}, f32[64,128]{1,0:T(8,128)S(1)}, u32[]{:S(2)}, u32[]{:S(2)}) collective-permute-start(f32[64,128]{1,0:T(8,128)S(1)} %get-tuple-element.10), channel_id=1, source_target_pairs={{0,1},{1,0},{2,3},{3,2},{4,5},{5,4},{6,7},{7,6},{8,9},{9,8},{10,11... | collective-permute-start | bytes 98312 | tf_op jit(solution)/shard_map/ppermute | solution.py:518
  47.2 0.9 %collective-permute-done.2.side_ref = f32[64,128]{1,0:T(8,128)S(1)} collective-permute-done((f32[64,128]{1,0:T(8,128)S(1)}, f32[64,128]{1,0:T(8,128)S(1)}, u32[]{:S(2)}, u32[]{:S(2)}) %collective-permute-start.2) | collective-permute-done | bytes 32800 | tf_op jit(solution)/shard_map/ppermute | solution.py:518
  48.1 5.7 %refine.1 = f32[32,64,128]{2,1,0:T(8,128)} custom-call(s32[3]{0:T(128)S(1)} %pad_add_fusion.spot_ref, bf16[3,192,192]{2,1,0:T(8,128)(2,1)S(1)} %tap_matrices.1.matrix, f32[38,64,128]{2,1,0:T(8,128)S(1)} %get-tuple-element.9.joined_ref, f32[64,128]{1,0:T(8,128)S(1)} %collective-permute-done.2.side_ref), custom_call_target="tpu_custom_call" | custom-call | tf_op jit(solution)/shard_map/refine/pallas_call | solution.py:464
  (6 shorter events, 0.1 us)
Async XLA Ops:
  0.6 25.2 %copy-start = (f32[32,64,128]{2,1,0:T(8,128)S(1)}, f32[32,64,128]{2,1,0:T(8,128)}, u32[]{:S(2)}) copy-start(f32[32,64,128]{2,1,0:T(8,128)} %prior_hbm.1) | copy-start | bytes 3145732
  14.9 11.0 %copy-start.1 = (f32[32,64,128]{2,1,0:T(8,128)S(1)}, f32[32,64,128]{2,1,0:T(8,128)}, u32[]{:S(2)}) copy-start(f32[32,64,128]{2,1,0:T(8,128)} %weight_hbm.1) | copy-start | bytes 3145732
  14.9 22.3 %all-to-all-start = ((s32[128,1,640]{2,1,0:T(1,128)}), s32[128,1,640]{2,1,0:T(1,128)S(1)}, u32[]{:S(2)}, u32[]{:S(2)}) async-start(s32[128,1,640]{2,1,0:T(1,128)} %bitcast.20), calls=%async_computation | async-start | bytes 655360 | tf_op jit(solution)/shard_map/all_to_all | solution.py:493
  25.9 9.7 %copy-start.2 = (bf16[3,64,16,3,3]{1,2,4,3,0:T(8,128)(2,1)S(1)}, bf16[3,64,16,3,3]{1,2,4,3,0:T(8,128)(2,1)}, u32[]{:S(2)}) copy-start(bf16[3,64,16,3,3]{1,2,4,3,0:T(8,128)(2,1)} %param.13) | copy-start | bytes 165892
  26.0 11.2 %collective-permute-start = (bf16[6,64,128]{2,1,0:T(8,128)(2,1)S(1)}, bf16[6,64,128]{2,1,0:T(8,128)(2,1)S(1)}, u32[]{:S(2)}, u32[]{:S(2)}) collective-permute-start(bf16[6,64,128]{2,1,0:T(8,128)(2,1)S(1)} %pad_maximum_fusion), channel_id=1, source_target_pairs={{0,2},{2,4},{4,6},{6,8},{8,10},{10,12},{12,14},{14,16},{16,18},{18... | collective-permute-start | bytes 294920 | tf_op jit(solution)/shard_map/ppermute | solution.py:500
  29.2 8.2 %collective-permute-start.1 = (bf16[6,64,128]{2,1,0:T(8,128)(2,1)S(1)}, bf16[6,64,128]{2,1,0:T(8,128)(2,1)S(1)}, u32[]{:S(2)}, u32[]{:S(2)}) collective-permute-start(bf16[6,64,128]{2,1,0:T(8,128)(2,1)S(1)} %pad_maximum_fusion.1), channel_id=1, source_target_pairs={{2,0},{4,2},{6,4},{8,6},{10,8},{12,10},{14,12},{16,14},{18,16},{20... | collective-permute-start | bytes 294920 | tf_op jit(solution)/shard_map/ppermute | solution.py:501
  45.7 2.4 %collective-permute-start.2 = (f32[64,128]{1,0:T(8,128)S(1)}, f32[64,128]{1,0:T(8,128)S(1)}, u32[]{:S(2)}, u32[]{:S(2)}) collective-permute-start(f32[64,128]{1,0:T(8,128)S(1)} %get-tuple-element.10), channel_id=1, source_target_pairs={{0,1},{1,0},{2,3},{3,2},{4,5},{5,4},{6,7},{7,6},{8,9},{9,8},{10,11... | collective-permute-start | bytes 98312 | tf_op jit(solution)/shard_map/ppermute | solution.py:518

commit v7 on v6

--- a/solution.py
+++ b/solution.py
@@ -372,27 +372,79 @@
     )(taps)
 
 
+def convolve_pair(taps, planes):
+    stack = jnp.concatenate([jnp.concatenate(planes[0:3], axis=0), jnp.concatenate(planes[1:4], axis=0)], axis=1)
+    part = jnp.dot(taps, stack, preferred_element_type=F32)
+    return [
+        [part[BINS * k : BINS * (k + 1), LANES * i : LANES * (i + 1)] for k in range(3)] for i in range(2)
+    ]
+
+
+def within(lane, left, mid, right):
+    response = mid + jnp.where(lane == 0, 0.0, pltpu.roll(left, 1, 1))
+    return response + jnp.where(lane == LANES - 1, 0.0, pltpu.roll(right, LANES - 1, 1))
+
+
+def geometry(spot_ref):
+    col = spot_ref[1]
+    lane = lax.broadcasted_iota(I32, (BINS, LANES), 1)
+    edge_lane = jnp.where(col == 0, LANES - 1, 0)
+    near = jnp.where(col == 0, 0, DEEP - 1)
+    return col, lane, edge_lane, near
+
+
+def outward_edge(col, lane, edge_lane, spot, left, right, injected):
+    outward = jnp.where(col == 0, left, right)
+    thrown = pltpu.roll(outward, (spot - edge_lane + LANES) % LANES, 1)
+    return jnp.where(lane == spot, thrown, injected)
+
+
+def open_kernel(spot_ref, matrix, joined_ref, partial_ref, injected_ref, active):
+    col, lane, edge_lane, near = geometry(spot_ref)
+    for row in range(EXT):
+        active[row] = silu(joined_ref[row]).astype(BF16)
+    partial_ref[0] = joined_ref[0]
+    partial_ref[EXT - 1] = joined_ref[EXT - 1]
+    injected = jnp.zeros((BINS, LANES), F32)
+    for row in range(1, EXT - 1, 2):
+        parts = convolve_pair(matrix[0], [active[row - 1 + i] for i in range(4)])
+        for i, (left, mid, right) in enumerate(parts):
+            partial_ref[row + i] = joined_ref[row + i] + within(lane, left, mid, right)
+            injected = outward_edge(col, lane, edge_lane, (row + i) * DEEP + near, left, right, injected)
+    injected_ref[...] = injected
+
+
+def open_layer(spot, matrix, joined):
+    vmem = pl.BlockSpec(memory_space=pltpu.VMEM)
+    return pl.pallas_call(
+        open_kernel,
+        out_shape=(
+            jax.ShapeDtypeStruct(joined.shape, F32),
+            jax.ShapeDtypeStruct((BINS, LANES), F32),
+        ),
+        in_specs=[pl.BlockSpec(memory_space=pltpu.SMEM), vmem, vmem],
+        out_specs=(vmem, vmem),
+        scratch_shapes=[pltpu.VMEM(joined.shape, BF16)],
+        compiler_params=pltpu.CompilerParams(vmem_limit_bytes=16 << 20),
+        cost_estimate=pl.CostEstimate(flops=400_000_000, bytes_accessed=3_000_000, transcendentals=311_296),
+        name="open_layer",
+    )(spot, matrix, joined)
+
+
 def refine_kernel(
-    spot_ref, matrix, joined_ref, side_ref, out_hbm, out_ref, current, active, side_active, sems
+    spot_ref, matrix, partial_ref, injected_ref, side_ref, out_hbm, out_ref, current, active, side_active, sems
 ):
-    row_index, col, last_row = spot_ref[0], spot_ref[1], spot_ref[2]
-    lane = lax.broadcasted_iota(I32, (BINS, LANES), 1)
+    row_index, last_row = spot_ref[0], spot_ref[2]
+    col, lane, edge_lane, near = geometry(spot_ref)
     has_above = row_index > 0
     has_below = row_index < last_row
     leaving = []
     inside = ((lane >= DEEP * DEEP) | has_above) & ((lane < (ROWS + DEEP) * DEEP) | has_below)
-    edge_lane = jnp.where(col == 0, LANES - 1, 0)
     at_edge = lane == edge_lane
-    near = jnp.where(col == 0, 0, DEEP - 1)
+    place = lane % DEEP
 
     side_current = side_ref[...]
     side_active[...] = silu(side_current).astype(BF16)
-
-    def fill(row, carry):
-        active[0, row] = silu(joined_ref[row]).astype(BF16)
-        return carry
-
-    lax.fori_loop(0, EXT, fill, 0, unroll=EXT)
 
     layers = matrix.shape[0]
     for layer in range(layers):
@@ -406,48 +458,46 @@
         side_left, side_mid, side_right = (side_part[BINS * i : BINS * (i + 1)] for i in range(3))
         side_edge = jnp.where(col == 0, side_right, side_left)
         first = 1 + layer
-        pairs = (EXT - 2 - 2 * layer) // 2
         final = layer == layers - 1
 
-        def pair(step, injected):
-            row = first + 2 * step
-            planes = [active[now, row - 1 + i] for i in range(4)]
-            stack = jnp.concatenate(
-                [jnp.concatenate(planes[0:3], axis=0), jnp.concatenate(planes[1:4], axis=0)], axis=1
-            )
-            part = jnp.dot(taps, stack, preferred_element_type=F32)
-            for i in range(2):
-                here = row + i
-                left, mid, right = (
-                    part[BINS * k : BINS * (k + 1), LANES * i : LANES * (i + 1)] for k in range(3)
-                )
-                spot = here * DEEP + near
-                moved = pltpu.roll(side_edge, (edge_lane - spot + LANES) % LANES, 1)
-                response = mid + jnp.where(lane == 0, 0.0, pltpu.roll(left, 1, 1))
-                response = response + jnp.where(lane == LANES - 1, 0.0, pltpu.roll(right, LANES - 1, 1))
-                before = joined_ref[here] if layer == 0 else current[here]
-                value = before + (response + jnp.where(at_edge, moved, 0.0))
-                if final:
-                    out_ref[here - DEEP] = value
-                else:
-                    current[here] = value
-                    keep = ((here >= DEEP) | has_above) & ((here < ROWS + DEEP) | has_below)
-                    active[later, here] = jnp.where(keep, silu(value), 0.0).astype(BF16)
-                    outward = jnp.where(col == 0, left, right)
-                    thrown = pltpu.roll(outward, (spot - edge_lane + LANES) % LANES, 1)
-                    injected = jnp.where(lane == spot, thrown, injected)
-            return injected
-
-        injected = jnp.zeros((BINS, LANES), F32)
-        for step in range(pairs):
-            injected = pair(step, injected)
-            if final and (step + 1) % SENT == 0:
-                rows = pl.ds(2 * (step + 1 - SENT), 2 * SENT)
-                copy = pltpu.make_async_copy(out_ref.at[rows], out_hbm.at[rows], sems.at[len(leaving)])
-                copy.start()
-                leaving.append(copy)
+        def inward(row):
+            spot = row * DEEP + near
+            moved = pltpu.roll(side_edge, (edge_lane - spot + LANES) % LANES, 1)
+            return jnp.where(at_edge, moved, 0.0)
+
+        def keep(row, value):
+            current[row] = value
+            if row < DEEP:
+                value = jnp.where(has_above, silu(value), 0.0)
+            elif row >= ROWS + DEEP:
+                value = jnp.where(has_below, silu(value), 0.0)
+            else:
+                value = silu(value)
+            active[later, row] = value.astype(BF16)
+
+        if layer == 0:
+            injected = injected_ref[...]
+            for row in range(first, EXT - first):
+                keep(row, partial_ref[row] + inward(row))
+        else:
+            injected = jnp.zeros((BINS, LANES), F32)
+            for row in range(first, EXT - first, 2):
+                parts = convolve_pair(taps, [active[now, row - 1 + i] for i in range(4)])
+                for i, (left, mid, right) in enumerate(parts):
+                    here = row + i
+                    value = current[here] + (within(lane, left, mid, right) + inward(here))
+                    if final:
+                        out_ref[here - DEEP] = value
+                    else:
+                        keep(here, value)
+                        injected = outward_edge(col, lane, edge_lane, here * DEEP + near, left, right, injected)
+                done = row + 2 - DEEP
+                if final and done % (2 * SENT) == 0:
+                    rows = pl.ds(done - 2 * SENT, 2 * SENT)
+                    copy = pltpu.make_async_copy(out_ref.at[rows], out_hbm.at[rows], sems.at[len(leaving)])
+                    copy.start()
+                    leaving.append(copy)
         if not final:
-            place = lane % DEEP
             from_left = jnp.where((place == 0) & (col == 0), injected, pltpu.roll(side_left, 1, 1))
             from_right = jnp.where((place == DEEP - 1) & (col != 0), injected, pltpu.roll(side_right, LANES - 1, 1))
             side_current = side_current + (side_mid + from_left + from_right)
@@ -456,26 +506,26 @@
         copy.wait()
 
 
-def refine(spot, matrix, joined, side):
+def refine(spot, matrix, partial, injected, side):
     vmem = pl.BlockSpec(memory_space=pltpu.VMEM)
     smem = pl.BlockSpec(memory_space=pltpu.SMEM)
     anywhere = pl.BlockSpec(memory_space=pl.ANY)
-    flat = (ROWS,) + joined.shape[1:]
+    flat = (ROWS,) + partial.shape[1:]
     return pl.pallas_call(
         refine_kernel,
         out_shape=jax.ShapeDtypeStruct(flat, F32),
-        in_specs=[smem, vmem, vmem, vmem],
+        in_specs=[smem, vmem, vmem, vmem, vmem],
         out_specs=anywhere,
         scratch_shapes=[
             pltpu.VMEM(flat, F32),
-            pltpu.VMEM(joined.shape, F32),
-            pltpu.VMEM((2,) + joined.shape, BF16),
+            pltpu.VMEM(partial.shape, F32),
+            pltpu.VMEM((2,) + partial.shape, BF16),
             pltpu.VMEM((BINS, LANES), BF16),
             pltpu.SemaphoreType.DMA((ROWS // (2 * SENT),)),
         ],
         compiler_params=pltpu.CompilerParams(vmem_limit_bytes=16 << 20),
         name="refine",
-    )(spot, matrix, joined, side)
+    )(spot, matrix, partial, injected, side)
 
 
 def on_device(tsdf_prior, prior_weight, depth_maps, confidence, frustum_tiles, pixel_index, conv_weights):
@@ -516,7 +566,8 @@
         prior_weight,
     )
     side = lax.ppermute(edge, "col", [(0, 1), (1, 0)])
-    refined = refine(spot, matrix, joined, side)
+    partial, injected = open_layer(spot, matrix, joined)
+    refined = refine(spot, matrix, partial, injected, side)
     return refined, new_weight
 
 

time: 54.6 us -> 54.3 us (level)
  waiting for transfers between devices: 1.84 us -> 0.98 us
  Pallas kernels: 28.5 us -> 29.2 us
    pallas_call x0 -> x1, Pallas kernels: none -> 1.84 us  [open_layer(): pl.pallas_call(open_kernel, out_shape=(jax.ShapeDtypeStruct(joined.shape,...]
    pallas_call x1, Pallas kernels: 5.72 us -> 4.59 us  [refine(): pl.pallas_call(refine_kernel, out_shape=jax.ShapeDtypeStruct(flat, F32),...]
    ppermute x1, waiting for transfers between devices: 0.86 us -> 0.01 us  [on_device(): side = lax.ppermute(edge, 'col', [(0, 1), (1, 0)])]
  transfers between devices with their start and end apart: 4 -> 4, of which waited for: 2 -> 1; matrix products, arithmetic and copies ran while one was open for 1% -> 1% of each run, Pallas kernels for 0% -> 4%
where the time goes in v7:
time: 54.3 us; the launch traced here: 54.1 us
  Pallas kernels  29.2 us (54%)
  starting transfers between devices  22.3 us (41%)
  between operations  0.99 us (2%)
  waiting for transfers between devices  0.98 us (2%)
    pallas_call x1, Pallas kernels, sample(): pl.pallas_call(sample_kernel, out_shape=jax.ShapeDtypeStruct((WIDTH * wan...  14.3 us
    all_to_all x1, starting transfers between devices, on_device(): lax.all_to_all(words.reshape(readers, 1, width), both, split_axis=0, conc...  10.8 us
    pallas_call x1, Pallas kernels, join(): pl.pallas_call(join_kernel, out_shape=(jax.ShapeDtypeStruct(tall, F32), j...  8.21 us
    ppermute x1, starting transfers between devices, on_device(): below = lax.ppermute(halo(0), 'row', down)  6.41 us
    pallas_call x1, Pallas kernels, refine(): pl.pallas_call(refine_kernel, out_shape=jax.ShapeDtypeStruct(flat, F32),...  4.59 us
    ppermute x1, starting transfers between devices, on_device(): above = lax.ppermute(halo(ROWS - DEEP), 'row', up)  3.1 us
    ppermute x1, starting transfers between devices, on_device(): side = lax.ppermute(edge, 'col', [(0, 1), (1, 0)])  1.9 us
    pallas_call x1, Pallas kernels, open_layer(): pl.pallas_call(open_kernel, out_shape=(jax.ShapeDtypeStruct(joined.shape,...  1.84 us
  transfers between devices with their start and end apart: 4, of which 1 were waited for; matrix products, arithmetic and copies ran while one was open for 1% of the time, Pallas kernels for 4%

profile of v7, /device:TPU:3, one launch (start us, length us, event | category | flops | bytes accessed | tf_op | source)
XLA Modules:
  0.0 54.1 jit_solution(13787229527253625891)
XLA Ops:
  0.6 0.0 copy-start
  0.6 14.3 %sample.1 = s32[640,128]{1,0:T(8,128)} custom-call(s32[256,128]{1,0:T(8,128)} %bitcast.24, s32[2,128]{1,0:T(2,128)} %bitcast.25, f32[1024,128]{1,0:T(8,128)} %bitcast.21, f32[1024,128]{1,0:T(8,128)} %bitcast.22), custom_call_target="tpu_custom_call" | custom-call | tf_op jit(solution)/shard_map/sample/pallas_call | solution.py:193
  14.9 0.0 copy-start.1
  14.9 10.8 %all-to-all-start = ((s32[128,1,640]{2,1,0:T(1,128)}), s32[128,1,640]{2,1,0:T(1,128)S(1)}, u32[]{:S(2)}, u32[]{:S(2)}) async-start(s32[128,1,640]{2,1,0:T(1,128)} %bitcast.20), calls=%async_computation | async-start | bytes 655360 | tf_op jit(solution)/shard_map/all_to_all | solution.py:543
  25.8 0.1 convert.12
  25.9 0.0 copy-start.2
  25.9 0.1 convert.13
  26.0 3.1 %collective-permute-start = (bf16[6,64,128]{2,1,0:T(8,128)(2,1)S(1)}, bf16[6,64,128]{2,1,0:T(8,128)(2,1)S(1)}, u32[]{:S(2)}, u32[]{:S(2)}) collective-permute-start(bf16[6,64,128]{2,1,0:T(8,128)(2,1)S(1)} %pad_maximum_fusion), channel_id=1, source_target_pairs={{0,2},{2,4},{4,6},{6,8},{8,10},{10,12},{12,14},{14,16},{16,18},{18... | collective-permute-start | bytes 294920 | tf_op jit(solution)/shard_map/ppermute | solution.py:550
  29.2 6.4 %collective-permute-start.1 = (bf16[6,64,128]{2,1,0:T(8,128)(2,1)S(1)}, bf16[6,64,128]{2,1,0:T(8,128)(2,1)S(1)}, u32[]{:S(2)}, u32[]{:S(2)}) collective-permute-start(bf16[6,64,128]{2,1,0:T(8,128)(2,1)S(1)} %pad_maximum_fusion.1), channel_id=1, source_target_pairs={{2,0},{4,2},{6,4},{8,6},{10,8},{12,10},{14,12},{16,14},{18,16},{20... | collective-permute-start | bytes 294920 | tf_op jit(solution)/shard_map/ppermute | solution.py:551
  35.6 0.0 copy-done.2
  35.6 0.1 copy.12
  35.7 0.1 reshape.26
  35.8 0.1 copy.13.taps_ref
  35.9 0.2 tap_matrices.1.matrix
  36.2 0.1 pad_add_fusion.spot_ref
  36.2 1.0 %collective-permute-done.above_ref = bf16[6,64,128]{2,1,0:T(8,128)(2,1)S(1)} collective-permute-done((bf16[6,64,128]{2,1,0:T(8,128)(2,1)S(1)}, bf16[6,64,128]{2,1,0:T(8,128)(2,1)S(1)}, u32[]{:S(2)}, u32[]{:S(2)}) %collective-permute-start) | collective-permute-done | bytes 98336 | tf_op jit(solution)/shard_map/ppermute | solution.py:550
  37.2 0.0 all-to-all-done
  37.3 0.1 fusion.list_ref
  37.4 0.0 collective-permute-done.1.below_ref
  37.4 8.2 %join.1 = (f32[38,64,128]{2,1,0:T(8,128)S(1)}, f32[32,64,128]{2,1,0:T(8,128)}, f32[64,128]{1,0:T(8,128)S(1)}) custom-call(s32[3]{0:T(128)S(1)} %pad_add_fusion.spot_ref, s32[128,4]{1,0:T(8,128)S(1)} %fusion.list_ref, s32[640,128]{1,0:T(8,128)S(1)} %bitcast.19, bf16[6,64,128]{2,1,0:T(8,128)(2,1)S(1)} %collective-permute-done.above_ref, ...), custom_call_target="tpu_custom_call" | custom-call | tf_op jit(solution)/shard_map/join/pallas_call | solution.py:322
  45.6 1.9 %collective-permute-start.2 = (f32[64,128]{1,0:T(8,128)S(1)}, f32[64,128]{1,0:T(8,128)S(1)}, u32[]{:S(2)}, u32[]{:S(2)}) collective-permute-start(f32[64,128]{1,0:T(8,128)S(1)} %get-tuple-element.14), channel_id=1, source_target_pairs={{0,1},{1,0},{2,3},{3,2},{4,5},{5,4},{6,7},{7,6},{8,9},{9,8},{10,11... | collective-permute-start | bytes 98312 | tf_op jit(solution)/shard_map/ppermute | solution.py:568
  47.5 1.8 %open_layer.1 = (f32[38,64,128]{2,1,0:T(8,128)S(1)}, f32[64,128]{1,0:T(8,128)S(1)}) custom-call(s32[3]{0:T(128)S(1)} %pad_add_fusion.spot_ref, bf16[3,192,192]{2,1,0:T(8,128)(2,1)S(1)} %tap_matrices.1.matrix, f32[38,64,128]{2,1,0:T(8,128)S(1)} %get-tuple-element.11.joined_ref), custom_call_target="tpu_custom_call" | custom-call | flops 400000000 | bytes 3000000 | tf_op jit(solution)/shard_map/open_layer/pallas_call | solution.py:419
  49.3 0.0 collective-permute-done.2.side_ref
  49.3 4.6 %refine.1 = f32[32,64,128]{2,1,0:T(8,128)} custom-call(s32[3]{0:T(128)S(1)} %pad_add_fusion.spot_ref, bf16[3,192,192]{2,1,0:T(8,128)(2,1)S(1)} %tap_matrices.1.matrix, f32[38,64,128]{2,1,0:T(8,128)S(1)} %get-tuple-element.12.partial_ref, f32[64,128]{1,0:T(8,128)S(1)} %get-tuple-element.13.injected_ref, f32[64,128]{1,0:T(8,128)S(1)} %collective-permute-done.2.side_ref), custom_call_target="tpu_custom_call" | custom-call | tf_op jit(solution)/shard_map/refine/pallas_call | solution.py:514
  (7 shorter events, 0.1 us)
Async XLA Ops:
  0.6 25.2 %copy-start = (f32[32,64,128]{2,1,0:T(8,128)S(1)}, f32[32,64,128]{2,1,0:T(8,128)}, u32[]{:S(2)}) copy-start(f32[32,64,128]{2,1,0:T(8,128)} %prior_hbm.1) | copy-start | bytes 3145732
  14.9 11.0 %copy-start.1 = (f32[32,64,128]{2,1,0:T(8,128)S(1)}, f32[32,64,128]{2,1,0:T(8,128)}, u32[]{:S(2)}) copy-start(f32[32,64,128]{2,1,0:T(8,128)} %weight_hbm.1) | copy-start | bytes 3145732
  14.9 22.3 %all-to-all-start = ((s32[128,1,640]{2,1,0:T(1,128)}), s32[128,1,640]{2,1,0:T(1,128)S(1)}, u32[]{:S(2)}, u32[]{:S(2)}) async-start(s32[128,1,640]{2,1,0:T(1,128)} %bitcast.20), calls=%async_computation | async-start | bytes 655360 | tf_op jit(solution)/shard_map/all_to_all | solution.py:543
  25.9 9.7 %copy-start.2 = (bf16[3,64,16,3,3]{1,2,4,3,0:T(8,128)(2,1)S(1)}, bf16[3,64,16,3,3]{1,2,4,3,0:T(8,128)(2,1)}, u32[]{:S(2)}) copy-start(bf16[3,64,16,3,3]{1,2,4,3,0:T(8,128)(2,1)} %param.13) | copy-start | bytes 165892
  26.0 11.2 %collective-permute-start = (bf16[6,64,128]{2,1,0:T(8,128)(2,1)S(1)}, bf16[6,64,128]{2,1,0:T(8,128)(2,1)S(1)}, u32[]{:S(2)}, u32[]{:S(2)}) collective-permute-start(bf16[6,64,128]{2,1,0:T(8,128)(2,1)S(1)} %pad_maximum_fusion), channel_id=1, source_target_pairs={{0,2},{2,4},{4,6},{6,8},{8,10},{10,12},{12,14},{14,16},{16,18},{18... | collective-permute-start | bytes 294920 | tf_op jit(solution)/shard_map/ppermute | solution.py:550
  29.2 8.2 %collective-permute-start.1 = (bf16[6,64,128]{2,1,0:T(8,128)(2,1)S(1)}, bf16[6,64,128]{2,1,0:T(8,128)(2,1)S(1)}, u32[]{:S(2)}, u32[]{:S(2)}) collective-permute-start(bf16[6,64,128]{2,1,0:T(8,128)(2,1)S(1)} %pad_maximum_fusion.1), channel_id=1, source_target_pairs={{2,0},{4,2},{6,4},{8,6},{10,8},{12,10},{14,12},{16,14},{18,16},{20... | collective-permute-start | bytes 294920 | tf_op jit(solution)/shard_map/ppermute | solution.py:551
  45.6 3.8 %collective-permute-start.2 = (f32[64,128]{1,0:T(8,128)S(1)}, f32[64,128]{1,0:T(8,128)S(1)}, u32[]{:S(2)}, u32[]{:S(2)}) collective-permute-start(f32[64,128]{1,0:T(8,128)S(1)} %get-tuple-element.14), channel_id=1, source_target_pairs={{0,1},{1,0},{2,3},{3,2},{4,5},{5,4},{6,7},{7,6},{8,9},{9,8},{10,11... | collective-permute-start | bytes 98312 | tf_op jit(solution)/shard_map/ppermute | solution.py:568

commit v8 on v7

--- a/solution.py
+++ b/solution.py
@@ -247,7 +247,7 @@
                 counts[side] = counts[side] + (1 + (pair[side] >> 31))
         return tuple(counts)
 
-    counts = lax.fori_loop(0, half // 2, pick, (jnp.int32(0), jnp.int32(0)), unroll=2)
+    counts = lax.fori_loop(0, half // 2, pick, (jnp.int32(0), jnp.int32(0)), unroll=8)
     for side in range(2):
         for i in range(AT_ONCE):
             order_ref[room * side + counts[side] + i] = entries

time: 54.3 us -> 54.3 us (level)
  starting transfers between devices: 22.3 us -> 21.4 us
    ppermute x1, starting transfers between devices: 1.9 us -> 1.08 us  [on_device(): side = lax.ppermute(edge, 'col', [(0, 1), (1, 0)])]
where the time goes in v8:
time: 54.3 us; the launch traced here: 53.7 us
  Pallas kernels  29.6 us (55%)
  starting transfers between devices  21.4 us (39%)
  between operations  0.99 us (2%)
  waiting for transfers between devices  0.98 us (2%)
    pallas_call x1, Pallas kernels, sample(): pl.pallas_call(sample_kernel, out_shape=jax.ShapeDtypeStruct((WIDTH * wan...  14.3 us
    all_to_all x1, starting transfers between devices, on_device(): lax.all_to_all(words.reshape(readers, 1, width), both, split_axis=0, conc...  10.8 us
    pallas_call x1, Pallas kernels, join(): pl.pallas_call(join_kernel, out_shape=(jax.ShapeDtypeStruct(tall, F32), j...  8.62 us
    ppermute x1, starting transfers between devices, on_device(): below = lax.ppermute(halo(0), 'row', down)  6.41 us
    pallas_call x1, Pallas kernels, refine(): pl.pallas_call(refine_kernel, out_shape=jax.ShapeDtypeStruct(flat, F32),...  4.59 us
    ppermute x1, starting transfers between devices, on_device(): above = lax.ppermute(halo(ROWS - DEEP), 'row', up)  3.1 us
    pallas_call x1, Pallas kernels, open_layer(): pl.pallas_call(open_kernel, out_shape=(jax.ShapeDtypeStruct(joined.shape,...  1.84 us
  transfers between devices with their start and end apart: 4, of which 1 were waited for; matrix products, arithmetic and copies ran while one was open for 1% of the time, Pallas kernels for 4%

profile of v8, /device:TPU:3, one launch (start us, length us, event | category | flops | bytes accessed | tf_op | source)
XLA Modules:
  0.0 53.7 jit_solution(1705690106134203116)
XLA Ops:
  0.6 0.0 copy-start
  0.6 14.3 %sample.1 = s32[640,128]{1,0:T(8,128)} custom-call(s32[256,128]{1,0:T(8,128)} %bitcast.24, s32[2,128]{1,0:T(2,128)} %bitcast.25, f32[1024,128]{1,0:T(8,128)} %bitcast.21, f32[1024,128]{1,0:T(8,128)} %bitcast.22), custom_call_target="tpu_custom_call" | custom-call | tf_op jit(solution)/shard_map/sample/pallas_call | solution.py:193
  14.9 0.0 copy-start.1
  14.9 10.8 %all-to-all-start = ((s32[128,1,640]{2,1,0:T(1,128)}), s32[128,1,640]{2,1,0:T(1,128)S(1)}, u32[]{:S(2)}, u32[]{:S(2)}) async-start(s32[128,1,640]{2,1,0:T(1,128)} %bitcast.20), calls=%async_computation | async-start | bytes 655360 | tf_op jit(solution)/shard_map/all_to_all | solution.py:543
  25.8 0.0 copy-done
  25.8 0.1 convert.12
  25.9 0.0 copy-start.2
  25.9 0.1 convert.13
  26.0 3.1 %collective-permute-start = (bf16[6,64,128]{2,1,0:T(8,128)(2,1)S(1)}, bf16[6,64,128]{2,1,0:T(8,128)(2,1)S(1)}, u32[]{:S(2)}, u32[]{:S(2)}) collective-permute-start(bf16[6,64,128]{2,1,0:T(8,128)(2,1)S(1)} %pad_maximum_fusion), channel_id=1, source_target_pairs={{0,2},{2,4},{4,6},{6,8},{8,10},{10,12},{12,14},{14,16},{16,18},{18... | collective-permute-start | bytes 294920 | tf_op jit(solution)/shard_map/ppermute | solution.py:550
  29.2 6.4 %collective-permute-start.1 = (bf16[6,64,128]{2,1,0:T(8,128)(2,1)S(1)}, bf16[6,64,128]{2,1,0:T(8,128)(2,1)S(1)}, u32[]{:S(2)}, u32[]{:S(2)}) collective-permute-start(bf16[6,64,128]{2,1,0:T(8,128)(2,1)S(1)} %pad_maximum_fusion.1), channel_id=1, source_target_pairs={{2,0},{4,2},{6,4},{8,6},{10,8},{12,10},{14,12},{16,14},{18,16},{20... | collective-permute-start | bytes 294920 | tf_op jit(solution)/shard_map/ppermute | solution.py:551
  35.6 0.1 copy.12
  35.7 0.1 reshape.26
  35.8 0.1 copy.13.taps_ref
  35.9 0.2 tap_matrices.1.matrix
  36.2 0.1 pad_add_fusion.spot_ref
  36.2 1.0 %collective-permute-done.above_ref = bf16[6,64,128]{2,1,0:T(8,128)(2,1)S(1)} collective-permute-done((bf16[6,64,128]{2,1,0:T(8,128)(2,1)S(1)}, bf16[6,64,128]{2,1,0:T(8,128)(2,1)S(1)}, u32[]{:S(2)}, u32[]{:S(2)}) %collective-permute-start) | collective-permute-done | bytes 98336 | tf_op jit(solution)/shard_map/ppermute | solution.py:550
  37.2 0.0 all-to-all-done
  37.3 0.1 fusion.list_ref
  37.4 0.0 collective-permute-done.1.below_ref
  37.4 8.6 %join.1 = (f32[38,64,128]{2,1,0:T(8,128)S(1)}, f32[32,64,128]{2,1,0:T(8,128)}, f32[64,128]{1,0:T(8,128)S(1)}) custom-call(s32[3]{0:T(128)S(1)} %pad_add_fusion.spot_ref, s32[128,4]{1,0:T(8,128)S(1)} %fusion.list_ref, s32[640,128]{1,0:T(8,128)S(1)} %bitcast.19, bf16[6,64,128]{2,1,0:T(8,128)(2,1)S(1)} %collective-permute-done.above_ref, ...), custom_call_target="tpu_custom_call" | custom-call | tf_op jit(solution)/shard_map/join/pallas_call | solution.py:322
  46.0 1.1 %collective-permute-start.2 = (f32[64,128]{1,0:T(8,128)S(1)}, f32[64,128]{1,0:T(8,128)S(1)}, u32[]{:S(2)}, u32[]{:S(2)}) collective-permute-start(f32[64,128]{1,0:T(8,128)S(1)} %get-tuple-element.14), channel_id=1, source_target_pairs={{0,1},{1,0},{2,3},{3,2},{4,5},{5,4},{6,7},{7,6},{8,9},{9,8},{10,11... | collective-permute-start | bytes 98312 | tf_op jit(solution)/shard_map/ppermute | solution.py:568
  47.1 1.8 %open_layer.1 = (f32[38,64,128]{2,1,0:T(8,128)S(1)}, f32[64,128]{1,0:T(8,128)S(1)}) custom-call(s32[3]{0:T(128)S(1)} %pad_add_fusion.spot_ref, bf16[3,192,192]{2,1,0:T(8,128)(2,1)S(1)} %tap_matrices.1.matrix, f32[38,64,128]{2,1,0:T(8,128)S(1)} %get-tuple-element.11.joined_ref), custom_call_target="tpu_custom_call" | custom-call | flops 400000000 | bytes 3000000 | tf_op jit(solution)/shard_map/open_layer/pallas_call | solution.py:419
  48.9 0.0 collective-permute-done.2.side_ref
  48.9 4.6 %refine.1 = f32[32,64,128]{2,1,0:T(8,128)} custom-call(s32[3]{0:T(128)S(1)} %pad_add_fusion.spot_ref, bf16[3,192,192]{2,1,0:T(8,128)(2,1)S(1)} %tap_matrices.1.matrix, f32[38,64,128]{2,1,0:T(8,128)S(1)} %get-tuple-element.12.partial_ref, f32[64,128]{1,0:T(8,128)S(1)} %get-tuple-element.13.injected_ref, f32[64,128]{1,0:T(8,128)S(1)} %collective-permute-done.2.side_ref), custom_call_target="tpu_custom_call" | custom-call | tf_op jit(solution)/shard_map/refine/pallas_call | solution.py:514
  (7 shorter events, 0.1 us)
Async XLA Ops:
  0.6 25.2 %copy-start = (f32[32,64,128]{2,1,0:T(8,128)S(1)}, f32[32,64,128]{2,1,0:T(8,128)}, u32[]{:S(2)}) copy-start(f32[32,64,128]{2,1,0:T(8,128)} %prior_hbm.1) | copy-start | bytes 3145732
  14.9 11.0 %copy-start.1 = (f32[32,64,128]{2,1,0:T(8,128)S(1)}, f32[32,64,128]{2,1,0:T(8,128)}, u32[]{:S(2)}) copy-start(f32[32,64,128]{2,1,0:T(8,128)} %weight_hbm.1) | copy-start | bytes 3145732
  14.9 22.3 %all-to-all-start = ((s32[128,1,640]{2,1,0:T(1,128)}), s32[128,1,640]{2,1,0:T(1,128)S(1)}, u32[]{:S(2)}, u32[]{:S(2)}) async-start(s32[128,1,640]{2,1,0:T(1,128)} %bitcast.20), calls=%async_computation | async-start | bytes 655360 | tf_op jit(solution)/shard_map/all_to_all | solution.py:543
  25.9 9.7 %copy-start.2 = (bf16[3,64,16,3,3]{1,2,4,3,0:T(8,128)(2,1)S(1)}, bf16[3,64,16,3,3]{1,2,4,3,0:T(8,128)(2,1)}, u32[]{:S(2)}) copy-start(bf16[3,64,16,3,3]{1,2,4,3,0:T(8,128)(2,1)} %param.13) | copy-start | bytes 165892
  26.0 11.2 %collective-permute-start = (bf16[6,64,128]{2,1,0:T(8,128)(2,1)S(1)}, bf16[6,64,128]{2,1,0:T(8,128)(2,1)S(1)}, u32[]{:S(2)}, u32[]{:S(2)}) collective-permute-start(bf16[6,64,128]{2,1,0:T(8,128)(2,1)S(1)} %pad_maximum_fusion), channel_id=1, source_target_pairs={{0,2},{2,4},{4,6},{6,8},{8,10},{10,12},{12,14},{14,16},{16,18},{18... | collective-permute-start | bytes 294920 | tf_op jit(solution)/shard_map/ppermute | solution.py:550
  29.2 8.2 %collective-permute-start.1 = (bf16[6,64,128]{2,1,0:T(8,128)(2,1)S(1)}, bf16[6,64,128]{2,1,0:T(8,128)(2,1)S(1)}, u32[]{:S(2)}, u32[]{:S(2)}) collective-permute-start(bf16[6,64,128]{2,1,0:T(8,128)(2,1)S(1)} %pad_maximum_fusion.1), channel_id=1, source_target_pairs={{2,0},{4,2},{6,4},{8,6},{10,8},{12,10},{14,12},{16,14},{18,16},{20... | collective-permute-start | bytes 294920 | tf_op jit(solution)/shard_map/ppermute | solution.py:551
  46.0 2.9 %collective-permute-start.2 = (f32[64,128]{1,0:T(8,128)S(1)}, f32[64,128]{1,0:T(8,128)S(1)}, u32[]{:S(2)}, u32[]{:S(2)}) collective-permute-start(f32[64,128]{1,0:T(8,128)S(1)} %get-tuple-element.14), channel_id=1, source_target_pairs={{0,1},{1,0},{2,3},{3,2},{4,5},{5,4},{6,7},{7,6},{8,9},{9,8},{10,11... | collective-permute-start | bytes 98312 | tf_op jit(solution)/shard_map/ppermute | solution.py:568
